TPU v7x, 32 devices: a whole 2x2x4 slice. The times are simulated.
32 devices in a mesh: img: 4 (over z), row: 4 (over y, x), col: 2 (over core).
Axes of the slice: x: 2, y: 2, z: 4, core: 2. Of those that a mesh axis runs over, the one named last changes fastest.
Arguments:
- feature_in: bfloat16 [8, 64, 64, 2048], P('img', 'row', 'col'), may hold values from -6 to 6
- orientation: int32 [8], P('img'), may hold values from 0 to 1
- offset_base: int32 [8, 64, 64, 18], P('img', 'row', 'col'), may hold values from -4 to 4
- w_reduce_a: bfloat16 [2048, 512], replicated, may hold values from -0.125 to 0.125
- w_offset_a: bfloat16 [4608, 18], replicated, may hold values from -0.25 to 0.25
- w_deform_a: bfloat16 [4608, 512], replicated, may hold values from -0.09375 to 0.09375
- w_expand_a: bfloat16 [512, 2048], replicated, may hold values from -0.25 to 0.25
- scale_a: float32 [3072], replicated, may hold values from 0.5 to 1.5
- shift_a: float32 [3072], replicated, may hold values from -1.5 to 1.5
- w_reduce_b: bfloat16 [2048, 512], replicated, may hold values from -0.125 to 0.125
- w_conv_b: bfloat16 [4608, 512], replicated, may hold values from -0.09375 to 0.09375
- w_expand_b: bfloat16 [512, 2048], replicated, may hold values from -0.25 to 0.25
- scale_b: float32 [3072], replicated, may hold values from 0.5 to 1.5
- shift_b: float32 [3072], replicated, may hold values from -1.5 to 1.5
- cotangent: bfloat16 [8, 64, 64, 2048], P('img', 'row', 'col'), may hold values from -6 to 6
Outputs:
- feature_out: bfloat16 [8, 64, 64, 2048], P('img', 'row', 'col')
- grad_in: bfloat16 [8, 64, 64, 2048], P('img', 'row', 'col')
- grad_reduce_a: float32 [2048, 512], P('img')
- grad_offset_a: float32 [4608, 18], P('img')
- grad_deform_a: float32 [4608, 512], P('img')
- grad_expand_a: float32 [512, 2048], P('img')
- grad_scale_a: float32 [3072], replicated
- grad_shift_a: float32 [3072], replicated
- batch_mean_a: float32 [3072], replicated
- batch_var_a: float32 [3072], replicated
- grad_reduce_b: float32 [2048, 512], P('img')
- grad_conv_b: float32 [4608, 512], P('img')
- grad_expand_b: float32 [512, 2048], P('img')
- grad_scale_b: float32 [3072], replicated
- grad_shift_b: float32 [3072], replicated
- batch_mean_b: float32 [3072], replicated
- batch_var_b: float32 [3072], replicated
Inputs may be any that keep to these rules, and one draw needn't show every extreme that they name: `orientation`: 0 marks an image of 44 rows by 64 columns, 1 one of 64 rows by 44 columns; either fills the top-left of a 64 x 64 canvas and the rest of the canvas is ignored. `offset_base`: channel 2k displaces tap k's rows, channel 2k + 1 its columns.
All inputs are finite; a program needn't handle non-finite values.
Results may differ from a plain program's by a relative error of at most 0.025.
Values may be sent and summed in bfloat16 or wider, within the bound.
A program may use at most 320 MiB of HBM per device.

v0:
```python
import jax
import jax.numpy as jnp
import numpy as np
from jax import lax
from jax.sharding import PartitionSpec as P

LONG = 64
SHORT = 44
BOUND = 4


EPSILON = 1e-05


def padded_2(shard, sides, width):
    for axis, dim in sides:
        count, length = (lax.axis_size(axis), shard.shape[dim])
        up = [(i, (i + 1) % count) for i in range(count - 1)]
        down = [(j, i) for i, j in up]
        last = lax.slice_in_dim(shard, length - width, length, axis=dim)
        initial = lax.slice_in_dim(shard, 0, width, axis=dim)
        before = lax.ppermute(last, axis, up)
        after = lax.ppermute(initial, axis, down)
        shard = jnp.concatenate([before, shard, after], axis=dim)
    return shard


def gelu_exact(values):
    return jax.nn.gelu(values, approximate=False)


def gelu_back(values, upstream):
    return jax.vjp(gelu_exact, values)[1](upstream)[0]


def norm_forward(pre_norm, weight_col, norm_gain, norm_shift, pixel_count):
    batch_mean = (
        lax.psum(jnp.sum(pre_norm * weight_col, axis=0), ("img", "row", "col")) / pixel_count
    )
    centered = pre_norm - batch_mean
    spread = (
        lax.psum(jnp.sum(centered * centered * weight_col, axis=0), ("img", "row", "col"))
        / pixel_count
    )
    inv_std = lax.rsqrt(spread + EPSILON)
    unit_value = (pre_norm - batch_mean) * inv_std
    return (unit_value * norm_gain + norm_shift, unit_value, inv_std, batch_mean, spread)


def norm_backward(grad_normed, unit_value, inv_std, norm_gain, weight_col, pixel_count):
    sum_grad, sum_unit = lax.psum(
        (jnp.sum(grad_normed, axis=0), jnp.sum(grad_normed * unit_value, axis=0)),
        ("img", "row", "col"),
    )
    grad_pre = (
        norm_gain
        * inv_std
        * (grad_normed - (sum_grad + unit_value * sum_unit) / pixel_count)
        * weight_col
    )
    return (grad_pre.astype(jnp.bfloat16), sum_unit, sum_grad)


def tap_stack(padded, reach_cells, tile_rows, tile_cols, direction):
    pieces = []
    for kernel_tap in range(9):
        step_row = reach_cells + direction * 2 * (kernel_tap // 3 - 1)
        step_col = reach_cells + direction * 2 * (kernel_tap % 3 - 1)
        pieces.append(
            padded[:, step_row : step_row + tile_rows, step_col : step_col + tile_cols, :]
        )
    return jnp.stack(pieces, axis=3)


def corner_tables(fraction, offset_base, reach_cells, tile_rows, tile_cols):
    side_cells = tile_cols + 2 * reach_cells
    images = offset_base.shape[0]
    frac_pairs = fraction.reshape(images, tile_rows, tile_cols, 9, 2)
    base_pairs = offset_base.reshape(images, tile_rows, tile_cols, 9, 2)
    tap_rows = jnp.asarray(
        np.array([2 * (kernel_tap // 3 - 1) for kernel_tap in range(9)]), jnp.int32
    )
    tap_cols = jnp.asarray(
        np.array([2 * (kernel_tap % 3 - 1) for kernel_tap in range(9)]), jnp.int32
    )
    row_ids = jnp.arange(tile_rows, dtype=jnp.int32).reshape(1, tile_rows, 1, 1)
    col_ids = jnp.arange(tile_cols, dtype=jnp.int32).reshape(1, 1, tile_cols, 1)
    upper = row_ids + reach_cells + tap_rows + base_pairs[..., 0]
    leftmost = col_ids + reach_cells + tap_cols + base_pairs[..., 1]
    frac_row = frac_pairs[..., 0]
    frac_col = frac_pairs[..., 1]
    row_weights = (1.0 - frac_row, frac_row)
    col_weights = (1.0 - frac_col, frac_col)
    corner_index = jnp.stack(
        [
            (upper + row_step) * side_cells + leftmost + col_step
            for row_step in (0, 1)
            for col_step in (0, 1)
        ],
        axis=-1,
    )
    corner_weight = jnp.stack(
        [
            row_weights[row_step] * col_weights[col_step]
            for row_step in (0, 1)
            for col_step in (0, 1)
        ],
        axis=-1,
    ).astype(jnp.bfloat16)
    corner_index = corner_index.reshape(images, tile_rows * tile_cols, 9, 4).transpose(0, 2, 1, 3)
    corner_weight = corner_weight.reshape(images, tile_rows * tile_cols, 9, 4).transpose(0, 2, 1, 3)
    return (corner_index, corner_weight, frac_row, frac_col)


def sample_table(index_tap, weight_tap, positions):
    matches = index_tap[:, :, None] == positions[None, None, :]
    return jnp.sum(
        jnp.where(matches, weight_tap[:, :, None].astype(jnp.float32), 0.0), axis=1
    ).astype(jnp.bfloat16)


def sample_image(operands):
    rim_flat, index_image, weight_image = operands
    positions = jnp.arange(rim_flat.shape[0], dtype=jnp.int32)

    def sample_one_tap(tap_operands):
        index_tap, weight_tap = tap_operands
        table = sample_table(index_tap, weight_tap, positions)
        return jnp.dot(table, rim_flat, preferred_element_type=jnp.float32).astype(jnp.bfloat16)

    return lax.map(sample_one_tap, (index_image, weight_image))


def return_image(operands):
    rim_flat, index_image, weight_image, grad_image = operands
    positions = jnp.arange(rim_flat.shape[0], dtype=jnp.int32)

    def return_one_tap(spill, tap_operands):
        index_tap, weight_tap, grad_tap = tap_operands
        table = sample_table(index_tap, weight_tap, positions)
        spill = spill + jnp.einsum("pq,pm->qm", table, grad_tap, preferred_element_type=jnp.float32)
        scores = jnp.einsum("pm,qm->pq", grad_tap, rim_flat, preferred_element_type=jnp.float32)
        matches = index_tap[:, :, None] == positions[None, None, :]
        picked = jnp.sum(jnp.where(matches, scores[:, None, :], 0.0), axis=2)
        return (spill, picked)

    start = jnp.zeros(rim_flat.shape, jnp.float32)
    return lax.scan(return_one_tap, start, (index_image, weight_image, grad_image))


def fold_edges(block, axis_dim, inner, reach_cells):
    own_part = lax.slice_in_dim(block, 2 * reach_cells, 2 * reach_cells + inner, axis=axis_dim)
    before = lax.slice_in_dim(block, 0, reach_cells, axis=axis_dim)
    after = lax.slice_in_dim(block, inner + 3 * reach_cells, inner + 4 * reach_cells, axis=axis_dim)
    pad_before = [(0, 0)] * block.ndim
    pad_before[axis_dim] = (0, inner - reach_cells)
    pad_after = [(0, 0)] * block.ndim
    pad_after[axis_dim] = (inner - reach_cells, 0)
    return own_part + jnp.pad(before, pad_before) + jnp.pad(after, pad_after)


def body(
    feature_in,
    orientation,
    offset_base,
    w_reduce_a,
    w_offset_a,
    w_deform_a,
    w_expand_a,
    scale_a,
    shift_a,
    w_reduce_b,
    w_conv_b,
    w_expand_b,
    scale_b,
    shift_b,
    cotangent,
):
    images, tile_rows, tile_cols, channels = feature_in.shape
    inner_width = w_reduce_a.shape[1]
    second_cut = 2 * inner_width
    reach_cells = BOUND + 3
    pixel_count = 1.0 * lax.axis_size("img") * images * LONG * SHORT
    unbias = pixel_count / (pixel_count - 1.0)
    row_ids = lax.axis_index("row") * tile_rows + jnp.arange(tile_rows, dtype=jnp.int32)
    col_ids = lax.axis_index("col") * tile_cols + jnp.arange(tile_cols, dtype=jnp.int32)
    landscape = jnp.broadcast_to((row_ids < SHORT)[:, None], (tile_rows, tile_cols))
    portrait = jnp.broadcast_to((col_ids < SHORT)[None, :], (tile_rows, tile_cols))
    inside = jnp.where(orientation[:, None, None] == 0, landscape[None], portrait[None]).astype(
        jnp.float32
    )
    weight_col = inside.reshape(-1, 1)
    pixels = weight_col.shape[0]
    block_in = (
        (feature_in.astype(jnp.float32) * inside[..., None])
        .astype(jnp.bfloat16)
        .reshape(pixels, channels)
    )
    reduced_a = jnp.dot(block_in, w_reduce_a, preferred_element_type=jnp.float32)
    normed_a1, unit_a1, inv_a1, mean_a1, spread_a1 = norm_forward(
        reduced_a, weight_col, scale_a[:inner_width], shift_a[:inner_width], pixel_count
    )
    hidden_a = (gelu_exact(normed_a1) * weight_col).astype(jnp.bfloat16)
    rim_a = padded_2(
        hidden_a.reshape(images, tile_rows, tile_cols, inner_width),
        (("row", 1), ("col", 2)),
        reach_cells,
    )
    taps_a = tap_stack(rim_a, reach_cells, tile_rows, tile_cols, 1).reshape(pixels, 9 * inner_width)
    offsets = jnp.dot(taps_a, w_offset_a, preferred_element_type=jnp.float32)
    fraction = jax.nn.sigmoid(offsets)
    corner_index, corner_weight, frac_row, frac_col = corner_tables(
        fraction, offset_base, reach_cells, tile_rows, tile_cols
    )
    rim_flat = rim_a.reshape(images, -1, inner_width)
    samples = lax.map(sample_image, (rim_flat, corner_index, corner_weight))
    deform_weight = w_deform_a.reshape(9, inner_width, inner_width)
    deformed = jnp.einsum(
        "ikpm,kmn->ipn", samples, deform_weight, preferred_element_type=jnp.float32
    ).reshape(pixels, inner_width)
    normed_a2, unit_a2, inv_a2, mean_a2, spread_a2 = norm_forward(
        deformed,
        weight_col,
        scale_a[inner_width:second_cut],
        shift_a[inner_width:second_cut],
        pixel_count,
    )
    hidden2_a = (gelu_exact(normed_a2) * weight_col).astype(jnp.bfloat16)
    expanded_a = jnp.dot(hidden2_a, w_expand_a, preferred_element_type=jnp.float32)
    normed_a3, unit_a3, inv_a3, mean_a3, spread_a3 = norm_forward(
        expanded_a, weight_col, scale_a[second_cut:], shift_a[second_cut:], pixel_count
    )
    pre_a = normed_a3 + block_in.astype(jnp.float32)
    middle = (gelu_exact(pre_a) * weight_col).astype(jnp.bfloat16)
    reduced_b = jnp.dot(middle, w_reduce_b, preferred_element_type=jnp.float32)
    normed_b1, unit_b1, inv_b1, mean_b1, spread_b1 = norm_forward(
        reduced_b, weight_col, scale_b[:inner_width], shift_b[:inner_width], pixel_count
    )
    hidden_b = (gelu_exact(normed_b1) * weight_col).astype(jnp.bfloat16)
    rim_b = padded_2(
        hidden_b.reshape(images, tile_rows, tile_cols, inner_width), (("row", 1), ("col", 2)), 2
    )
    taps_b = tap_stack(rim_b, 2, tile_rows, tile_cols, 1).reshape(pixels, 9 * inner_width)
    conv_out = jnp.dot(taps_b, w_conv_b, preferred_element_type=jnp.float32)
    normed_b2, unit_b2, inv_b2, mean_b2, spread_b2 = norm_forward(
        conv_out,
        weight_col,
        scale_b[inner_width:second_cut],
        shift_b[inner_width:second_cut],
        pixel_count,
    )
    hidden2_b = (gelu_exact(normed_b2) * weight_col).astype(jnp.bfloat16)
    expanded_b = jnp.dot(hidden2_b, w_expand_b, preferred_element_type=jnp.float32)
    normed_b3, unit_b3, inv_b3, mean_b3, spread_b3 = norm_forward(
        expanded_b, weight_col, scale_b[second_cut:], shift_b[second_cut:], pixel_count
    )
    pre_b = normed_b3 + middle.astype(jnp.float32)
    feature_out = (gelu_exact(pre_b) * weight_col).astype(jnp.bfloat16).reshape(feature_in.shape)
    upstream = cotangent.astype(jnp.float32).reshape(pixels, channels) * weight_col
    grad_pre_b = gelu_back(pre_b, upstream)
    grad_expand_out, gain_b3, bias_b3 = norm_backward(
        grad_pre_b, unit_b3, inv_b3, scale_b[second_cut:], weight_col, pixel_count
    )
    gw_expand_b = jnp.einsum(
        "pm,pc->mc", hidden2_b, grad_expand_out, preferred_element_type=jnp.float32
    )
    grad_hidden2_b = jnp.einsum(
        "pc,mc->pm", grad_expand_out, w_expand_b, preferred_element_type=jnp.float32
    )
    grad_normed_b2 = gelu_back(normed_b2, grad_hidden2_b * weight_col)
    grad_conv_out, gain_b2, bias_b2 = norm_backward(
        grad_normed_b2, unit_b2, inv_b2, scale_b[inner_width:second_cut], weight_col, pixel_count
    )
    gw_conv_b = jnp.einsum("pk,pm->km", taps_b, grad_conv_out, preferred_element_type=jnp.float32)
    back_rim = padded_2(
        grad_conv_out.reshape(images, tile_rows, tile_cols, inner_width),
        (("row", 1), ("col", 2)),
        2,
    )
    back_taps = tap_stack(back_rim, 2, tile_rows, tile_cols, -1).reshape(pixels, 9, inner_width)
    grad_hidden_b = jnp.einsum(
        "pkn,kmn->pm",
        back_taps,
        w_conv_b.reshape(9, inner_width, inner_width),
        preferred_element_type=jnp.float32,
    )
    grad_normed_b1 = gelu_back(normed_b1, grad_hidden_b * weight_col)
    grad_reduce_out, gain_b1, bias_b1 = norm_backward(
        grad_normed_b1, unit_b1, inv_b1, scale_b[:inner_width], weight_col, pixel_count
    )
    gw_reduce_b = jnp.einsum(
        "pc,pm->cm", middle, grad_reduce_out, preferred_element_type=jnp.float32
    )
    grad_middle = grad_pre_b + jnp.einsum(
        "pm,cm->pc", grad_reduce_out, w_reduce_b, preferred_element_type=jnp.float32
    )
    grad_pre_a = gelu_back(pre_a, grad_middle * weight_col)
    grad_expand_a, gain_a3, bias_a3 = norm_backward(
        grad_pre_a, unit_a3, inv_a3, scale_a[second_cut:], weight_col, pixel_count
    )
    gw_expand_a = jnp.einsum(
        "pm,pc->mc", hidden2_a, grad_expand_a, preferred_element_type=jnp.float32
    )
    grad_hidden2_a = jnp.einsum(
        "pc,mc->pm", grad_expand_a, w_expand_a, preferred_element_type=jnp.float32
    )
    grad_normed_a2 = gelu_back(normed_a2, grad_hidden2_a * weight_col)
    grad_deformed, gain_a2, bias_a2 = norm_backward(
        grad_normed_a2, unit_a2, inv_a2, scale_a[inner_width:second_cut], weight_col, pixel_count
    )
    grad_deform_image = grad_deformed.reshape(images, -1, inner_width)
    gw_deform_a = jnp.einsum(
        "ikpm,ipn->kmn", samples, grad_deform_image, preferred_element_type=jnp.float32
    ).reshape(9 * inner_width, inner_width)
    grad_samples = jnp.einsum(
        "ipn,kmn->ikpm", grad_deform_image, deform_weight, preferred_element_type=jnp.float32
    ).astype(jnp.bfloat16)
    spill, picked = lax.map(return_image, (rim_flat, corner_index, corner_weight, grad_samples))
    picked = picked.transpose(0, 2, 1, 3).reshape(images, tile_rows, tile_cols, 9, 4)
    grad_row = (picked[..., 2] - picked[..., 0]) * (1.0 - frac_col) + (
        picked[..., 3] - picked[..., 1]
    ) * frac_col
    grad_col = (picked[..., 1] - picked[..., 0]) * (1.0 - frac_row) + (
        picked[..., 3] - picked[..., 2]
    ) * frac_row
    grad_fraction = jnp.stack([grad_row, grad_col], axis=-1).reshape(pixels, 18)
    grad_offsets = (grad_fraction * fraction * (1.0 - fraction)).astype(jnp.bfloat16)
    gw_offset_a = jnp.einsum("pk,po->ko", taps_a, grad_offsets, preferred_element_type=jnp.float32)
    offset_back = jnp.einsum(
        "po,ko->pk", grad_offsets, w_offset_a, preferred_element_type=jnp.float32
    ).reshape(images, tile_rows, tile_cols, 9, inner_width)
    spill = spill.reshape(
        images, tile_rows + 2 * reach_cells, tile_cols + 2 * reach_cells, inner_width
    )
    for kernel_tap in range(9):
        step_row = reach_cells + 2 * (kernel_tap // 3 - 1)
        step_col = reach_cells + 2 * (kernel_tap % 3 - 1)
        spill = spill.at[
            :, step_row : step_row + tile_rows, step_col : step_col + tile_cols, :
        ].add(offset_back[:, :, :, kernel_tap, :])
    returned = padded_2(spill.astype(jnp.bfloat16), (("row", 1), ("col", 2)), reach_cells).astype(
        spill.dtype
    )
    grad_hidden_a = fold_edges(
        fold_edges(returned, 1, tile_rows, reach_cells), 2, tile_cols, reach_cells
    ).reshape(pixels, inner_width)
    grad_normed_a1 = gelu_back(normed_a1, grad_hidden_a * weight_col)
    grad_reduce_a, gain_a1, bias_a1 = norm_backward(
        grad_normed_a1, unit_a1, inv_a1, scale_a[:inner_width], weight_col, pixel_count
    )
    gw_reduce_a = jnp.einsum(
        "pc,pm->cm", block_in, grad_reduce_a, preferred_element_type=jnp.float32
    )
    grad_block_in = grad_pre_a + jnp.einsum(
        "pm,cm->pc", grad_reduce_a, w_reduce_a, preferred_element_type=jnp.float32
    )
    grad_in = (grad_block_in * weight_col).astype(jnp.bfloat16).reshape(feature_in.shape)
    every_part = (
        lax.psum_scatter(
            gw_reduce_a.astype(jnp.bfloat16), "img", scatter_dimension=0, tiled=True
        ).astype(jnp.float32),
        lax.psum_scatter(
            gw_offset_a.astype(jnp.bfloat16), "img", scatter_dimension=0, tiled=True
        ).astype(jnp.float32),
        lax.psum_scatter(
            gw_deform_a.astype(jnp.bfloat16), "img", scatter_dimension=0, tiled=True
        ).astype(jnp.float32),
        lax.psum_scatter(
            gw_expand_a.astype(jnp.bfloat16), "img", scatter_dimension=0, tiled=True
        ).astype(jnp.float32),
        lax.psum_scatter(
            gw_reduce_b.astype(jnp.bfloat16), "img", scatter_dimension=0, tiled=True
        ).astype(jnp.float32),
        lax.psum_scatter(
            gw_conv_b.astype(jnp.bfloat16), "img", scatter_dimension=0, tiled=True
        ).astype(jnp.float32),
        lax.psum_scatter(
            gw_expand_b.astype(jnp.bfloat16), "img", scatter_dimension=0, tiled=True
        ).astype(jnp.float32),
    )
    every_part = (
        lax.psum(every_part[0].astype(jnp.bfloat16), ("row", "col")).astype(jnp.float32),
        lax.psum(every_part[1].astype(jnp.bfloat16), ("row", "col")).astype(jnp.float32),
        lax.psum(every_part[2].astype(jnp.bfloat16), ("row", "col")).astype(jnp.float32),
        lax.psum(every_part[3].astype(jnp.bfloat16), ("row", "col")).astype(jnp.float32),
        lax.psum(every_part[4].astype(jnp.bfloat16), ("row", "col")).astype(jnp.float32),
        lax.psum(every_part[5].astype(jnp.bfloat16), ("row", "col")).astype(jnp.float32),
        lax.psum(every_part[6].astype(jnp.bfloat16), ("row", "col")).astype(jnp.float32),
    )
    deform_parts = every_part[:4]
    plain_parts = every_part[4:]
    batch_mean_a = jnp.concatenate([mean_a1, mean_a2, mean_a3])
    batch_var_a = jnp.concatenate([spread_a1, spread_a2, spread_a3]) * unbias
    batch_mean_b = jnp.concatenate([mean_b1, mean_b2, mean_b3])
    batch_var_b = jnp.concatenate([spread_b1, spread_b2, spread_b3]) * unbias
    grad_scale_a = jnp.concatenate([gain_a1, gain_a2, gain_a3])
    grad_shift_a = jnp.concatenate([bias_a1, bias_a2, bias_a3])
    grad_scale_b = jnp.concatenate([gain_b1, gain_b2, gain_b3])
    grad_shift_b = jnp.concatenate([bias_b1, bias_b2, bias_b3])
    return (
        feature_out,
        grad_in,
        deform_parts[0],
        deform_parts[1],
        deform_parts[2],
        deform_parts[3],
        grad_scale_a,
        grad_shift_a,
        batch_mean_a,
        batch_var_a,
        plain_parts[0],
        plain_parts[1],
        plain_parts[2],
        grad_scale_b,
        grad_shift_b,
        batch_mean_b,
        batch_var_b,
    )


def solution(mesh):
    in_specs = (
        P("img", "row", "col", None),
        P("img"),
        P("img", "row", "col", None),
        P(),
        P(),
        P(),
        P(),
        P(),
        P(),
        P(),
        P(),
        P(),
        P(),
        P(),
        P("img", "row", "col", None),
    )
    out_specs = (
        P("img", "row", "col", None),
        P("img", "row", "col", None),
        P("img", None),
        P("img", None),
        P("img", None),
        P("img", None),
        P(),
        P(),
        P(),
        P(),
        P("img", None),
        P("img", None),
        P("img", None),
        P(),
        P(),
        P(),
        P(),
    )
    return jax.shard_map(body, mesh=mesh, in_specs=in_specs, out_specs=out_specs, check_vma=False)
```

profile of v0, /device:TPU:0, one launch (start us, length us, event | category | flops | bytes accessed | tf_op | source)
XLA Modules:
  0.0 2411.5 jit_solution(14507500194639954905)
XLA Ops:
  17.0 42.0 %psum.217 = f32[512]{0:T(512)S(1)} all-reduce(f32[512]{0:T(512)S(1)} %get-tuple-element.527), channel_id=1, replica_groups=mesh['img'=4,'row'=4,'col'=2] {'img','row','col'}, use_global_device_ids=true, to_apply=%region_1.2 | all-reduce | flops 512 | bytes 4096 | tf_op jit(solution)/shard_map/psum | solution.py:38
  60.8 40.2 %psum.218 = f32[512]{0:T(512)S(1)} all-reduce(f32[512]{0:T(512)S(1)} %multiply_reduce_fusion.15), channel_id=1, replica_groups=mesh['img'=4,'row'=4,'col'=2] {'img','row','col'}, use_global_device_ids=true, to_apply=%region_3.4 | all-reduce | flops 512 | bytes 4096 | tf_op jit(solution)/shard_map/psum | solution.py:42
  217.7 211.6 %while.56 = (s32[]{:T(128)}, bf16[2,9,512,512]{3,2,1,0:T(8,128)(2,1)}, s32[2,9,512,4]{2,3,1,0:T(4,128)S(1)}, bf16[2,9,512,4]{2,3,1,0:T(4,128)(2,1)S(1)}, bf16[2,...) while((s32[]{:T(128)}, bf16[2,9,512,512]{3,2,1,0:T(8,128)(2,1)}, ...), condition=%wide.region_8.9_spmd, body=%wide.region_4.8_spmd.sunk | while | flops 731553792 | bytes 19063148 | solution.py:216
  220.5 98.1 %while.59 = (s32[]{:T(128)}, bf16[9,512,512]{2,1,0:T(8,128)(2,1)}, s32[9,512,4]{1,2,0:T(4,128)}, bf16[9,512,4]{1,2,0:T(4,128)(2,1)S(1)}, bf16[1380,512]{1,0:T(8,128)(2,1)S(1)}, /*index=5*/s32[]{:T(128)}) while((s32[]{:T(128)}, bf16[9,512,512]{2,1,0:T(8,128)(2,1)}, s32[9,512,4]{1,2,0:T(4,128)}, bf16[9,512,4]{1,2,0:T(4,128)(2,1)S(1)}, ...), condition=%wide.region_7.7_spmd.clone, body=%wide.region_5.6_spmd.clone.sunk | while | flops 731553792 | bytes 4808793 | solution.py:131
  326.2 98.1 %while.59 = (s32[]{:T(128)}, bf16[9,512,512]{2,1,0:T(8,128)(2,1)}, s32[9,512,4]{1,2,0:T(4,128)}, bf16[9,512,4]{1,2,0:T(4,128)(2,1)S(1)}, bf16[1380,512]{1,0:T(8,128)(2,1)S(1)}, /*index=5*/s32[]{:T(128)}) while((s32[]{:T(128)}, bf16[9,512,512]{2,1,0:T(8,128)(2,1)}, s32[9,512,4]{1,2,0:T(4,128)}, bf16[9,512,4]{1,2,0:T(4,128)(2,1)S(1)}, ...), condition=%wide.region_7.7_spmd.clone, body=%wide.region_5.6_spmd.clone.sunk | while | flops 731553792 | bytes 4808793 | solution.py:131
  487.9 40.1 %psum.220 = f32[512]{0:T(512)S(1)} all-reduce(f32[512]{0:T(512)S(1)} %multiply_reduce_fusion.14), channel_id=1, replica_groups=mesh['img'=4,'row'=4,'col'=2] {'img','row','col'}, use_global_device_ids=true, to_apply=%region_12.13 | all-reduce | flops 512 | bytes 4096 | tf_op jit(solution)/shard_map/psum | solution.py:42
  541.8 40.0 %psum.221 = f32[2048]{0:T(1024)S(1)} all-reduce(f32[2048]{0:T(1024)S(1)} %get-tuple-element.531), channel_id=1, replica_groups=mesh['img'=4,'row'=4,'col'=2] {'img','row','col'}, use_global_device_ids=true, to_apply=%region_14.15 | all-reduce | flops 2048 | bytes 16384 | tf_op jit(solution)/shard_map/psum | solution.py:38
  586.3 40.4 %psum.222 = f32[2048]{0:T(1024)S(1)} all-reduce(f32[2048]{0:T(1024)S(1)} %multiply_reduce_fusion.4), channel_id=1, replica_groups=mesh['img'=4,'row'=4,'col'=2] {'img','row','col'}, use_global_device_ids=true, to_apply=%region_16.17 | all-reduce | flops 2048 | bytes 16384 | tf_op jit(solution)/shard_map/psum | solution.py:42
  653.8 40.0 %psum.223 = f32[512]{0:T(512)S(1)} all-reduce(f32[512]{0:T(512)S(1)} %get-tuple-element.533), channel_id=1, replica_groups=mesh['img'=4,'row'=4,'col'=2] {'img','row','col'}, use_global_device_ids=true, to_apply=%region_18.19 | all-reduce | flops 512 | bytes 4096 | tf_op jit(solution)/shard_map/psum | solution.py:38
  695.7 40.2 %psum.224 = f32[512]{0:T(512)S(1)} all-reduce(f32[512]{0:T(512)S(1)} %multiply_reduce_fusion.12), channel_id=1, replica_groups=mesh['img'=4,'row'=4,'col'=2] {'img','row','col'}, use_global_device_ids=true, to_apply=%region_20.21 | all-reduce | flops 512 | bytes 4096 | tf_op jit(solution)/shard_map/psum | solution.py:42
  861.1 41.4 %psum.226 = f32[512]{0:T(512)S(1)} all-reduce(f32[512]{0:T(512)S(1)} %multiply_reduce_fusion.10), channel_id=1, replica_groups=mesh['img'=4,'row'=4,'col'=2] {'img','row','col'}, use_global_device_ids=true, to_apply=%region_24.25 | all-reduce | flops 512 | bytes 4096 | tf_op jit(solution)/shard_map/psum | solution.py:42
  959.6 41.4 %psum.228 = f32[2048]{0:T(1024)S(1)} all-reduce(f32[2048]{0:T(1024)S(1)} %multiply_reduce_fusion.2), channel_id=1, replica_groups=mesh['img'=4,'row'=4,'col'=2] {'img','row','col'}, use_global_device_ids=true, to_apply=%region_28.29 | all-reduce | flops 2048 | bytes 16384 | tf_op jit(solution)/shard_map/psum | solution.py:42
  1085.9 41.4 %all-reduce.6 = (f32[512]{0:T(512)S(1)}, f32[512]{0:T(512)S(1)}) all-reduce(f32[512]{0:T(512)S(1)} %get-tuple-element.367, f32[512]{0:T(512)S(1)} %get-tuple-element.366), channel_id=1, replica_groups=mesh['img'=4,'row'=4,'col'=2] {'img','row','col'}, use_global_device_ids=true, to_apply=%region_36.37 | all-reduce | flops 1024 | bytes 8192 | tf_op jit(solution)/shard_map/psum | solution.py:51
  1163.8 39.4 %all-reduce.5 = (f32[512]{0:T(512)S(1)}, f32[512]{0:T(512)S(1)}) all-reduce(f32[512]{0:T(512)S(1)} %get-tuple-element.365, f32[512]{0:T(512)S(1)} %get-tuple-element.364), channel_id=1, replica_groups=mesh['img'=4,'row'=4,'col'=2] {'img','row','col'}, use_global_device_ids=true, to_apply=%region_40.41 | all-reduce | flops 1024 | bytes 8192 | tf_op jit(solution)/shard_map/psum | solution.py:51
  1223.2 40.9 %all-reduce.4 = (f32[2048]{0:T(1024)S(1)}, f32[2048]{0:T(1024)S(1)}) all-reduce(f32[2048]{0:T(1024)S(1)} %get-tuple-element.357, f32[2048]{0:T(1024)S(1)} %get-tuple-element.356), channel_id=1, replica_groups=mesh['img'=4,'row'=4,'col'=2] {'img','row','col'}, use_global_device_ids=true, to_apply=%region_44.45 | all-reduce | flops 4096 | bytes 32768 | tf_op jit(solution)/shard_map/psum | solution.py:51
  1276.7 39.5 %all-reduce.3 = (f32[512]{0:T(512)S(1)}, f32[512]{0:T(512)S(1)}) all-reduce(f32[512]{0:T(512)S(1)} %get-tuple-element.363, f32[512]{0:T(512)S(1)} %get-tuple-element.362), channel_id=1, replica_groups=mesh['img'=4,'row'=4,'col'=2] {'img','row','col'}, use_global_device_ids=true, to_apply=%region_48.49 | all-reduce | flops 1024 | bytes 8192 | tf_op jit(solution)/shard_map/psum | solution.py:51
  1328.8 389.7 %while.58 = (s32[]{:T(128)}, f32[2,1380,512]{2,1,0:T(8,128)}, f32[2,9,512,4]{2,3,1,0:T(4,128)S(1)}, s32[2,9,512,4]{2,3,1,0:T(4,128)S(1)}, bf16[2,9,512,4]{2,3,1,...) while((s32[]{:T(128)}, f32[2,1380,512]{2,1,0:T(8,128)}, ...), condition=%wide.region_54.55_spmd, body=%wide.region_49.54_spmd.sunk | while | flops 1461872640 | bytes 34959712 | solution.py:318
  1336.2 185.6 %while.60 = (s32[]{:T(128)}, f32[1380,512]{1,0:T(8,128)S(1)}, f32[9,512,4]{1,2,0:T(4,128)S(1)}, s32[9,512,4]{1,2,0:T(4,128)S(1)}, bf16[9,512,4]{1,2,0:T(4,128)(2...) while((s32[]{:T(128)}, f32[1380,512]{1,0:T(8,128)S(1)}, ...), condition=%wide.region_53.53_spmd.clone, body=%wide.region_50.52_spmd.clone.sunk | while | flops 1461872640 | bytes 16666755 | solution.py:148
  1531.1 185.6 %while.60 = (s32[]{:T(128)}, f32[1380,512]{1,0:T(8,128)S(1)}, f32[9,512,4]{1,2,0:T(4,128)S(1)}, s32[9,512,4]{1,2,0:T(4,128)S(1)}, bf16[9,512,4]{1,2,0:T(4,128)(2...) while((s32[]{:T(128)}, f32[1380,512]{1,0:T(8,128)S(1)}, ...), condition=%wide.region_53.53_spmd.clone, body=%wide.region_50.52_spmd.clone.sunk | while | flops 1461872640 | bytes 16666755 | solution.py:148
  1760.1 53.4 %fusion.114 = (f32[2,16,32,1,512]{4,3,2,1,0:T(1,128)S(1)}, f32[2,16,32,1,512]{4,3,2,1,0:T(1,128)}, f32[2,16,32,1,512]{4,3,2,1,0:T(1,128)}, f32[2,16,32,1,512]{4,...) fusion(f32[2,16,32,9,512]{4,3,2,1,0:T(8,128)} %reshape.701), kind=kLoop, calls=%fused_computation.362 | loop fusion | bytes 37748736 | tf_op jit(solution)/shard_map/slice | solution.py:340
  1996.8 51.4 %all-reduce.2 = (f32[512]{0:T(512)S(1)}, f32[512]{0:T(512)S(1)}) all-reduce(f32[512]{0:T(512)S(1)} %get-tuple-element.361, f32[512]{0:T(512)S(1)} %get-tuple-element.360), channel_id=1, replica_groups=mesh['img'=4,'row'=4,'col'=2] {'img','row','col'}, use_global_device_ids=true, to_apply=%region_58.59 | all-reduce | flops 1024 | bytes 8192 | tf_op jit(solution)/shard_map/psum | solution.py:51
  2098.6 86.8 %reduce-scatter.18.cloned.1.call-done = bf16[1152,512]{1,0:T(8,128)(2,1)} async-done(((bf16[4608,512]{1,0:T(8,128)(2,1)}), bf16[1152,512]{1,0:T(8,128)(2,1)}) %reduce-scatter.18.cloned.1.call-update) | async-done | bytes 1179664 | tf_op jit(solution)/shard_map/reduce_scatter | solution.py:374
  2185.3 88.0 %reduce-scatter.12.cloned.1.call-done = bf16[1152,512]{1,0:T(8,128)(2,1)} async-done(((bf16[4608,512]{1,0:T(8,128)(2,1)}), bf16[1152,512]{1,0:T(8,128)(2,1)}) %reduce-scatter.12.cloned.1.call-update) | async-done | bytes 1179664 | tf_op jit(solution)/shard_map/reduce_scatter | solution.py:365
  2343.0 51.4 %all-reduce.11.cloned.1.call-done = (bf16[512,512]{1,0:T(8,128)(2,1)}, bf16[1152,512]{1,0:T(8,128)(2,1)}, bf16[128,2048]{1,0:T(8,128)(2,1)}, bf16[512,512]{1,0:T...) async-done(((bf16[512,512]{1,0:T(8,128)(2,1)}, bf16[1152,512]{1,0:T(8,128)(2,1)}, bf16[128,2048]{1,0:T(8,128)(2,1)}, bf16[512,512]{1,0:T(8,128)(2,1)}, ...) | async-done | bytes 4456464 | tf_op jit(solution)/shard_map/psum | solution.py:382
  (741 shorter events, 1536.1 us)
Async XLA Ops:
  7.2 2089.3 %reduce-scatter.20.cloned.1.call-start = ((), (), s32[]{:S(2)}) async-start(), calls=%async_computation.12 | async-start | bytes 2621440 | tf_op jit(solution)/shard_map/reduce_scatter | solution.py:377
  108.4 13.1 collective-permute-start
  112.6 20.6 collective-permute-start.1
  135.1 11.8 collective-permute-start.3
  136.3 10.5 collective-permute-start.2
  742.5 6.7 collective-permute-start.4
  746.7 7.2 collective-permute-start.5
  754.6 6.3 collective-permute-start.7
  755.9 5.0 collective-permute-start.6
  1131.1 9.4 collective-permute-start.8
  1135.3 6.9 collective-permute-start.9
  1140.4 956.1 %reduce-scatter.14.cloned.1.call-start = ((), (), s32[]{:S(2)}) async-start(), calls=%async_computation.9 | async-start | bytes 2621440 | tf_op jit(solution)/shard_map/reduce_scatter | solution.py:368
  1142.3 2.8 collective-permute-start.11
  1143.6 3.2 collective-permute-start.10
  1813.5 283.0 %reduce-scatter.16.cloned.1.call-start = ((), (), s32[]{:S(2)}) async-start(), calls=%async_computation.10 | async-start | bytes 2621440 | tf_op jit(solution)/shard_map/reduce_scatter | solution.py:371
  1956.4 20.2 collective-permute-start.13
  1957.7 20.1 collective-permute-start.12
  1967.3 131.3 %reduce-scatter.10.cloned.1.call-start = ((), (), s32[]{:S(2)}) async-start(), calls=%async_computation.7 | async-start | bytes 2621440 | tf_op jit(solution)/shard_map/reduce_scatter | solution.py:359
  1980.1 5.3 collective-permute-start.15
  1982.2 4.7 collective-permute-start.14
  2054.8 130.5 %reduce-scatter.18.cloned.1.call-start = ((), (), s32[]{:S(2)}) async-start(), calls=%async_computation.11 | async-start | bytes 5898240 | tf_op jit(solution)/shard_map/reduce_scatter | solution.py:374
  2066.5 206.8 %reduce-scatter.12.cloned.1.call-start = ((), (), s32[]{:S(2)}) async-start(), calls=%async_computation.8 | async-start | bytes 5898240 | tf_op jit(solution)/shard_map/reduce_scatter | solution.py:365
  2089.8 216.1 %reduce-scatter.22.cloned.1.call-start = ((), (), s32[]{:S(2)}) async-start(), calls=%async_computation.13 | async-start | bytes 1474560
  2096.4 297.9 %all-reduce.11.cloned.1.call-start = ((), (), s32[]{:S(2)}) async-start(), calls=%async_computation.14 | async-start | bytes 8912896 | tf_op jit(solution)/shard_map/psum | solution.py:382
  (143 other events, 5675.5 us)
Sparse Core Ops, SparseCore 0:
  1140.5 44.8 reduce-scatter.19
  1813.6 44.4 reduce-scatter.13
  1967.4 43.2 reduce-scatter.15
  2054.9 43.6 reduce-scatter.9
  2100.7 84.5 reduce-scatter.17
  2187.5 85.7 reduce-scatter.11
  2276.2 29.6 reduce-scatter.21
  2309.9 84.3 all-reduce.10
where the time goes:
time: 2430 us; the launch traced here: 2410 us
  blocking collectives  759 us (31%)
  other arithmetic  646 us (27%)
  local copies, waits for them, and re-layouts  387 us (16%)
  waiting for transfers between devices  296 us (12%)
  matrix products  264 us (11%)
  starting transfers between devices  42.6 us (2%)
    reduce_sum x18, other arithmetic, return_one_tap(): picked = jnp.sum(jnp.where(matches, scores[:, None, :], 0.0), axis=2)  283 us
    psum x6, blocking collectives, norm_backward(): lax.psum((jnp.sum(grad_normed, axis=0), jnp.sum(grad_normed * unit_value,...  251 us
    psum x6, blocking collectives, norm_forward(): lax.psum(jnp.sum(centered * centered * weight_col, axis=0), ('img', 'row'...  244 us
    psum x6, blocking collectives, norm_forward(): lax.psum(jnp.sum(pre_norm * weight_col, axis=0), ('img', 'row', 'col'))  238 us
    reduce_sum x18, other arithmetic, sample_table(): jnp.sum(jnp.where(matches, weight_tap[:, :, None].astype(jnp.float32), 0....  151 us
    scatter-add x9, local copies, waits for them, and re-layouts, body(): spill = spill.at[:, step_row:step_row + tile_rows, step_col:step_col + ti...  98.1 us
    reduce_scatter x1, waiting for transfers between devices, body(): lax.psum_scatter(gw_deform_a.astype(jnp.bfloat16), 'img', scatter_dimensi...  88 us
    reduce_scatter x1, waiting for transfers between devices, body(): lax.psum_scatter(gw_conv_b.astype(jnp.bfloat16), 'img', scatter_dimension...  86.8 us
  transfers between devices with their start and end apart: 24, of which 13 were waited for; matrix products, arithmetic and copies ran while one was open for 32% of the time, Pallas kernels for 0%

commit v1 on v0

v1 whole, which is shorter than its diff:
```python
import functools

import jax
import jax.numpy as jnp
import numpy as np
from jax import lax
from jax.experimental import pallas as pl
from jax.experimental.pallas import tpu as pltpu
from jax.sharding import PartitionSpec as P

LONG = 64
SHORT = 44
BOUND = 4
EPSILON = 1e-05
MESH = pl.DeviceIdType.MESH
VMEM = pl.BlockSpec(memory_space=pltpu.VMEM)
VMEM_LIMIT = 60 * 1024 * 1024
F32 = jnp.float32
BF16 = jnp.bfloat16
REACH = BOUND + 3
PAD = 8
HALF = 16
CID = {"stats512": 0, "sums512": 1, "stats2048": 2, "sums2048": 3, "halo_a": 4, "halo_b": 5, "spill": 6}


def gelu_exact(values):
    return jax.nn.gelu(values, approximate=False)


def gelu_back(values, upstream):
    return jax.vjp(gelu_exact, values)[1](upstream)[0]


def group_of(axes):
    sizes = [lax.axis_size(a) for a in axes]
    total = int(np.prod(sizes))
    place = lax.axis_index(axes[0])
    for axis, size in zip(axes[1:], sizes[1:]):
        place = place * size + lax.axis_index(axis)

    def device(step):
        spot = lax.rem(place + step, total)
        coords = {}
        for axis, size in zip(reversed(axes), reversed(sizes)):
            coords[axis] = lax.rem(spot, size)
            spot = spot // size
        return coords

    return place, total, device


PLANE = ("row", "col")
LINE = ("img",)


def entry_barrier(groups):
    barrier = pltpu.get_barrier_semaphore()
    count = 0
    for axes in groups:
        _, total, device = group_of(axes)
        for step in range(1, total):
            pl.semaphore_signal(barrier, inc=1, device_id=device(step), device_id_type=MESH)
        count += total - 1
    pl.semaphore_wait(barrier, count)


def gather_start(axes, slots, send_sem, recv_sem):
    _, total, device = group_of(axes)
    for step in range(1, total):
        pltpu.make_async_remote_copy(
            src_ref=slots.at[0],
            dst_ref=slots.at[step],
            send_sem=send_sem,
            recv_sem=recv_sem,
            device_id=device(step),
            device_id_type=MESH,
        ).start()


def gather_wait(axes, slots, sem):
    _, total, _ = group_of(axes)
    others = slots.at[pl.ds(1, total - 1)]
    pltpu.make_async_copy(others, others, sem).wait()


def in_order(axes, slots):
    place, total, _ = group_of(axes)
    return [slots[lax.rem(place - spot + total, total)] for spot in range(total)]


def sums_kernel(x_ref, o_ref, slots1, slots2, send_sems, recv_sems):
    entry_barrier((PLANE, LINE))
    slots1[0] = x_ref[...]
    gather_start(PLANE, slots1, send_sems.at[0], recv_sems.at[0])
    gather_wait(PLANE, slots1, recv_sems.at[0])
    slots2[0] = functools.reduce(lambda a, b: a + b, in_order(PLANE, slots1))
    gather_start(LINE, slots2, send_sems.at[1], recv_sems.at[1])
    gather_wait(LINE, slots2, recv_sems.at[1])
    o_ref[...] = functools.reduce(lambda a, b: a + b, in_order(LINE, slots2))
    gather_wait(PLANE, slots1, send_sems.at[0])
    gather_wait(LINE, slots2, send_sems.at[1])


def stats_kernel(plane_count, x_ref, count_ref, o_ref, slots1, slots2, send_sems, recv_sems):
    entry_barrier((PLANE, LINE))
    half = x_ref.shape[0] // 2
    total_count = plane_count * lax.axis_size("img")
    slots1[0] = x_ref[...]
    gather_start(PLANE, slots1, send_sems.at[0], recv_sems.at[0])
    gather_wait(PLANE, slots1, recv_sems.at[0])
    parts = in_order(PLANE, slots1)
    total = functools.reduce(lambda a, b: a + b, [p[:half] for p in parts])
    center = total / plane_count
    spread = functools.reduce(lambda a, b: a + b, [p[half:] for p in parts])
    for spot, part in enumerate(parts):
        count = count_ref[spot : spot + 1, :]
        away = part[:half] / jnp.maximum(count, 1.0) - center
        spread = spread + count * (away * away)
    slots2[0, :half] = total
    slots2[0, half:] = spread
    gather_start(LINE, slots2, send_sems.at[1], recv_sems.at[1])
    gather_wait(LINE, slots2, recv_sems.at[1])
    parts = in_order(LINE, slots2)
    center = functools.reduce(lambda a, b: a + b, [p[:half] for p in parts]) / total_count
    spread = functools.reduce(lambda a, b: a + b, [p[half:] for p in parts])
    for part in parts:
        away = part[:half] / plane_count - center
        spread = spread + plane_count * (away * away)
    o_ref[:half] = center
    o_ref[half:] = spread / total_count
    gather_wait(PLANE, slots1, send_sems.at[0])
    gather_wait(LINE, slots2, send_sems.at[1])


def exchange(kernel, name, rows, operands):
    scratch = []
    for axes in (PLANE, LINE):
        total = int(np.prod([lax.axis_size(a) for a in axes]))
        scratch.append(pltpu.VMEM((total, rows, 128), F32))
    scratch += [pltpu.SemaphoreType.DMA((2,)), pltpu.SemaphoreType.DMA((2,))]
    return pl.pallas_call(
        kernel,
        out_shape=jax.ShapeDtypeStruct((rows, 128), F32),
        in_specs=[VMEM] * len(operands),
        out_specs=VMEM,
        scratch_shapes=scratch,
        compiler_params=pltpu.CompilerParams(collective_id=CID[name], has_side_effects=True),
        name=name,
    )(*operands)


def sums_over_devices(first, second):
    width = first.shape[0]
    both = jnp.concatenate([first, second]).reshape(-1, 128)
    out = exchange(sums_kernel, f"sums{width}", both.shape[0], (both,)).reshape(2, width)
    return out[0], out[1]


def stats_over_devices(total, spread, counts, plane_count):
    width = total.shape[0]
    both = jnp.concatenate([total, spread]).reshape(-1, 128)
    kernel = functools.partial(stats_kernel, plane_count)
    out = exchange(kernel, f"stats{width}", both.shape[0], (both, counts)).reshape(2, width)
    return out[0], out[1]


def halo_peers():
    row, rows, col = lax.axis_index("row"), lax.axis_size("row"), lax.axis_index("col")
    return row, rows, col, {"col": 1 - col}, {"row": row - 1}, {"row": row + 1}


def halo_barrier():
    row, rows, _, pair, above, below = halo_peers()
    barrier = pltpu.get_barrier_semaphore()
    pl.semaphore_signal(barrier, inc=1, device_id=pair, device_id_type=MESH)

    @pl.when(row > 0)
    def _():
        pl.semaphore_signal(barrier, inc=1, device_id=above, device_id_type=MESH)

    @pl.when(row < rows - 1)
    def _():
        pl.semaphore_signal(barrier, inc=1, device_id=below, device_id_type=MESH)

    count = 1 + (row > 0).astype(jnp.int32) + (row < rows - 1).astype(jnp.int32)
    pl.semaphore_wait(barrier, count)


def halo_kernel(pad, reach, h_ref, o_ref, send_sems, recv_sems):
    row, rows, col, pair, above, below = halo_peers()
    tile_rows, tile_cols = h_ref.shape[1], h_ref.shape[2]
    off = pl.multiple_of(HALF * col, HALF)
    spot = pl.multiple_of(2 * HALF * col, HALF)
    own = pl.ds(off, tile_cols)
    mid = pl.ds(HALF, HALF)
    upper = pl.ds(pad - reach, reach)
    lower = pl.ds(pad + tile_rows, reach)
    zero_row = jnp.zeros((h_ref.shape[0],) + o_ref.shape[2:], o_ref.dtype)

    def blank(at):
        for k in range(at.start, at.stop):
            o_ref[:, k] = zero_row

    blank(slice(0, pad - reach))
    blank(slice(pad + tile_rows + reach, 2 * pad + tile_rows))

    @pl.when(row == 0)
    def _():
        blank(slice(pad - reach, pad))

    @pl.when(row == rows - 1)
    def _():
        blank(slice(pad + tile_rows, pad + tile_rows + reach))

    halo_barrier()

    def copy(src, dst, k, device):
        return pltpu.make_async_remote_copy(
            src_ref=src,
            dst_ref=dst,
            send_sem=send_sems.at[k],
            recv_sem=recv_sems.at[k],
            device_id=device,
            device_id_type=MESH,
        )

    to_pair = copy(
        h_ref.at[:, :, pl.ds(pl.multiple_of(HALF * (1 - col), HALF), HALF)],
        o_ref.at[:, pl.ds(pad, tile_rows), pl.ds(spot, HALF)],
        0,
        pair,
    )
    up = copy(h_ref.at[:, pl.ds(0, reach)], o_ref.at[:, lower, own], 1, above)
    down = copy(h_ref.at[:, pl.ds(tile_rows - reach, reach)], o_ref.at[:, upper, own], 2, below)
    from_below = copy(o_ref.at[:, lower, mid], o_ref.at[:, lower, pl.ds(spot, HALF)], 3, pair)
    from_above = copy(o_ref.at[:, upper, mid], o_ref.at[:, upper, pl.ds(spot, HALF)], 4, pair)

    @pl.when(row > 0)
    def _():
        up.start()

    @pl.when(row < rows - 1)
    def _():
        down.start()

    to_pair.start()
    for n in range(h_ref.shape[0]):
        o_ref[n, pl.ds(pad, tile_rows), own, :] = h_ref[n]

    @pl.when(row < rows - 1)
    def _():
        up.wait_recv()
        from_below.start()

    @pl.when(row > 0)
    def _():
        down.wait_recv()
        from_above.start()

    to_pair.wait()

    @pl.when(row < rows - 1)
    def _():
        down.wait_send()
        from_below.wait()

    @pl.when(row > 0)
    def _():
        up.wait_send()
        from_above.wait()


def with_halo(tile, pad, reach, name):
    images, rows, cols, width = tile.shape
    return pl.pallas_call(
        functools.partial(halo_kernel, pad, reach),
        out_shape=jax.ShapeDtypeStruct((images, rows + 2 * pad, cols + HALF, width), tile.dtype),
        in_specs=[VMEM],
        out_specs=VMEM,
        scratch_shapes=[pltpu.SemaphoreType.DMA((5,)), pltpu.SemaphoreType.DMA((5,))],
        compiler_params=pltpu.CompilerParams(
            collective_id=CID[name], has_side_effects=True, vmem_limit_bytes=VMEM_LIMIT
        ),
        name=name,
    )(tile)


def spill_kernel(s_ref, o_ref, side_out, side_in, up_out, down_out, up_in, down_in, send_sems, recv_sems):
    row, rows, col, pair, above, below = halo_peers()
    images, tile_rows, tile_cols, width = o_ref.shape
    off = pl.multiple_of(HALF * col, HALF)
    own = pl.ds(off, tile_cols)
    away = pl.ds(pl.multiple_of(2 * HALF * (1 - col), HALF), HALF)
    near = pl.ds(pl.multiple_of(HALF * (1 - col), HALF), HALF)
    all_rows = s_ref.shape[1]

    def cast_side(k, carry):
        for n in range(images):
            side_out[n, k] = s_ref[n, k, away, :].astype(BF16)
        return carry

    lax.fori_loop(0, all_rows, cast_side, 0)
    halo_barrier()

    def copy(src, dst, k, device):
        return pltpu.make_async_remote_copy(
            src_ref=src,
            dst_ref=dst,
            send_sem=send_sems.at[k],
            recv_sem=recv_sems.at[k],
            device_id=device,
            device_id_type=MESH,
        )

    side = copy(side_out, side_in, 0, pair)
    up = copy(up_out, down_in, 1, above)
    down = copy(down_out, up_in, 2, below)
    side.start()
    side.wait_recv()

    def edge(buffer, first):
        for k in range(REACH):
            for n in range(images):
                wide = s_ref[n, first + k, own, :]
                buffer[n, k] = wide.astype(BF16)
                part = s_ref[n, first + k, pl.ds(HALF, HALF), :]
                buffer[n, k, near, :] = (part + side_in[n, first + k].astype(F32)).astype(BF16)

    @pl.when(row > 0)
    def _():
        edge(up_out, PAD - REACH)
        up.start()

    @pl.when(row < rows - 1)
    def _():
        edge(down_out, PAD + tile_rows)
        down.start()

    def fill(k, carry):
        for n in range(images):
            o_ref[n, k] = s_ref[n, PAD + k, own, :]
            part = s_ref[n, PAD + k, pl.ds(HALF, HALF), :]
            o_ref[n, k, near, :] = part + side_in[n, PAD + k].astype(F32)
        return carry

    lax.fori_loop(0, tile_rows, fill, 0)

    @pl.when(row > 0)
    def _():
        down.wait_recv()
        for k in range(REACH):
            for n in range(images):
                o_ref[n, k] = o_ref[n, k] + up_in[n, k].astype(F32)
        up.wait_send()

    @pl.when(row < rows - 1)
    def _():
        up.wait_recv()
        for k in range(REACH):
            for n in range(images):
                at = tile_rows - REACH + k
                o_ref[n, at] = o_ref[n, at] + down_in[n, k].astype(F32)
        down.wait_send()

    side.wait_send()


def spill_home(spill):
    images, rows, cols, width = spill.shape
    strip = pltpu.VMEM((images, REACH, cols - HALF, width), BF16)
    side = pltpu.VMEM((images, rows, HALF, width), BF16)
    return pl.pallas_call(
        spill_kernel,
        out_shape=jax.ShapeDtypeStruct((images, rows - 2 * PAD, cols - HALF, width), F32),
        in_specs=[VMEM],
        out_specs=VMEM,
        scratch_shapes=[
            side,
            side,
            strip,
            strip,
            strip,
            strip,
            pltpu.SemaphoreType.DMA((3,)),
            pltpu.SemaphoreType.DMA((3,)),
        ],
        compiler_params=pltpu.CompilerParams(
            collective_id=CID["spill"], has_side_effects=True, vmem_limit_bytes=VMEM_LIMIT
        ),
        name="spill",
    )(spill)


BLOCK_ROWS = 8
SPAN = 17
WINDOW = 3 * BLOCK_ROWS


def tap_span(group, cols):
    first = 2 + 2 * group
    start = first * cols // 128 * 128
    stop = -(-(first + SPAN) * cols // 128) * 128
    return first, start, stop


def tap_weights(tap, block, cols, up_ref, left_ref, fr_ref, fc_ref):
    pixels = up_ref.shape[-1]
    up = up_ref[0, tap : tap + 1, :] - block * BLOCK_ROWS
    left = left_ref[0, tap : tap + 1, :]
    fr = fr_ref[0, tap : tap + 1, :]
    fc = fc_ref[0, tap : tap + 1, :]

    def pair(size, at, frac):
        ids = lax.broadcasted_iota(jnp.int32, (size, pixels), 0)
        first, second = ids == at, ids == at + 1
        value = jnp.where(first, 1.0 - frac, jnp.where(second, frac, 0.0))
        slope = jnp.where(second, 1.0, jnp.where(first, -1.0, 0.0))
        return value, slope

    return pair(WINDOW, up, fr) + pair(cols, left, fc)


def write_table(table, lane, row_w, col_w, group, cols):
    first, start, stop = tap_span(group, cols)
    pixels = row_w.shape[1]
    low = start // cols
    high = -(-stop // cols)
    for r in range(low, min(high, WINDOW)):
        table[r * cols : (r + 1) * cols, lane : lane + pixels] = (
            row_w[r : r + 1, :] * col_w
        ).astype(BF16)


def sample_kernel(rim_ref, w_ref, up_ref, left_ref, fr_ref, fc_ref, s_ref, d_ref, table):
    block = pl.program_id(1)
    width = rim_ref.shape[1]
    cols = table.shape[0] // WINDOW
    base = block * (BLOCK_ROWS * cols)
    for tap in range(9):
        row_w, _, col_w, _ = tap_weights(tap, block, cols, up_ref, left_ref, fr_ref, fc_ref)
        write_table(table, 0, row_w, col_w, tap // 3, cols)
        _, start, stop = tap_span(tap // 3, cols)
        cells = pl.ds(pl.multiple_of(base + start, 128), stop - start)
        value = jnp.dot(rim_ref[0, :, cells], table[start:stop, :], preferred_element_type=F32)
        s_ref[tap * width : (tap + 1) * width, :] = value.astype(BF16)
    d_ref[...] = jnp.dot(w_ref[...], s_ref[...], preferred_element_type=F32)


def sample_forward(rim_t, w_t, up, left, fr, fc, cols):
    images, width, cells = rim_t.shape
    pixels = up.shape[-1]
    blocks = 2
    step = pixels // blocks
    tap_spec = pl.BlockSpec((1, 9, step), lambda i, b: (i, 0, b))
    return pl.pallas_call(
        sample_kernel,
        grid=(images, blocks),
        out_shape=(
            jax.ShapeDtypeStruct((9 * width, images * pixels), BF16),
            jax.ShapeDtypeStruct((width, images * pixels), F32),
        ),
        in_specs=[
            pl.BlockSpec((1, width, cells), lambda i, b: (i, 0, 0)),
            pl.BlockSpec((width, 9 * width), lambda i, b: (0, 0)),
            tap_spec,
            tap_spec,
            tap_spec,
            tap_spec,
        ],
        out_specs=(
            pl.BlockSpec((9 * width, step), lambda i, b: (0, i * blocks + b)),
            pl.BlockSpec((width, step), lambda i, b: (0, i * blocks + b)),
        ),
        scratch_shapes=[pltpu.VMEM((WINDOW * cols, step), BF16)],
        compiler_params=pltpu.CompilerParams(vmem_limit_bytes=VMEM_LIMIT),
        name="sample",
    )(rim_t, w_t, up, left, fr, fc)


def unsample_kernel(
    rim_ref, g_ref, w_ref, up_ref, left_ref, fr_ref, fc_ref, spill_ref, gr_ref, gc_ref, table, grads
):
    block = pl.program_id(1)
    width = rim_ref.shape[2]
    cols = table.shape[0] // WINDOW
    pixels = up_ref.shape[-1]
    base = block * (BLOCK_ROWS * cols)

    @pl.when(block == 0)
    def _():
        spill_ref[...] = jnp.zeros_like(spill_ref)

    for group in range(3):
        first, start, stop = tap_span(group, cols)
        cells = pl.ds(pl.multiple_of(base + start, 128), stop - start)
        for j in range(3):
            tap = 3 * group + j
            lanes = slice(j * pixels, (j + 1) * pixels)
            row_w, row_s, col_w, col_s = tap_weights(
                tap, block, cols, up_ref, left_ref, fr_ref, fc_ref
            )
            write_table(table, j * pixels, row_w, col_w, group, cols)
            grad = jnp.dot(
                w_ref[tap * width : (tap + 1) * width, :], g_ref[...], preferred_element_type=F32
            ).astype(BF16)
            grads[:, lanes] = grad
            scores = jnp.dot(rim_ref[0, cells, :], grad, preferred_element_type=F32)
            by_value = jnp.zeros((cols, pixels), F32)
            by_slope = jnp.zeros((cols, pixels), F32)
            for r in range(first, first + SPAN):
                line = scores[r * cols - start : (r + 1) * cols - start]
                by_value = by_value + line * row_w[r : r + 1, :]
                by_slope = by_slope + line * row_s[r : r + 1, :]
            gr_ref[0, tap : tap + 1, :] = jnp.sum(by_slope * col_w, axis=0, keepdims=True)
            gc_ref[0, tap : tap + 1, :] = jnp.sum(by_value * col_s, axis=0, keepdims=True)
        spill_ref[0, cells, :] += lax.dot_general(
            table[start:stop, :], grads[...], (((1,), (1,)), ((), ())), preferred_element_type=F32
        )


def sample_backward(rim, grad_t, w, up, left, fr, fc, cols):
    images, cells, width = rim.shape
    pixels = up.shape[-1]
    blocks = 2
    step = pixels // blocks
    tap_spec = pl.BlockSpec((1, 9, step), lambda i, b: (i, 0, b))
    map_spec = pl.BlockSpec((1, cells, width), lambda i, b: (i, 0, 0))
    return pl.pallas_call(
        unsample_kernel,
        grid=(images, blocks),
        out_shape=(
            jax.ShapeDtypeStruct(rim.shape, F32),
            jax.ShapeDtypeStruct(up.shape, F32),
            jax.ShapeDtypeStruct(up.shape, F32),
        ),
        in_specs=[
            map_spec,
            pl.BlockSpec((width, step), lambda i, b: (0, i * blocks + b)),
            pl.BlockSpec((9 * width, width), lambda i, b: (0, 0)),
            tap_spec,
            tap_spec,
            tap_spec,
            tap_spec,
        ],
        out_specs=(map_spec, tap_spec, tap_spec),
        scratch_shapes=[
            pltpu.VMEM((WINDOW * cols, 3 * step), BF16),
            pltpu.VMEM((width, 3 * step), BF16),
        ],
        compiler_params=pltpu.CompilerParams(vmem_limit_bytes=VMEM_LIMIT),
        name="unsample",
    )(rim, grad_t, w, up, left, fr, fc)


def build_shifted(rim_ref, shifted):
    images, rows, cols, width = rim_ref.shape
    col = lax.axis_index("col")
    tile = cols - HALF

    def fill(first):
        def one_row(k, carry):
            for n in range(images):
                line = rim_ref[n, k].astype(F32)
                none = jnp.zeros((2, width), F32)
                for d in range(3):
                    at = first + 2 * (d - 1)
                    if at < 0:
                        part = jnp.concatenate([none, line[: tile - 2]], axis=0)
                    elif at + tile > cols:
                        part = jnp.concatenate([line[at:], none], axis=0)
                    else:
                        part = line[at : at + tile]
                    shifted[n, k, :, d * width : (d + 1) * width] = part.astype(BF16)
            return carry

        lax.fori_loop(0, rows, one_row, 0)

    @pl.when(col == 0)
    def _():
        fill(0)

    @pl.when(col == 1)
    def _():
        fill(HALF)


def conv_kernel(rim_ref, w_ref, o_ref, shifted):
    images, rows, cols, width = rim_ref.shape
    build_shifted(rim_ref, shifted)
    tile_rows = rows - 4
    pixels = tile_rows * (cols - HALF)
    for n in range(images):
        total = None
        for i in range(3):
            taps = shifted[n, 2 * i : 2 * i + tile_rows].reshape(pixels, 3 * width)
            term = jnp.dot(
                taps, w_ref[3 * i * width : 3 * (i + 1) * width, :], preferred_element_type=F32
            )
            total = term if total is None else total + term
        o_ref[n * pixels : (n + 1) * pixels, :] = total


def conv_forward(rim, w):
    images, rows, cols, width = rim.shape
    pixels = images * (rows - 4) * (cols - HALF)
    return pl.pallas_call(
        conv_kernel,
        out_shape=jax.ShapeDtypeStruct((pixels, width), F32),
        in_specs=[VMEM, VMEM],
        out_specs=VMEM,
        scratch_shapes=[pltpu.VMEM((images, rows, cols - HALF, 3 * width), BF16)],
        compiler_params=pltpu.CompilerParams(vmem_limit_bytes=VMEM_LIMIT),
        name="conv",
    )(rim, w)


def unconv_kernel(rim_ref, back_ref, w_ref, g_ref, o_ref, gw_ref, shifted):
    images, rows, cols, width = rim_ref.shape
    tile_rows = rows - 4
    pixels = tile_rows * (cols - HALF)
    build_shifted(rim_ref, shifted)
    for i in range(3):
        total = None
        for n in range(images):
            taps = shifted[n, 2 * i : 2 * i + tile_rows].reshape(pixels, 3 * width)
            term = lax.dot_general(
                g_ref[n * pixels : (n + 1) * pixels, :],
                taps,
                (((0,), (0,)), ((), ())),
                preferred_element_type=F32,
            )
            total = term if total is None else total + term
        gw_ref[:, 3 * i * width : 3 * (i + 1) * width] = total.astype(BF16)
    build_shifted(back_ref, shifted)
    for n in range(images):
        total = None
        for tap in range(9):
            i, d = 2 - tap // 3, 2 - tap % 3
            grads = shifted[n, 2 * i : 2 * i + tile_rows, :, d * width : (d + 1) * width]
            term = lax.dot_general(
                grads.reshape(pixels, width),
                w_ref[tap * width : (tap + 1) * width, :],
                (((1,), (1,)), ((), ())),
                preferred_element_type=F32,
            )
            total = term if total is None else total + term
        o_ref[n * pixels : (n + 1) * pixels, :] = total


def conv_backward(rim, back_rim, w, grad):
    images, rows, cols, width = rim.shape
    return pl.pallas_call(
        unconv_kernel,
        out_shape=(
            jax.ShapeDtypeStruct(grad.shape, F32),
            jax.ShapeDtypeStruct((width, 9 * width), BF16),
        ),
        in_specs=[VMEM] * 4,
        out_specs=(VMEM, VMEM),
        scratch_shapes=[pltpu.VMEM((images, rows, cols - HALF, 3 * width), BF16)],
        compiler_params=pltpu.CompilerParams(vmem_limit_bytes=VMEM_LIMIT),
        name="unconv",
    )(rim, back_rim, w, grad)


def local_stats(values, weight_col, count):
    total = jnp.sum(values * weight_col, axis=0)
    away = values - total / jnp.maximum(count, 1.0)
    return total, jnp.sum(away * away * weight_col, axis=0)


def norm_forward(pre_norm, weight_col, norm_gain, norm_shift, counts):
    own_count, all_counts, plane_count = counts
    total, spread = local_stats(pre_norm, weight_col, own_count)
    batch_mean, spread = stats_over_devices(total, spread, all_counts, plane_count)
    inv_std = lax.rsqrt(spread + EPSILON)
    unit_value = (pre_norm - batch_mean) * inv_std
    return (unit_value * norm_gain + norm_shift, unit_value, inv_std, batch_mean, spread)


def norm_backward(grad_normed, unit_value, inv_std, norm_gain, weight_col, pixel_count):
    sum_grad, sum_unit = sums_over_devices(
        jnp.sum(grad_normed, axis=0), jnp.sum(grad_normed * unit_value, axis=0)
    )
    grad_pre = (
        norm_gain
        * inv_std
        * (grad_normed - (sum_grad + unit_value * sum_unit) / pixel_count)
        * weight_col
    )
    return (grad_pre.astype(BF16), sum_unit, sum_grad)


def inside_counts(orientation, tile_rows, tile_cols):
    rows, cols = lax.axis_size("row"), lax.axis_size("col")
    tall = np.clip(SHORT - np.arange(rows) * tile_rows, 0, tile_rows)[:, None] * tile_cols
    wide = np.clip(SHORT - np.arange(cols) * tile_cols, 0, tile_cols)[None, :] * tile_rows
    tall = jnp.asarray(np.broadcast_to(tall, (rows, cols)).reshape(-1), F32)
    wide = jnp.asarray(np.broadcast_to(wide, (rows, cols)).reshape(-1), F32)
    flat = (orientation == 0).astype(F32)[:, None]
    each = jnp.sum(flat * tall + (1.0 - flat) * wide, axis=0)
    place = lax.axis_index("row") * cols + lax.axis_index("col")
    own = lax.dynamic_index_in_dim(each, place, keepdims=False)
    return own, jnp.broadcast_to(each[:, None], (rows * cols, 128))


def body(
    feature_in,
    orientation,
    offset_base,
    w_reduce_a,
    w_offset_a,
    w_deform_a,
    w_expand_a,
    scale_a,
    shift_a,
    w_reduce_b,
    w_conv_b,
    w_expand_b,
    scale_b,
    shift_b,
    cotangent,
):
    images, tile_rows, tile_cols, channels = feature_in.shape
    inner_width = w_reduce_a.shape[1]
    second_cut = 2 * inner_width
    tile_pixels = tile_rows * tile_cols
    win_cols = tile_cols + HALF
    win_rows = tile_rows + 2 * PAD
    plane_count = 1.0 * images * LONG * SHORT
    pixel_count = plane_count * lax.axis_size("img")
    unbias = pixel_count / (pixel_count - 1.0)
    col_at = lax.axis_index("col")
    row_ids = lax.axis_index("row") * tile_rows + jnp.arange(tile_rows, dtype=jnp.int32)
    col_ids = col_at * tile_cols + jnp.arange(tile_cols, dtype=jnp.int32)
    landscape = jnp.broadcast_to((row_ids < SHORT)[:, None], (tile_rows, tile_cols))
    portrait = jnp.broadcast_to((col_ids < SHORT)[None, :], (tile_rows, tile_cols))
    inside = jnp.where(orientation[:, None, None] == 0, landscape[None], portrait[None]).astype(F32)
    weight_col = inside.reshape(-1, 1)
    pixels = weight_col.shape[0]
    own_count, all_counts = inside_counts(orientation, tile_rows, tile_cols)
    counts = (own_count, all_counts, plane_count)
    block_in = (
        (feature_in.astype(F32) * inside[..., None]).astype(BF16).reshape(pixels, channels)
    )
    reduced_a = jnp.dot(block_in, w_reduce_a, preferred_element_type=F32)
    normed_a1, unit_a1, inv_a1, mean_a1, spread_a1 = norm_forward(
        reduced_a, weight_col, scale_a[:inner_width], shift_a[:inner_width], counts
    )
    hidden_a = (gelu_exact(normed_a1) * weight_col).astype(BF16)
    rim_a = with_halo(
        hidden_a.reshape(images, tile_rows, tile_cols, inner_width), PAD, REACH, "halo_a"
    )
    rim_flat = rim_a.reshape(images, -1, inner_width)
    own_at = HALF * col_at
    w_off = w_offset_a.reshape(9, inner_width, 18).transpose(1, 0, 2).reshape(inner_width, 162)
    spread_taps = jnp.dot(
        rim_flat.reshape(-1, inner_width), w_off, preferred_element_type=F32
    ).reshape(images, win_rows, win_cols, 162)
    spread_taps = jnp.pad(spread_taps, ((0, 0), (0, 0), (2, 2), (0, 0)))
    spread_taps = lax.dynamic_slice_in_dim(spread_taps, own_at, tile_cols + 4, axis=2)
    offsets = 0.0
    for tap in range(9):
        i, j = 2 * (tap // 3), 2 * (tap % 3)
        offsets = offsets + spread_taps[
            :, PAD - 2 + i : PAD - 2 + i + tile_rows, j : j + tile_cols, 18 * tap : 18 * tap + 18
        ]
    fraction = jax.nn.sigmoid(offsets).reshape(images, tile_pixels, 18).transpose(0, 2, 1)
    frac_row, frac_col = fraction[:, 0::2], fraction[:, 1::2]
    base = offset_base.reshape(images, tile_pixels, 18).transpose(0, 2, 1)
    cell = np.arange(tile_pixels)
    tap_row = np.array([2 * (tap // 3 - 1) for tap in range(9)])[:, None]
    tap_col = np.array([2 * (tap % 3 - 1) for tap in range(9)])[:, None]
    upper = base[:, 0::2] + jnp.asarray(cell // tile_cols + PAD + tap_row, jnp.int32)
    left = base[:, 1::2] + jnp.asarray(cell % tile_cols + tap_col, jnp.int32) + own_at
    samples, deformed = sample_forward(
        rim_flat.transpose(0, 2, 1), w_deform_a.T, upper, left, frac_row, frac_col, win_cols
    )
    deformed = deformed.T
    normed_a2, unit_a2, inv_a2, mean_a2, spread_a2 = norm_forward(
        deformed,
        weight_col,
        scale_a[inner_width:second_cut],
        shift_a[inner_width:second_cut],
        counts,
    )
    hidden2_a = (gelu_exact(normed_a2) * weight_col).astype(BF16)
    expanded_a = jnp.dot(hidden2_a, w_expand_a, preferred_element_type=F32)
    normed_a3, unit_a3, inv_a3, mean_a3, spread_a3 = norm_forward(
        expanded_a, weight_col, scale_a[second_cut:], shift_a[second_cut:], counts
    )
    pre_a = normed_a3 + block_in.astype(F32)
    middle = (gelu_exact(pre_a) * weight_col).astype(BF16)
    reduced_b = jnp.dot(middle, w_reduce_b, preferred_element_type=F32)
    normed_b1, unit_b1, inv_b1, mean_b1, spread_b1 = norm_forward(
        reduced_b, weight_col, scale_b[:inner_width], shift_b[:inner_width], counts
    )
    hidden_b = (gelu_exact(normed_b1) * weight_col).astype(BF16)
    tile_shape = (images, tile_rows, tile_cols, inner_width)
    rim_b = with_halo(hidden_b.reshape(tile_shape), 2, 2, "halo_b")
    conv_out = conv_forward(rim_b, w_conv_b)
    normed_b2, unit_b2, inv_b2, mean_b2, spread_b2 = norm_forward(
        conv_out,
        weight_col,
        scale_b[inner_width:second_cut],
        shift_b[inner_width:second_cut],
        counts,
    )
    hidden2_b = (gelu_exact(normed_b2) * weight_col).astype(BF16)
    expanded_b = jnp.dot(hidden2_b, w_expand_b, preferred_element_type=F32)
    normed_b3, unit_b3, inv_b3, mean_b3, spread_b3 = norm_forward(
        expanded_b, weight_col, scale_b[second_cut:], shift_b[second_cut:], counts
    )
    pre_b = normed_b3 + middle.astype(F32)
    feature_out = (gelu_exact(pre_b) * weight_col).astype(BF16).reshape(feature_in.shape)
    upstream = cotangent.astype(F32).reshape(pixels, channels) * weight_col
    grad_pre_b = gelu_back(pre_b, upstream)
    grad_expand_out, gain_b3, bias_b3 = norm_backward(
        grad_pre_b, unit_b3, inv_b3, scale_b[second_cut:], weight_col, pixel_count
    )
    gw_expand_b = jnp.einsum("pm,pc->mc", hidden2_b, grad_expand_out, preferred_element_type=F32)
    grad_hidden2_b = jnp.einsum(
        "pc,mc->pm", grad_expand_out, w_expand_b, preferred_element_type=F32
    )
    grad_normed_b2 = gelu_back(normed_b2, grad_hidden2_b * weight_col)
    grad_conv_out, gain_b2, bias_b2 = norm_backward(
        grad_normed_b2, unit_b2, inv_b2, scale_b[inner_width:second_cut], weight_col, pixel_count
    )
    back_rim = with_halo(grad_conv_out.reshape(tile_shape), 2, 2, "halo_b")
    grad_hidden_b, gw_conv_b = conv_backward(rim_b, back_rim, w_conv_b, grad_conv_out)
    grad_normed_b1 = gelu_back(normed_b1, grad_hidden_b * weight_col)
    grad_reduce_out, gain_b1, bias_b1 = norm_backward(
        grad_normed_b1, unit_b1, inv_b1, scale_b[:inner_width], weight_col, pixel_count
    )
    gw_reduce_b = jnp.einsum("pc,pm->cm", middle, grad_reduce_out, preferred_element_type=F32)
    grad_middle = grad_pre_b + jnp.einsum(
        "pm,cm->pc", grad_reduce_out, w_reduce_b, preferred_element_type=F32
    )
    grad_pre_a = gelu_back(pre_a, grad_middle * weight_col)
    grad_expand_a, gain_a3, bias_a3 = norm_backward(
        grad_pre_a, unit_a3, inv_a3, scale_a[second_cut:], weight_col, pixel_count
    )
    gw_expand_a = jnp.einsum("pm,pc->mc", hidden2_a, grad_expand_a, preferred_element_type=F32)
    grad_hidden2_a = jnp.einsum("pc,mc->pm", grad_expand_a, w_expand_a, preferred_element_type=F32)
    grad_normed_a2 = gelu_back(normed_a2, grad_hidden2_a * weight_col)
    grad_deformed, gain_a2, bias_a2 = norm_backward(
        grad_normed_a2, unit_a2, inv_a2, scale_a[inner_width:second_cut], weight_col, pixel_count
    )
    gw_deform_a = jnp.dot(samples, grad_deformed, preferred_element_type=F32)
    spill, grad_row, grad_col = sample_backward(
        rim_flat, grad_deformed.T, w_deform_a, upper, left, frac_row, frac_col, win_cols
    )
    grad_fraction = jnp.stack([grad_row, grad_col], axis=2).reshape(images, 18, tile_pixels)
    grad_offsets = (grad_fraction * fraction * (1.0 - fraction)).astype(BF16)
    grad_offsets = grad_offsets.transpose(0, 2, 1).reshape(images, tile_rows, tile_cols, 18)
    placed = jnp.zeros((images, tile_rows, win_cols + 4, 18), BF16)
    placed = lax.dynamic_update_slice(placed, grad_offsets, (0, 0, own_at + 2, 0))
    on_cells = []
    for tap in range(9):
        i, j = 2 * (tap // 3 - 1), 2 * (tap % 3 - 1)
        moved = placed[:, :, 2 - j : 2 - j + win_cols]
        on_cells.append(jnp.pad(moved, ((0, 0), (PAD + i, PAD - i), (0, 0), (0, 0))))
    on_cells = jnp.concatenate(on_cells, axis=-1).reshape(-1, 162)
    gw_offset_a = jnp.einsum(
        "qm,qo->mo", rim_flat.reshape(-1, inner_width), on_cells, preferred_element_type=F32
    )
    gw_offset_a = gw_offset_a.reshape(inner_width, 9, 18).transpose(1, 0, 2).reshape(-1, 18)
    spill = spill.reshape(-1, inner_width) + jnp.einsum(
        "qo,mo->qm", on_cells, w_off, preferred_element_type=F32
    )
    grad_hidden_a = spill_home(spill.reshape(rim_a.shape)).reshape(pixels, inner_width)
    grad_normed_a1 = gelu_back(normed_a1, grad_hidden_a * weight_col)
    grad_reduce_a, gain_a1, bias_a1 = norm_backward(
        grad_normed_a1, unit_a1, inv_a1, scale_a[:inner_width], weight_col, pixel_count
    )
    gw_reduce_a = jnp.einsum("pc,pm->cm", block_in, grad_reduce_a, preferred_element_type=F32)
    grad_block_in = grad_pre_a + jnp.einsum(
        "pm,cm->pc", grad_reduce_a, w_reduce_a, preferred_element_type=F32
    )
    grad_in = (grad_block_in * weight_col).astype(BF16).reshape(feature_in.shape)

    def over_devices(grad, dim):
        part = lax.psum_scatter(grad.astype(BF16), "img", scatter_dimension=dim, tiled=True)
        return lax.psum(part, ("row", "col"))

    gw_expand_b = over_devices(gw_expand_b, 0).astype(F32)
    gw_conv_b = over_devices(gw_conv_b, 1).T.astype(F32)
    gw_reduce_b = over_devices(gw_reduce_b, 0).astype(F32)
    gw_expand_a = over_devices(gw_expand_a, 0).astype(F32)
    gw_deform_a = over_devices(gw_deform_a, 0).astype(F32)
    gw_offset_a = over_devices(gw_offset_a, 0).astype(F32)
    gw_reduce_a = over_devices(gw_reduce_a, 0).astype(F32)
    return (
        feature_out,
        grad_in,
        gw_reduce_a,
        gw_offset_a,
        gw_deform_a,
        gw_expand_a,
        jnp.concatenate([gain_a1, gain_a2, gain_a3]),
        jnp.concatenate([bias_a1, bias_a2, bias_a3]),
        jnp.concatenate([mean_a1, mean_a2, mean_a3]),
        jnp.concatenate([spread_a1, spread_a2, spread_a3]) * unbias,
        gw_reduce_b,
        gw_conv_b,
        gw_expand_b,
        jnp.concatenate([gain_b1, gain_b2, gain_b3]),
        jnp.concatenate([bias_b1, bias_b2, bias_b3]),
        jnp.concatenate([mean_b1, mean_b2, mean_b3]),
        jnp.concatenate([spread_b1, spread_b2, spread_b3]) * unbias,
    )


def solution(mesh):
    tiles = P("img", "row", "col", None)
    in_specs = (tiles, P("img"), tiles) + (P(),) * 11 + (tiles,)
    shares = P("img", None)
    out_specs = (tiles, tiles) + (shares,) * 4 + (P(),) * 4 + (shares,) * 3 + (P(),) * 4
    return jax.shard_map(body, mesh=mesh, in_specs=in_specs, out_specs=out_specs, check_vma=False)
```

time: 2430 us -> 998 us (0.41)
  blocking collectives: 759 us -> 25.9 us
  other arithmetic: 646 us -> 166 us
  local copies, waits for them, and re-layouts: 387 us -> 83.6 us
  Pallas kernels: 0 us -> 289 us
  matrix products: 264 us -> 106 us
  starting transfers between devices: 42.6 us -> 0.33 us
    psum x19 -> x1, blocking collectives: 759 us -> 25.9 us  [over_devices(): return lax.psum(part, ('row', 'col'))]
    reduce_sum x42 -> x9, other arithmetic: 450 us -> 7.93 us  [the longest x6 3.94 us: local_stats(): return (total, jnp.sum(away * away * weight_col, axis=0))]
    pallas_call x0 -> x20, Pallas kernels: none -> 289 us  [the longest x12 152 us: exchange(): pl.pallas_call(kernel, out_shape=jax.ShapeDtypeStruct((rows, 128), F32),...]
    dot_general x69 -> x10, matrix products: 221 us -> 52.9 us  [the longest x1 11.6 us: body(): gw_deform_a = jnp.dot(samples, grad_deformed, preferred_element_type=F32)]
    scatter-add x9 -> x0, local copies, waits for them, and re-layouts: 98.1 us -> none  [body(): spill = spill.at[:, step_row:step_row + tile_rows, step_col:step_col + ti...]
    another operation x14 -> x1, local copies, waits for them, and re-layouts: 67.1 us -> 0.06 us  [body(): jnp.stack([grad_row, grad_col], axis=2).reshape(images, 18, tile_pixels)]
    slice x14 -> x6, local copies, waits for them, and re-layouts: 61.4 us -> 3.06 us  [the longest x2 1.3 us: body(): frac_row, frac_col = (fraction[:, 0::2], fraction[:, 1::2])]
    reduce_scatter x6 -> x5, waiting for transfers between devices: 177 us -> 223 us  [over_devices(): lax.psum_scatter(grad.astype(BF16), 'img', scatter_dimension=dim, tiled=T...]
  transfers between devices with their start and end apart: 24 -> 8, of which waited for: 13 -> 6; matrix products, arithmetic and copies ran while one was open for 32% -> 15% of each run, Pallas kernels for 0% -> 11%
where the time goes in v1:
time: 998 us; the launch traced here: 989 us
  waiting for transfers between devices  302 us (30%)
  Pallas kernels  289 us (29%)
  other arithmetic  166 us (17%)
  matrix products  106 us (11%)
  local copies, waits for them, and re-layouts  83.6 us (8%)
  blocking collectives  25.9 us (3%)
  between operations  16.1 us (2%)
    reduce_scatter x5, waiting for transfers between devices, over_devices(): lax.psum_scatter(grad.astype(BF16), 'img', scatter_dimension=dim, tiled=T...  223 us
    pallas_call x12, Pallas kernels, exchange(): pl.pallas_call(kernel, out_shape=jax.ShapeDtypeStruct((rows, 128), F32),...  152 us
    psum x1, waiting for transfers between devices, over_devices(): return lax.psum(part, ('row', 'col'))  60.6 us
    pallas_call x3, Pallas kernels, with_halo(): pl.pallas_call(functools.partial(halo_kernel, pad, reach), out_shape=jax....  38.9 us
    reduce_sum x3, other arithmetic, norm_backward(): jnp.sum(grad_normed, axis=0)  35.5 us
    convert_element_type x4, other arithmetic, norm_backward(): return (grad_pre.astype(BF16), sum_unit, sum_grad)  34.4 us
    pallas_call x1, Pallas kernels, sample_backward(): pl.pallas_call(unsample_kernel, grid=(images, blocks), out_shape=(jax.Sha...  31.4 us
    unnamed x144, local copies, waits for them, and re-layouts  30 us
  transfers between devices with their start and end apart: 8, of which 6 were waited for; matrix products, arithmetic and copies ran while one was open for 15% of the time, Pallas kernels for 11%

profile of v1, /device:TPU:0, one launch (start us, length us, event | category | flops | bytes accessed | tf_op | source)
XLA Modules:
  0.0 988.9 jit_solution(17595357338493989999)
XLA Ops:
  24.2 12.7 %stats512.4 = f32[8,128]{1,0:T(8,128)} custom-call(f32[8,128]{1,0:T(8,128)} %pad_maximum_fusion.11.x_ref, f32[8,128]{1,0:T(8,128)} %broadcast_in_dim.31.count_ref), custom_call_target="tpu_custom_call" | custom-call | tf_op jit(solution)/shard_map/stats512/pallas_call | solution.py:141
  49.3 18.5 %halo_a.1 = bf16[2,32,48,512]{3,2,1,0:T(8,128)(2,1)} custom-call(bf16[2,16,32,512]{3,2,1,0:T(8,128)(2,1)} %bitcast.239), custom_call_target="tpu_custom_call" | custom-call | tf_op jit(solution)/shard_map/halo_a/pallas_call | solution.py:275
  86.7 21.3 %sample.1 = (bf16[4608,1024]{1,0:T(8,128)(2,1)}, f32[512,1024]{1,0:T(8,128)}) custom-call(bf16[2,512,1536]{2,1,0:T(8,128)(2,1)} %copy.170.rim_ref, bf16[512,4608]{1,0:T(8,128)(2,1)} %bitcast.227, s32[2,9,512]{2,1,0:T(8,128)} %broadcast_add_fusion.up_ref, s32[2,9,512]{2,1,0:T(8,128)} %add_add_fusion.left_ref, f32[2,9,512]{2,1,0:T(8,128)} %slice.207.fr_ref, ...), custom_call_target="tpu_custom_call" | custom-call | tf_op jit(solution)/shard_map/sample/pallas_call | solution.py:455
  111.2 18.2 %stats512.5 = f32[8,128]{1,0:T(8,128)} custom-call(f32[8,128]{1,0:T(8,128)} %pad_maximum_fusion.12.x_ref, f32[8,128]{1,0:T(8,128)} %broadcast_in_dim.31.count_ref), custom_call_target="tpu_custom_call" | custom-call | tf_op jit(solution)/shard_map/stats512/pallas_call | solution.py:141
  158.7 23.4 %multiply_convert_fusion.4 = (bf16[1024,2048]{1,0:T(8,128)(2,1)S(1)}, f32[1024,2048]{1,0:T(8,128)}, f32[1024,2048]{1,0:T(8,128)}) fusion(f32[1024]{0:T(1024)S(1)} %reshape.341, bf16[2,16,32,2048]{3,2,1,0:T(8,128)(2,1)} %multiply_convert_fusion.5, f32[2048]{0:T(1024)S(1)} %slice-done, f32[2048]{0:T(1024)S(1)} %get-tuple-element.179, ...), kind=kLoop, calls=%fused_computation.36 | loop fusion | flops 150994944 | bytes 33591296 | tf_op jit(solution)/shard_map/convert_element_type | solution.py:793
  235.1 11.4 %stats512.7 = f32[8,128]{1,0:T(8,128)} custom-call(f32[8,128]{1,0:T(8,128)} %pad_maximum_fusion.14.x_ref, f32[8,128]{1,0:T(8,128)} %broadcast_in_dim.31.count_ref), custom_call_target="tpu_custom_call" | custom-call | tf_op jit(solution)/shard_map/stats512/pallas_call | solution.py:141
  275.5 26.2 %fusion.98 = (f32[2048]{0:T(1024)S(1)}, f32[2048]{0:T(1024)S(1)}, f32[1024,2048]{1,0:T(8,128)}, f32[1024,2048]{1,0:T(8,128)}) fusion(f32[2048]{0:T(1024)S(1)} %get-tuple-element.173, f32[1024,2048]{1,0:T(8,128)} %copy-done.2, f32[2048]{0:T(1024)S(1)} %get-tuple-element.165, f32[1024]{0:T(1024)S(1)} %reshape.341, bf16[2,16,32,2048]{3,2,1,0:T(8,128)(2,1)} %param.33, ...), kind=kLoop, calls=%fused_computation.300 | loop fusion | flops 171962368 | bytes 33607680 | tf_op jit(solution)/shard_map/reduce_sum | solution.py:683
  313.5 14.5 %multiply_convert_fusion.2 = (bf16[1024,2048]{1,0:T(8,128)(2,1)S(1)}, bf16[1024,2048]{1,0:T(8,128)(2,1)}) fusion(f32[1024,2048]{1,0:T(8,128)} %get-tuple-element.137, f32[1024,2048]{1,0:T(8,128)} %copy-done.2, f32[2048]{0:T(1024)S(1)} %get-tuple-element.175, f32[2048]{0:T(1024)S(1)} %get-tuple-element.174, f32[2048]{0:T(1024)S(1)} %get-tuple-element.172, ...), kind=kLoop, calls=%fused_computation.17 | loop fusion | flops 35651584 | bytes 37810176 | tf_op jit(solution)/shard_map/convert_element_type | solution.py:691
  359.2 16.4 %unconv.1 = (f32[1024,512]{1,0:T(8,128)}, bf16[512,4608]{1,0:T(8,128)(2,1)}) custom-call(bf16[2,20,48,512]{3,2,1,0:T(8,128)(2,1)} %halo_b.2.rim_ref, bf16[2,20,48,512]{3,2,1,0:T(8,128)(2,1)} %halo_b.3.back_ref, bf16[4608,512]{1,0:T(8,128)(2,1)} %w_ref.4, bf16[1024,512]{1,0:T(8,128)(2,1)} %copy.179.g_ref), custom_call_target="tpu_custom_call" | custom-call | tf_op jit(solution)/shard_map/unconv/pallas_call | solution.py:652
  391.0 12.6 %sums512.5 = f32[8,128]{1,0:T(8,128)} custom-call(f32[8,128]{1,0:T(8,128)} %pad_maximum_fusion.16.x_ref), custom_call_target="tpu_custom_call" | custom-call | tf_op jit(solution)/shard_map/sums512/pallas_call | solution.py:141
  404.3 20.5 %fusion.97 = (f32[2048]{0:T(1024)S(1)}, f32[2048]{0:T(1024)S(1)}, f32[1024,2048]{1,0:T(8,128)}) fusion(f32[2048]{0:T(1024)S(1)} %get-tuple-element.169, f32[1024,2048]{1,0:T(8,128)} %copy-done.1, f32[2048]{0:T(1024)S(1)} %get-tuple-element.167, f32[1024,2048]{1,0:T(8,128)} %get-tuple-element.144, f32[1024,2048]{1,0:T(8,128)} %get-tuple-element.145, ...), kind=kOutput, calls=%fused_computation.299 | convolution fusion | flops 2194141184 | bytes 48281600 | tf_op jit(solution)/shard_map/pm,cm->pc/dot_general | solution.py:836
  425.5 12.3 %sums2048.3 = f32[32,128]{1,0:T(8,128)} custom-call(f32[32,128]{1,0:T(8,128)} %pad_maximum_fusion.4.x_ref), custom_call_target="tpu_custom_call" | custom-call | tf_op jit(solution)/shard_map/sums2048/pallas_call | solution.py:141
  451.9 11.3 %sums512.6 = f32[8,128]{1,0:T(8,128)} custom-call(f32[8,128]{1,0:T(8,128)} %pad_maximum_fusion.17.x_ref), custom_call_target="tpu_custom_call" | custom-call | tf_op jit(solution)/shard_map/sums512/pallas_call | solution.py:141
  472.7 31.4 %unsample.1 = (f32[2,1536,512]{2,1,0:T(8,128)}, f32[2,9,512]{2,1,0:T(8,128)}, f32[2,9,512]{2,1,0:T(8,128)}) custom-call(bf16[2,1536,512]{2,1,0:T(8,128)(2,1)} %bitcast.223, bf16[512,1024]{1,0:T(8,128)(2,1)} %fusion.31.g_ref, bf16[4608,512]{1,0:T(8,128)(2,1)} %w_ref.5, s32[2,9,512]{2,1,0:T(8,128)} %broadcast_add_fusion.up_ref, ...), custom_call_target="tpu_custom_call" | custom-call | tf_op jit(solution)/shard_map/unsample/pallas_call | solution.py:528
  526.2 19.4 %spill.1 = f32[2,16,32,512]{3,2,1,0:T(8,128)} custom-call(f32[2,32,48,512]{3,2,1,0:T(8,128)} %bitcast.225), custom_call_target="tpu_custom_call" | custom-call | tf_op jit(solution)/shard_map/spill/pallas_call | solution.py:372
  554.0 21.7 %sums512.7 = f32[8,128]{1,0:T(8,128)} custom-call(f32[8,128]{1,0:T(8,128)} %pad_maximum_fusion.18.x_ref), custom_call_target="tpu_custom_call" | custom-call | tf_op jit(solution)/shard_map/sums512/pallas_call | solution.py:141
  606.4 11.6 %convolution_convert_fusion = bf16[4608,512]{1,0:T(8,128)(2,1)} fusion(bf16[4608,1024]{1,0:T(8,128)(2,1)} %get-tuple-element.29, f32[1024,512]{0,1:T(8,128)} %get-tuple-element.135, f32[512]{0:T(512)S(1)} %get-tuple-element.201, f32[512]{0:T(512)S(1)} %get-tuple-element.200, f32[512]{0:T(512)S(1)} %copy-done.58, f32[1024]{0:T(1024)S(1)} %reshape.341, ...), kind=kOutput, calls=%fused_computation.56 | convolution fusion | flops 4838916096 | bytes 18364416 | tf_op jit(solution)/shard_map/dot_general | solution.py:849
  628.2 45.5 %reduce-scatter.16.cloned.1.call-done = bf16[128,2048]{1,0:T(8,128)(2,1)} async-done(((bf16[512,2048]{1,0:T(8,128)(2,1)}), bf16[128,2048]{1,0:T(8,128)(2,1)}) %reduce-scatter.16.cloned.1.call-update) | async-done | bytes 524304 | tf_op jit(solution)/shard_map/reduce_scatter | solution.py:883
  673.6 45.4 %reduce-scatter.18.cloned.1.call-done = bf16[512,512]{1,0:T(8,128)(2,1)} async-done(((bf16[2048,512]{1,0:T(8,128)(2,1)}), bf16[512,512]{1,0:T(8,128)(2,1)}) %reduce-scatter.18.cloned.1.call-update) | async-done | bytes 524304 | tf_op jit(solution)/shard_map/reduce_scatter | solution.py:883
  719.0 45.4 %reduce-scatter.20.cloned.1.call-done = bf16[128,2048]{1,0:T(8,128)(2,1)} async-done(((bf16[512,2048]{1,0:T(8,128)(2,1)}), bf16[128,2048]{1,0:T(8,128)(2,1)}) %reduce-scatter.20.cloned.1.call-update) | async-done | bytes 524304 | tf_op jit(solution)/shard_map/reduce_scatter | solution.py:883
  764.5 86.8 %reduce-scatter.14.cloned.1.call-done = bf16[1152,512]{1,0:T(8,128)(2,1)} async-done(((bf16[4608,512]{1,0:T(8,128)(2,1)}), bf16[1152,512]{1,0:T(8,128)(2,1)}) %reduce-scatter.14.cloned.1.call-update) | async-done | bytes 1179664 | tf_op jit(solution)/shard_map/reduce_scatter | solution.py:883
  865.4 17.9 %reduce-scatter.22.cloned.1.call-done = bf16[1152,18]{1,0:T(8,128)(2,1)} async-done(((bf16[4608,18]{1,0:T(8,128)(2,1)}), bf16[1152,18]{1,0:T(8,128)(2,1)}) %reduce-scatter.22.cloned.1.call-update) | async-done | bytes 41488
  884.4 25.9 %psum.50 = bf16[1152,18]{0,1:T(8,128)(2,1)S(1)} all-reduce(bf16[1152,18]{0,1:T(8,128)(2,1)S(1)} %copy.202), channel_id=1, replica_groups=mesh['img'=4,'row'=4,'col'=2] {'row','col'}, use_global_device_ids=true, to_apply=%region_28.29 | all-reduce | flops 20736 | bytes 82944 | tf_op jit(solution)/shard_map/psum | solution.py:884
  911.0 60.6 %all-reduce.13.cloned.1.call-done = (bf16[1152,512]{0,1:T(8,128)(2,1)}, bf16[512,512]{1,0:T(8,128)(2,1)}, bf16[1152,512]{1,0:T(8,128)(2,1)}, bf16[128,2048]{1,0:...) async-done(((bf16[1152,512]{0,1:T(8,128)(2,1)}, bf16[512,512]{1,0:T(8,128)(2,1)}, bf16[1152,512]{1,0:T(8,128)(2,1)}, bf16[128,2048]{1,0:T(8,128)(2,1)}, ...) | async-done | bytes 4456464 | tf_op jit(solution)/shard_map/psum | solution.py:884
  (297 shorter events, 342.1 us)
Async XLA Ops:
  7.2 132.4 %copy-start = (bf16[512,2048]{1,0:T(8,128)(2,1)S(1)}, bf16[512,2048]{1,0:T(8,128)(2,1)}, u32[]{:S(2)}) copy-start(bf16[512,2048]{1,0:T(8,128)(2,1)} %param.25) | copy-start | bytes 6291460
  7.2 618.5 %reduce-scatter.24.cloned.1.call-start = ((), (), s32[]{:S(2)}) async-start(), calls=%async_computation.13 | async-start | bytes 5898240
  8.1 32.3 %copy-start.47 = (f32[512]{0:T(512)}, f32[512]{0:T(512)S(1)}, u32[]{:S(2)}) copy-start(f32[512]{0:T(512)S(1)} %get-tuple-element.186) | copy-start | bytes 6148
  8.1 123.9 %copy-start.30 = (f32[512]{0:T(512)}, f32[512]{0:T(512)S(1)}, u32[]{:S(2)}) copy-start(f32[512]{0:T(512)S(1)} %get-tuple-element.187) | copy-start | bytes 6148
  21.2 17.7 %copy-start.22 = (s32[2,16,32,18]{2,1,3,0:T(8,128)S(1)}, s32[2,16,32,18]{2,1,3,0:T(8,128)}, u32[]{:S(2)}) copy-start(s32[2,16,32,18]{2,1,3,0:T(8,128)} %param.21) | copy-start | bytes 221188
  49.3 18.5 %copy-start.24 = (bf16[4608,18]{0,1:T(8,128)(2,1)S(1)}, bf16[4608,18]{0,1:T(8,128)(2,1)}, u32[]{:S(2)}) copy-start(bf16[4608,18]{0,1:T(8,128)(2,1)} %param.23) | copy-start | bytes 497668
  108.0 21.4 %copy-start.25 = (f32[8,128]{1,0:T(8,128)S(1)}, f32[8,128]{1,0:T(8,128)}, u32[]{:S(2)}) copy-start(f32[8,128]{1,0:T(8,128)} %stats512.4) | copy-start | bytes 12292
  108.0 21.4 %copy-start.51 = (f32[3072]{0:T(1024)S(1)}, f32[3072]{0:T(1024)}, u32[]{:S(2)}) copy-start(f32[3072]{0:T(1024)} %param.26) | copy-start | bytes 36868
  142.1 16.5 %slice-start = ((f32[3072]{0:T(1024)}), f32[2048]{0:T(1024)S(1)}, s32[]{:S(2)}) async-start(f32[3072]{0:T(1024)} %param.27), calls=%async_computation.15 | async-start | bytes 16384 | tf_op jit(solution)/shard_map/slice | solution.py:790
  158.7 23.4 %copy-start.68 = (bf16[2048,512]{1,0:T(8,128)(2,1)S(1)}, bf16[2048,512]{1,0:T(8,128)(2,1)}, u32[]{:S(2)}) copy-start(bf16[2048,512]{1,0:T(8,128)(2,1)} %param.28) | copy-start | bytes 6291460
  184.6 15.2 %copy-start.52 = (f32[3072]{0:T(1024)S(1)}, f32[3072]{0:T(1024)}, u32[]{:S(2)}) copy-start(f32[3072]{0:T(1024)} %param.31) | copy-start | bytes 36868
  199.8 49.4 %copy-start.55 = (f32[512]{0:T(512)}, f32[512]{0:T(512)S(1)}, u32[]{:S(2)}) copy-start(f32[512]{0:T(512)S(1)} %get-tuple-element.184) | copy-start | bytes 6148
  247.8 80.2 %copy-start.36 = (f32[512]{0:T(512)}, f32[512]{0:T(512)S(1)}, u32[]{:S(2)}) copy-start(f32[512]{0:T(512)S(1)} %get-tuple-element.188) | copy-start | bytes 6148
  259.4 16.0 %copy-start.54 = (f32[3072]{0:T(1024)S(1)}, f32[3072]{0:T(1024)}, u32[]{:S(2)}) copy-start(f32[3072]{0:T(1024)} %param.32) | copy-start | bytes 36868
  382.3 245.9 %reduce-scatter.12.cloned.1.call-start = ((), (), s32[]{:S(2)}) async-start(), calls=%async_computation.7 | async-start | bytes 2621440 | tf_op jit(solution)/shard_map/reduce_scatter | solution.py:883
  385.7 18.6 %copy-start.63 = (f32[512]{0:T(512)S(1)}, f32[512]{0:T(512)}, u32[]{:S(2)}) copy-start(f32[512]{0:T(512)} %get-tuple-element.180) | copy-start | bytes 6148
  446.2 17.8 %copy-start.58 = (f32[512]{0:T(512)S(1)}, f32[512]{0:T(512)}, u32[]{:S(2)}) copy-start(f32[512]{0:T(512)} %get-tuple-element.177) | copy-start | bytes 6148
  548.8 27.7 %copy-start.57 = (f32[512]{0:T(512)S(1)}, f32[512]{0:T(512)}, u32[]{:S(2)}) copy-start(f32[512]{0:T(512)} %get-tuple-element.176) | copy-start | bytes 6148
  584.3 89.3 %reduce-scatter.16.cloned.1.call-start = ((), (), s32[]{:S(2)}) async-start(), calls=%async_computation.9 | async-start | bytes 2621440 | tf_op jit(solution)/shard_map/reduce_scatter | solution.py:883
  591.4 127.6 %reduce-scatter.18.cloned.1.call-start = ((), (), s32[]{:S(2)}) async-start(), calls=%async_computation.10 | async-start | bytes 2621440 | tf_op jit(solution)/shard_map/reduce_scatter | solution.py:883
  599.2 165.2 %reduce-scatter.20.cloned.1.call-start = ((), (), s32[]{:S(2)}) async-start(), calls=%async_computation.11 | async-start | bytes 2621440 | tf_op jit(solution)/shard_map/reduce_scatter | solution.py:883
  606.3 244.9 %reduce-scatter.14.cloned.1.call-start = ((), (), s32[]{:S(2)}) async-start(), calls=%async_computation.8 | async-start | bytes 5898240 | tf_op jit(solution)/shard_map/reduce_scatter | solution.py:883
  618.0 265.4 %reduce-scatter.22.cloned.1.call-start = ((), (), s32[]{:S(2)}) async-start(), calls=%async_computation.12 | async-start | bytes 1474560
  625.7 346.0 %all-reduce.13.cloned.1.call-start = ((), (), s32[]{:S(2)}) async-start(), calls=%async_computation.14 | async-start | bytes 8912896 | tf_op jit(solution)/shard_map/psum | solution.py:884
  (54 other events, 293.5 us)
Sparse Core Ops, SparseCore 0:
  382.4 87.5 reduce-scatter.23
  584.4 42.8 reduce-scatter.11
  630.4 43.2 reduce-scatter.15
  675.8 43.1 reduce-scatter.17
  721.3 43.1 reduce-scatter.19
  766.6 84.5 reduce-scatter.13
  853.6 29.6 reduce-scatter.21
  887.3 84.2 all-reduce.12

commit v2 on v1

--- a/solution.py
+++ b/solution.py
@@ -20,7 +20,7 @@
 REACH = BOUND + 3
 PAD = 8
 HALF = 16
-CID = {"stats512": 0, "sums512": 1, "stats2048": 2, "sums2048": 3, "halo_a": 4, "halo_b": 5, "spill": 6}
+CID = {"stats512": 0, "sums512": 1, "stats2048": 2, "sums2048": 3, "halo_a": 4, "halo_b": 5, "spill": 6, "reduce": 7}
 
 
 def gelu_exact(values):
@@ -661,6 +661,169 @@
         compiler_params=pltpu.CompilerParams(vmem_limit_bytes=VMEM_LIMIT),
         name="unconv",
     )(rim, back_rim, w, grad)
+
+
+class Reduction:
+    count = 7
+
+    def __init__(self, index, src, out, bufs, send_sems, recv_sems):
+        self.src, self.out, self.bufs = src, out, bufs
+        self.send, self.recv = send_sems.at[index], recv_sems.at[index]
+        self.order = (0, 1) if index % 2 == 0 else (1, 0)
+        self.img, self.row, self.col = (lax.axis_index(a) for a in ("img", "row", "col"))
+        self.images = src.shape[0]
+        self.bits = (lax.rem(self.row, 2), self.row // 2)
+
+    @staticmethod
+    def scratch(shape):
+        images, _, rows, width = shape
+        return [
+            pltpu.VMEM((images, 4, rows, width), BF16),
+            pltpu.VMEM((images, 2, rows, width), BF16),
+            pltpu.VMEM((images, rows, width), BF16),
+            pltpu.VMEM((images, rows, width), BF16),
+        ]
+
+    def copy(self, src, dst, k, device):
+        return pltpu.make_async_remote_copy(
+            src_ref=src,
+            dst_ref=dst,
+            send_sem=self.send.at[k],
+            recv_sem=self.recv.at[k],
+            device_id=device,
+            device_id_type=MESH,
+        )
+
+    def neighbour(self, bit):
+        here = self.bits[bit]
+        return {"row": self.row + (1 - 2 * here) * (1 + bit)}
+
+    def wait(self, ref, k):
+        pltpu.make_async_copy(ref, ref, self.recv.at[k]).wait()
+
+    def wait_sent(self, ref, k):
+        pltpu.make_async_copy(ref, ref, self.send.at[k]).wait()
+
+    def step(self, k):
+        images, (half, quarter, eighth, line) = self.images, self.bufs
+        mine = 4 * self.col
+        first, second = self.order
+        a, b = self.bits[first], self.bits[second]
+        if k == 0:
+            other = pl.ds(4 * (1 - self.col), 4)
+            self.copy(self.src.at[:, other], half, 0, {"col": 1 - self.col}).start()
+        elif k == 1:
+            self.wait(half, 0)
+
+            def add(i, carry):
+                for s in range(4):
+                    own = self.src[i, mine + s].astype(F32)
+                    half[i, s] = (own + half[i, s].astype(F32)).astype(BF16)
+                return carry
+
+            lax.fori_loop(0, images, add, 0)
+            for i in range(2):
+                spot = self.piece(1 - a, i)
+                self.copy(half.at[:, spot], quarter.at[:, i], 1, self.neighbour(first)).start()
+        elif k == 2:
+            self.wait(quarter, 1)
+
+            def add(i, carry):
+                for s in range(2):
+                    own = half[i, self.piece(a, s)].astype(F32)
+                    quarter[i, s] = (own + quarter[i, s].astype(F32)).astype(BF16)
+                return carry
+
+            lax.fori_loop(0, images, add, 0)
+            self.copy(quarter.at[:, 1 - b], eighth, 2, self.neighbour(second)).start()
+        elif k == 3:
+            self.wait(eighth, 2)
+
+            def add(i, carry):
+                own = quarter[i, b].astype(F32)
+                eighth[i] = (own + eighth[i].astype(F32)).astype(BF16)
+                return carry
+
+            lax.fori_loop(0, images, add, 0)
+            for j in range(1, images):
+                there = lax.rem(self.img + j, images)
+                self.copy(eighth.at[there], line.at[j], 3, {"img": there}).start()
+        elif k == 4:
+            arrived = line.at[pl.ds(1, images - 1)]
+            self.wait(arrived, 3)
+            total = eighth[self.img].astype(F32)
+            for j in range(1, images):
+                total = total + line[j].astype(F32)
+            self.out[mine + self.row] = total.astype(BF16)
+            for j in range(1, 4):
+                there = lax.rem(self.row + j, 4)
+                spot = self.out.at[mine + self.row]
+                self.copy(spot, spot, 4, {"row": there}).start()
+        elif k == 5:
+            three = self.out.at[pl.ds(0, 3)]
+            self.wait(three, 4)
+            four = self.out.at[pl.ds(mine, 4)]
+            self.copy(four, four, 5, {"col": 1 - self.col}).start()
+        elif k == 6:
+            four = self.out.at[pl.ds(0, 4)]
+            self.wait(four, 5)
+            self.wait_sent(half, 0)
+            self.wait_sent(quarter, 1)
+            self.wait_sent(eighth, 2)
+            self.wait_sent(line.at[pl.ds(1, images - 1)], 3)
+            self.wait_sent(self.out.at[pl.ds(0, 3)], 4)
+            self.wait_sent(four, 5)
+
+    def piece(self, bit_value, free):
+        if self.order[0] == 0:
+            return bit_value + 2 * free
+        return 2 * bit_value + free
+
+
+def reduction_peers():
+    row, col, img = lax.axis_index("row"), lax.axis_index("col"), lax.axis_index("img")
+    images = lax.axis_size("img")
+    peers = [{"col": 1 - col}]
+    peers += [{"row": lax.rem(row + j, 4)} for j in range(1, 4)]
+    peers += [{"img": lax.rem(img + j, images)} for j in range(1, images)]
+    return peers
+
+
+def reduce_kernel(count, *refs):
+    srcs, outs, rest = refs[:count], refs[count : 2 * count], refs[2 * count :]
+    send_sems, recv_sems = rest[4 * count :]
+    barrier = pltpu.get_barrier_semaphore()
+    peers = reduction_peers()
+    for peer in peers:
+        pl.semaphore_signal(barrier, inc=1, device_id=peer, device_id_type=MESH)
+    pl.semaphore_wait(barrier, len(peers))
+    parts = [
+        Reduction(t, srcs[t], outs[t], rest[4 * t : 4 * t + 4], send_sems, recv_sems)
+        for t in range(count)
+    ]
+    for now in range(Reduction.count + count - 1):
+        for t in range(count):
+            if 0 <= now - t < Reduction.count:
+                parts[t].step(now - t)
+
+
+def reduce_all(grads):
+    count = len(grads)
+    scratch = []
+    for grad in grads:
+        scratch += Reduction.scratch(grad.shape)
+    scratch += [pltpu.SemaphoreType.DMA((count, 6)), pltpu.SemaphoreType.DMA((count, 6))]
+    return pl.pallas_call(
+        functools.partial(reduce_kernel, count),
+        out_shape=[jax.ShapeDtypeStruct(g.shape[1:], BF16) for g in grads],
+        in_specs=[VMEM] * count,
+        out_specs=[VMEM] * count,
+        scratch_shapes=scratch,
+        compiler_params=pltpu.CompilerParams(
+            collective_id=CID["reduce"], has_side_effects=True, vmem_limit_bytes=VMEM_LIMIT
+        ),
+        name="reduce",
+    )(*grads)
 
 
 def local_stats(values, weight_col, count):
@@ -879,17 +1042,34 @@
     )
     grad_in = (grad_block_in * weight_col).astype(BF16).reshape(feature_in.shape)
 
-    def over_devices(grad, dim):
-        part = lax.psum_scatter(grad.astype(BF16), "img", scatter_dimension=dim, tiled=True)
-        return lax.psum(part, ("row", "col"))
-
-    gw_expand_b = over_devices(gw_expand_b, 0).astype(F32)
-    gw_conv_b = over_devices(gw_conv_b, 1).T.astype(F32)
-    gw_reduce_b = over_devices(gw_reduce_b, 0).astype(F32)
-    gw_expand_a = over_devices(gw_expand_a, 0).astype(F32)
-    gw_deform_a = over_devices(gw_deform_a, 0).astype(F32)
-    gw_offset_a = over_devices(gw_offset_a, 0).astype(F32)
-    gw_reduce_a = over_devices(gw_reduce_a, 0).astype(F32)
+    images_axis = lax.axis_size("img")
+    grads = [gw_expand_b, gw_conv_b, gw_reduce_b, gw_expand_a, gw_deform_a, gw_offset_a, gw_reduce_a]
+    if gw_expand_b.shape[0] % (images_axis * 8 * 16) == 0:
+        gw_offset = jnp.pad(gw_offset_a, ((0, 0), (0, 128 - 18)))
+        grads[5] = gw_offset
+        cut = 9 * inner_width // images_axis
+        shaped = []
+        for k, grad in enumerate(grads):
+            grad = grad.astype(BF16)
+            if k == 1:
+                grad = jnp.stack([grad[:, cut * i : cut * (i + 1)] for i in range(images_axis)])
+                shaped.append(grad.reshape(images_axis, 8, -1, cut))
+            else:
+                shaped.append(grad.reshape(images_axis, 8, -1, grad.shape[-1]))
+        grads = [g.reshape(-1, g.shape[-1]) for g in reduce_all(shaped)]
+        grads[1] = grads[1].T
+        grads[5] = grads[5][:, :18]
+    else:
+
+        def over_devices(grad, dim):
+            part = lax.psum_scatter(grad.astype(BF16), "img", scatter_dimension=dim, tiled=True)
+            return lax.psum(part, ("row", "col"))
+
+        grads = [over_devices(g, 1 if k == 1 else 0) for k, g in enumerate(grads)]
+        grads[1] = grads[1].T
+    gw_expand_b, gw_conv_b, gw_reduce_b, gw_expand_a, gw_deform_a, gw_offset_a, gw_reduce_a = (
+        g.astype(F32) for g in grads
+    )
     return (
         feature_out,
         grad_in,

time: 998 us -> 829 us (0.83)
  waiting for transfers between devices: 302 us -> 0 us
  Pallas kernels: 289 us -> 481 us
  blocking collectives: 25.9 us -> 0 us
  between operations: 16.1 us -> 3.33 us
  matrix products: 106 us -> 93.3 us
  local copies, waits for them, and re-layouts: 83.6 us -> 73.1 us
    reduce_scatter x5 -> x0, waiting for transfers between devices: 223 us -> none  [over_devices(): lax.psum_scatter(grad.astype(BF16), 'img', scatter_dimension=dim, tiled=T...]
    pallas_call x0 -> x1, Pallas kernels: none -> 197 us  [reduce_all(): pl.pallas_call(functools.partial(reduce_kernel, count), out_shape=[jax.Sh...]
    psum x1 -> x0, waiting for transfers between devices: 60.6 us -> none  [over_devices(): return lax.psum(part, ('row', 'col'))]
    psum x1 -> x0, blocking collectives: 25.9 us -> none  [over_devices(): return lax.psum(part, ('row', 'col'))]
    unnamed x10 -> x0, waiting for transfers between devices: 18 us -> none
    unnamed x144 -> x249, local copies, waits for them, and re-layouts: 30 us -> 16.8 us
  transfers between devices with their start and end apart: 8 -> 0, of which waited for: 6 -> 0; matrix products, arithmetic and copies ran while one was open for 15% -> 0% of each run, Pallas kernels for 11% -> 0%
where the time goes in v2:
time: 829 us; the launch traced here: 822 us
  Pallas kernels  481 us (58%)
  other arithmetic  172 us (21%)
  matrix products  93.3 us (11%)
  local copies, waits for them, and re-layouts  73.1 us (9%)
    pallas_call x1, Pallas kernels, reduce_all(): pl.pallas_call(functools.partial(reduce_kernel, count), out_shape=[jax.Sh...  197 us
    pallas_call x12, Pallas kernels, exchange(): pl.pallas_call(kernel, out_shape=jax.ShapeDtypeStruct((rows, 128), F32),...  147 us
    pallas_call x3, Pallas kernels, with_halo(): pl.pallas_call(functools.partial(halo_kernel, pad, reach), out_shape=jax....  39 us
    reduce_sum x3, other arithmetic, norm_backward(): jnp.sum(grad_normed, axis=0)  35.3 us
    convert_element_type x4, other arithmetic, norm_backward(): return (grad_pre.astype(BF16), sum_unit, sum_grad)  34.4 us
    pallas_call x1, Pallas kernels, sample_backward(): pl.pallas_call(unsample_kernel, grid=(images, blocks), out_shape=(jax.Sha...  31.2 us
    convert_element_type x1, other arithmetic, body(): middle = (gelu_exact(pre_a) * weight_col).astype(BF16)  23 us
    pallas_call x1, Pallas kernels, sample_forward(): pl.pallas_call(sample_kernel, grid=(images, blocks), out_shape=(jax.Shape...  21.3 us

profile of v2, /device:TPU:0, one launch (start us, length us, event | category | flops | bytes accessed | tf_op | source)
XLA Modules:
  0.0 822.1 jit_solution(14147461240621769642)
XLA Ops:
  13.3 12.7 %stats512.4 = f32[8,128]{1,0:T(8,128)} custom-call(f32[8,128]{1,0:T(8,128)} %pad_maximum_fusion.12.x_ref, f32[8,128]{1,0:T(8,128)} %broadcast_in_dim.31.count_ref), custom_call_target="tpu_custom_call" | custom-call | tf_op jit(solution)/shard_map/stats512/pallas_call | solution.py:141
  36.9 18.5 %halo_a.1 = bf16[2,32,48,512]{3,2,1,0:T(8,128)(2,1)} custom-call(bf16[2,16,32,512]{3,2,1,0:T(8,128)(2,1)} %bitcast.272), custom_call_target="tpu_custom_call" | custom-call | tf_op jit(solution)/shard_map/halo_a/pallas_call | solution.py:275
  79.6 21.3 %sample.1 = (bf16[4608,1024]{1,0:T(8,128)(2,1)}, f32[512,1024]{1,0:T(8,128)}) custom-call(bf16[2,512,1536]{2,1,0:T(8,128)(2,1)} %copy.144.rim_ref, bf16[512,4608]{1,0:T(8,128)(2,1)} %bitcast.253, s32[2,9,512]{2,1,0:T(8,128)} %broadcast_add_fusion.up_ref, s32[2,9,512]{2,1,0:T(8,128)} %add_add_fusion.left_ref, f32[2,9,512]{2,1,0:T(8,128)} %slice.222.fr_ref, ...), custom_call_target="tpu_custom_call" | custom-call | tf_op jit(solution)/shard_map/sample/pallas_call | solution.py:455
  104.2 18.1 %stats512.5 = f32[8,128]{1,0:T(8,128)} custom-call(f32[8,128]{1,0:T(8,128)} %pad_maximum_fusion.13.x_ref, f32[8,128]{1,0:T(8,128)} %broadcast_in_dim.31.count_ref), custom_call_target="tpu_custom_call" | custom-call | tf_op jit(solution)/shard_map/stats512/pallas_call | solution.py:141
  139.4 10.7 %stats2048.2 = f32[32,128]{1,0:T(8,128)} custom-call(f32[32,128]{1,0:T(8,128)} %pad_maximum_fusion.2.x_ref, f32[8,128]{1,0:T(8,128)} %broadcast_in_dim.31.count_ref), custom_call_target="tpu_custom_call" | custom-call | tf_op jit(solution)/shard_map/stats2048/pallas_call | solution.py:141
  152.7 23.0 %multiply_convert_fusion.4 = (bf16[1024,2048]{1,0:T(8,128)(2,1)S(1)}, f32[1024,2048]{1,0:T(8,128)}, f32[1024,2048]{1,0:T(8,128)}) fusion(f32[1024]{0:T(1024)S(1)} %reshape.399, bf16[2,16,32,2048]{3,2,1,0:T(8,128)(2,1)} %copy-done.14, f32[2048]{0:T(1024)S(1)} %slice-done.2, f32[2048]{0:T(1024)S(1)} %get-tuple-element.106, f32[2048]{0:T(1024)S(1)} %get-tuple-element.96, ...), kind=kLoop, calls=%fused_computation.36 | loop fusion | flops 150994944 | bytes 33591296 | tf_op jit(solution)/shard_map/convert_element_type | solution.py:956
  180.7 10.0 %stats512.6 = f32[8,128]{1,0:T(8,128)} custom-call(f32[8,128]{1,0:T(8,128)} %pad_maximum_fusion.14.x_ref, f32[8,128]{1,0:T(8,128)} %broadcast_in_dim.31.count_ref), custom_call_target="tpu_custom_call" | custom-call | tf_op jit(solution)/shard_map/stats512/pallas_call | solution.py:141
  201.6 10.3 %halo_b.2.rim_ref = bf16[2,20,48,512]{3,2,1,0:T(8,128)(2,1)} custom-call(bf16[2,16,32,512]{3,2,1,0:T(8,128)(2,1)} %bitcast.271), custom_call_target="tpu_custom_call" | custom-call | tf_op jit(solution)/shard_map/halo_b/pallas_call | solution.py:275
  228.1 11.4 %stats512.7 = f32[8,128]{1,0:T(8,128)} custom-call(f32[8,128]{1,0:T(8,128)} %pad_maximum_fusion.15.x_ref, f32[8,128]{1,0:T(8,128)} %broadcast_in_dim.31.count_ref), custom_call_target="tpu_custom_call" | custom-call | tf_op jit(solution)/shard_map/stats512/pallas_call | solution.py:141
  256.3 10.7 %stats2048.3 = f32[32,128]{1,0:T(8,128)} custom-call(f32[32,128]{1,0:T(8,128)} %pad_maximum_fusion.3.x_ref, f32[8,128]{1,0:T(8,128)} %broadcast_in_dim.31.count_ref), custom_call_target="tpu_custom_call" | custom-call | tf_op jit(solution)/shard_map/stats2048/pallas_call | solution.py:141
  269.0 26.2 %fusion.98 = (f32[2048]{0:T(1024)S(1)}, f32[2048]{0:T(1024)S(1)}, f32[1024,2048]{1,0:T(8,128)}, f32[1024,2048]{1,0:T(8,128)}) fusion(f32[2048]{0:T(1024)S(1)} %get-tuple-element.100, f32[1024,2048]{1,0:T(8,128)} %copy-done.3, f32[2048]{0:T(1024)S(1)} %get-tuple-element.92, f32[1024]{0:T(1024)S(1)} %reshape.399, bf16[2,16,32,2048]{3,2,1,0:T(8,128)(2,1)} %param.33, ...), kind=kLoop, calls=%fused_computation.307 | loop fusion | flops 171962368 | bytes 33607680 | tf_op jit(solution)/shard_map/reduce_sum | solution.py:846
  295.9 10.4 %sums2048.2 = f32[32,128]{1,0:T(8,128)} custom-call(f32[32,128]{1,0:T(8,128)} %pad_maximum_fusion.4.x_ref), custom_call_target="tpu_custom_call" | custom-call | tf_op jit(solution)/shard_map/sums2048/pallas_call | solution.py:141
  307.1 14.5 %multiply_convert_fusion.2 = (bf16[1024,2048]{1,0:T(8,128)(2,1)S(1)}, bf16[1024,2048]{1,0:T(8,128)(2,1)}) fusion(f32[1024,2048]{1,0:T(8,128)} %get-tuple-element.60, f32[1024,2048]{1,0:T(8,128)} %copy-done.3, f32[2048]{0:T(1024)S(1)} %get-tuple-element.102, f32[2048]{0:T(1024)S(1)} %get-tuple-element.101, f32[2048]{0:T(1024)S(1)} %get-tuple-element.99, ...), kind=kLoop, calls=%fused_computation.17 | loop fusion | flops 35651584 | bytes 37810176 | tf_op jit(solution)/shard_map/convert_element_type | solution.py:854
  326.8 10.1 %sums512.4 = f32[8,128]{1,0:T(8,128)} custom-call(f32[8,128]{1,0:T(8,128)} %pad_maximum_fusion.16.x_ref), custom_call_target="tpu_custom_call" | custom-call | tf_op jit(solution)/shard_map/sums512/pallas_call | solution.py:141
  342.7 10.2 %halo_b.3.back_ref = bf16[2,20,48,512]{3,2,1,0:T(8,128)(2,1)} custom-call(bf16[2,16,32,512]{3,2,1,0:T(8,128)(2,1)} %bitcast.258), custom_call_target="tpu_custom_call" | custom-call | tf_op jit(solution)/shard_map/halo_b/pallas_call | solution.py:275
  352.9 16.4 %unconv.1 = (f32[1024,512]{1,0:T(8,128)}, bf16[512,4608]{1,0:T(8,128)(2,1)}) custom-call(bf16[2,20,48,512]{3,2,1,0:T(8,128)(2,1)} %halo_b.2.rim_ref, bf16[2,20,48,512]{3,2,1,0:T(8,128)(2,1)} %halo_b.3.back_ref, bf16[4608,512]{1,0:T(8,128)(2,1)} %w_ref.4, bf16[1024,512]{1,0:T(8,128)(2,1)} %copy.153.g_ref), custom_call_target="tpu_custom_call" | custom-call | tf_op jit(solution)/shard_map/unconv/pallas_call | solution.py:652
  378.0 11.5 %sums512.5 = f32[8,128]{1,0:T(8,128)} custom-call(f32[8,128]{1,0:T(8,128)} %pad_maximum_fusion.17.x_ref), custom_call_target="tpu_custom_call" | custom-call | tf_op jit(solution)/shard_map/sums512/pallas_call | solution.py:141
  390.3 20.3 %fusion.97 = (f32[2048]{0:T(1024)S(1)}, f32[2048]{0:T(1024)S(1)}, f32[1024,2048]{1,0:T(8,128)}) fusion(f32[2048]{0:T(1024)S(1)} %get-tuple-element.96, f32[1024,2048]{1,0:T(8,128)} %copy-done.2, f32[2048]{0:T(1024)S(1)} %get-tuple-element.94, f32[1024,2048]{1,0:T(8,128)} %get-tuple-element.67, f32[1024,2048]{1,0:T(8,128)} %get-tuple-element.68, ...), kind=kOutput, calls=%fused_computation.306 | convolution fusion | flops 2194141184 | bytes 48281600 | tf_op jit(solution)/shard_map/pm,cm->pc/dot_general | solution.py:999
  411.2 10.7 %sums2048.3 = f32[32,128]{1,0:T(8,128)} custom-call(f32[32,128]{1,0:T(8,128)} %pad_maximum_fusion.5.x_ref), custom_call_target="tpu_custom_call" | custom-call | tf_op jit(solution)/shard_map/sums2048/pallas_call | solution.py:141
  455.6 31.2 %unsample.1 = (f32[2,1536,512]{2,1,0:T(8,128)}, f32[2,9,512]{2,1,0:T(8,128)}, f32[2,9,512]{2,1,0:T(8,128)}) custom-call(bf16[2,1536,512]{2,1,0:T(8,128)(2,1)} %bitcast.250, bf16[512,1024]{1,0:T(8,128)(2,1)} %fusion.31.g_ref, bf16[4608,512]{1,0:T(8,128)(2,1)} %w_ref.5, s32[2,9,512]{2,1,0:T(8,128)} %broadcast_add_fusion.up_ref, ...), custom_call_target="tpu_custom_call" | custom-call | tf_op jit(solution)/shard_map/unsample/pallas_call | solution.py:528
  509.1 18.8 %spill.1 = f32[2,16,32,512]{3,2,1,0:T(8,128)} custom-call(f32[2,32,48,512]{3,2,1,0:T(8,128)} %bitcast.252), custom_call_target="tpu_custom_call" | custom-call | tf_op jit(solution)/shard_map/spill/pallas_call | solution.py:372
  536.2 20.6 %sums512.7 = f32[8,128]{1,0:T(8,128)} custom-call(f32[8,128]{1,0:T(8,128)} %pad_maximum_fusion.19.x_ref), custom_call_target="tpu_custom_call" | custom-call | tf_op jit(solution)/shard_map/sums512/pallas_call | solution.py:141
  557.5 10.6 %multiply_convert_fusion = bf16[1024,2048]{1,0:T(8,128)(2,1)} fusion(f32[1024,2048]{1,0:T(8,128)} %get-tuple-element.144, f32[1024]{0:T(1024)S(1)} %reshape.399, bf16[2048,512]{1,0:T(8,128)(2,1)} %param.22, f32[1024,512]{0,1:T(8,128)} %get-tuple-element.57, f32[1024,512]{0,1:T(8,128)S(1)} %copy-done.8, f32[512]{0:T(512)S(1)} %get-tuple-element.126, ...), kind=kOutput, calls=%fused_computation.13 | convolution fusion | flops 2158493696 | bytes 18888704 | tf_op jit(solution)/shard_map/pm,cm->pc/dot_general | solution.py:1040
  609.9 197.1 %reduce.3 = (bf16[8,16,2048]{2,1,0:T(8,128)(2,1)}, bf16[8,64,1152]{2,1,0:T(8,128)(2,1)}, bf16[8,64,512]{2,1,0:T(8,128)(2,1)}, bf16[8,16,2048]{2,1,0:T(8,128)(2,1...) custom-call(bf16[4,8,16,2048]{3,2,1,0:T(8,128)(2,1)} %bitcast.274, ...), custom_call_target="tpu_custom_call" | custom-call | tf_op jit(solution)/shard_map/reduce/pallas_call | solution.py:816
  (383 shorter events, 263.3 us)
Async XLA Ops:
  0.7 132.3 %copy-start = (bf16[512,2048]{1,0:T(8,128)(2,1)S(1)}, bf16[512,2048]{1,0:T(8,128)(2,1)}, u32[]{:S(2)}) copy-start(bf16[512,2048]{1,0:T(8,128)(2,1)} %param.25) | copy-start | bytes 6291460
  4.8 23.2 %copy-start.85 = (f32[512]{0:T(512)}, f32[512]{0:T(512)S(1)}, u32[]{:S(2)}) copy-start(f32[512]{0:T(512)S(1)} %get-tuple-element.113) | copy-start | bytes 6148
  4.8 120.2 %copy-start.56 = (f32[512]{0:T(512)}, f32[512]{0:T(512)S(1)}, u32[]{:S(2)}) copy-start(f32[512]{0:T(512)S(1)} %get-tuple-element.114) | copy-start | bytes 6148
  8.6 17.4 %copy-start.89 = (f32[3072]{0:T(1024)S(1)}, f32[3072]{0:T(1024)}, u32[]{:S(2)}) copy-start(f32[3072]{0:T(1024)} %param.26) | copy-start | bytes 36868
  100.9 21.4 %copy-start.36 = (f32[8,128]{1,0:T(8,128)S(1)}, f32[8,128]{1,0:T(8,128)}, u32[]{:S(2)}) copy-start(f32[8,128]{1,0:T(8,128)} %stats512.4) | copy-start | bytes 12292
  135.5 17.2 %slice-start.2 = ((f32[3072]{0:T(1024)}), f32[2048]{0:T(1024)S(1)}, s32[]{:S(2)}) async-start(f32[3072]{0:T(1024)} %param.27), calls=%async_computation.2 | async-start | bytes 16384 | tf_op jit(solution)/shard_map/slice | solution.py:953
  152.7 23.0 %copy-start.115 = (bf16[2048,512]{1,0:T(8,128)(2,1)S(1)}, bf16[2048,512]{1,0:T(8,128)(2,1)}, u32[]{:S(2)}) copy-start(bf16[2048,512]{1,0:T(8,128)(2,1)} %param.28) | copy-start | bytes 6291460
  178.3 22.1 %copy-start.87 = (f32[512]{0:T(512)}, f32[512]{0:T(512)S(1)}, u32[]{:S(2)}) copy-start(f32[512]{0:T(512)S(1)} %get-tuple-element.112) | copy-start | bytes 6148
  178.3 63.9 %copy-start.92 = (f32[512]{0:T(512)}, f32[512]{0:T(512)S(1)}, u32[]{:S(2)}) copy-start(f32[512]{0:T(512)S(1)} %get-tuple-element.111) | copy-start | bytes 6148
  178.3 22.0 %copy-start.83 = (f32[512]{0:T(512)}, f32[512]{0:T(512)S(1)}, u32[]{:S(2)}) copy-start(f32[512]{0:T(512)S(1)} %slice.234) | copy-start | bytes 6148
  192.7 197.5 %copy-start.53 = (f32[512]{0:T(512)}, f32[512]{0:T(512)S(1)}, u32[]{:S(2)}) copy-start(f32[512]{0:T(512)S(1)} %get-tuple-element.118) | copy-start | bytes 6148
  224.9 14.7 %copy-start.37 = (f32[8,128]{1,0:T(8,128)S(1)}, f32[8,128]{1,0:T(8,128)}, u32[]{:S(2)}) copy-start(f32[8,128]{1,0:T(8,128)} %stats512.6) | copy-start | bytes 12292
  240.9 80.7 %copy-start.63 = (f32[512]{0:T(512)}, f32[512]{0:T(512)S(1)}, u32[]{:S(2)}) copy-start(f32[512]{0:T(512)S(1)} %get-tuple-element.115) | copy-start | bytes 6148
  242.2 95.6 %copy-start.44 = (f32[512]{0:T(512)}, f32[512]{0:T(512)S(1)}, u32[]{:S(2)}) copy-start(f32[512]{0:T(512)S(1)} %get-tuple-element.120) | copy-start | bytes 6148
  307.0 14.5 %copy-start.23 = (f32[1024,512]{0,1:T(8,128)S(1)}, f32[1024,512]{0,1:T(8,128)}, u32[]{:S(2)}) copy-start(f32[1024,512]{0,1:T(8,128)} %get-tuple-element.63) | copy-start | bytes 6291460
  307.0 14.5 %copy-start.93 = (f32[512]{0:T(512)S(1)}, f32[512]{0:T(512)}, u32[]{:S(2)}) copy-start(f32[512]{0:T(512)} %copy-done.92) | copy-start | bytes 6148
  307.0 14.6 %copy-start.114 = (bf16[512,2048]{1,0:T(8,128)(2,1)S(1)}, bf16[512,2048]{1,0:T(8,128)(2,1)}, u32[]{:S(2)}) copy-start(bf16[512,2048]{1,0:T(8,128)(2,1)} %param.30) | copy-start | bytes 6291460
  321.6 16.1 %copy-start.98 = (f32[512]{0:T(512)S(1)}, f32[512]{0:T(512)}, u32[]{:S(2)}) copy-start(f32[512]{0:T(512)} %get-tuple-element.108) | copy-start | bytes 6148
  372.6 17.6 %copy-start.109 = (f32[512]{0:T(512)S(1)}, f32[512]{0:T(512)}, u32[]{:S(2)}) copy-start(f32[512]{0:T(512)} %get-tuple-element.107) | copy-start | bytes 6148
  390.2 20.4 %copy-start.103 = (f32[512]{0:T(512)}, f32[512]{0:T(512)S(1)}, u32[]{:S(2)}) copy-start(f32[512]{0:T(512)S(1)} %get-tuple-element.129) | copy-start | bytes 6148
  390.2 20.4 %copy-start.106 = (f32[512]{0:T(512)}, f32[512]{0:T(512)S(1)}, u32[]{:S(2)}) copy-start(f32[512]{0:T(512)S(1)} %get-tuple-element.130) | copy-start | bytes 6148
  390.2 32.4 %copy-start.38 = (f32[2048]{0:T(1024)S(1)}, f32[2048]{0:T(1024)}, u32[]{:S(2)}) copy-start(f32[2048]{0:T(1024)} %get-tuple-element.95) | copy-start | bytes 24580
  430.2 16.4 %copy-start.96 = (f32[512]{0:T(512)S(1)}, f32[512]{0:T(512)}, u32[]{:S(2)}) copy-start(f32[512]{0:T(512)} %get-tuple-element.104) | copy-start | bytes 6148
  531.2 26.3 %copy-start.94 = (f32[512]{0:T(512)S(1)}, f32[512]{0:T(512)}, u32[]{:S(2)}) copy-start(f32[512]{0:T(512)} %get-tuple-element.103) | copy-start | bytes 6148
  (100 other events, 484.1 us)

commit v3 on v1

v3 whole, which is shorter than its diff:
```python
import functools
import types

import jax
import jax.numpy as jnp
import numpy as np
from jax import lax
from jax.experimental import pallas as pl
from jax.experimental.pallas import tpu as pltpu
from jax.sharding import PartitionSpec as P

LONG = 64
SHORT = 44
BOUND = 4
EPSILON = 1e-05
IMG, ROW, COL = "img", "row", "col"
MESH = pl.DeviceIdType.MESH
VMEM = pl.BlockSpec(memory_space=pltpu.VMEM)
VMEM_LIMIT = 60 * 1024 * 1024
F32 = jnp.float32
BF16 = jnp.bfloat16
REACH = BOUND + 3
PAD = 8
HALF = 16
STATS_CID, HALO_CID, FORWARD_A_CID, FORWARD_B_CID = 0, 1, 2, 3
BACKWARD_B_CID, BACKWARD_A_CID, BACKWARD_S_CID, LAST_CID = 4, 5, 6, 7


def gelu_exact(values):
    return jax.nn.gelu(values, approximate=False)


def group_of(axes):
    sizes = [lax.axis_size(a) for a in axes]
    total = int(np.prod(sizes))
    place = lax.axis_index(axes[0])
    for axis, size in zip(axes[1:], sizes[1:]):
        place = place * size + lax.axis_index(axis)

    def device(step):
        spot = lax.rem(place + step, total)
        coords = {}
        for axis, size in zip(reversed(axes), reversed(sizes)):
            coords[axis] = lax.rem(spot, size)
            spot = spot // size
        return coords

    return place, total, device


PLANE = (ROW, COL)
LINE = (IMG,)


def entry_barrier(groups):
    barrier = pltpu.get_barrier_semaphore()
    count = 0
    for axes in groups:
        _, total, device = group_of(axes)
        for step in range(1, total):
            pl.semaphore_signal(barrier, inc=1, device_id=device(step), device_id_type=MESH)
        count += total - 1
    pl.semaphore_wait(barrier, count)


def gather_start(axes, slots, send_sem, recv_sem):
    _, total, device = group_of(axes)
    for step in range(1, total):
        pltpu.make_async_remote_copy(
            src_ref=slots.at[0],
            dst_ref=slots.at[step],
            send_sem=send_sem,
            recv_sem=recv_sem,
            device_id=device(step),
            device_id_type=MESH,
        ).start()


def gather_wait(axes, slots, sem):
    _, total, _ = group_of(axes)
    others = slots.at[pl.ds(1, total - 1)]
    pltpu.make_async_copy(others, others, sem).wait()


def in_order(axes, slots):
    place, total, _ = group_of(axes)
    return [slots[lax.rem(place - spot + total, total)] for spot in range(total)]


def stats_kernel(plane_count, x_ref, count_ref, o_ref, slots1, slots2, send_sems, recv_sems):
    entry_barrier((PLANE, LINE))
    half = x_ref.shape[0] // 2
    total_count = plane_count * lax.axis_size(IMG)
    slots1[0] = x_ref[...]
    gather_start(PLANE, slots1, send_sems.at[0], recv_sems.at[0])
    gather_wait(PLANE, slots1, recv_sems.at[0])
    parts = in_order(PLANE, slots1)
    total = functools.reduce(lambda a, b: a + b, [p[:half] for p in parts])
    center = total / plane_count
    spread = functools.reduce(lambda a, b: a + b, [p[half:] for p in parts])
    for spot, part in enumerate(parts):
        count = count_ref[spot : spot + 1, :]
        away = part[:half] / jnp.maximum(count, 1.0) - center
        spread = spread + count * (away * away)
    slots2[0, :half] = total
    slots2[0, half:] = spread
    gather_start(LINE, slots2, send_sems.at[1], recv_sems.at[1])
    gather_wait(LINE, slots2, recv_sems.at[1])
    parts = in_order(LINE, slots2)
    center = functools.reduce(lambda a, b: a + b, [p[:half] for p in parts]) / total_count
    spread = functools.reduce(lambda a, b: a + b, [p[half:] for p in parts])
    for part in parts:
        away = part[:half] / plane_count - center
        spread = spread + plane_count * (away * away)
    o_ref[:half] = center
    o_ref[half:] = spread / total_count
    gather_wait(PLANE, slots1, send_sems.at[0])
    gather_wait(LINE, slots2, send_sems.at[1])


def stats_over_devices(total, spread, counts, plane_count):
    width = total.shape[0]
    both = jnp.concatenate([total, spread]).reshape(-1, 128)
    rows = both.shape[0]
    scratch = []
    for axes in (PLANE, LINE):
        size = int(np.prod([lax.axis_size(a) for a in axes]))
        scratch.append(pltpu.VMEM((size, rows, 128), F32))
    scratch += [pltpu.SemaphoreType.DMA((2,)), pltpu.SemaphoreType.DMA((2,))]
    out = pl.pallas_call(
        functools.partial(stats_kernel, plane_count),
        out_shape=jax.ShapeDtypeStruct((rows, 128), F32),
        in_specs=[VMEM, VMEM],
        out_specs=VMEM,
        scratch_shapes=scratch,
        compiler_params=pltpu.CompilerParams(collective_id=STATS_CID, has_side_effects=True),
    )(both, counts)
    out = out.reshape(2, width)
    return out[0], out[1]


def halo_peers():
    row, rows, col = lax.axis_index(ROW), lax.axis_size(ROW), lax.axis_index(COL)
    return row, rows, col, {COL: 1 - col}, {ROW: row - 1}, {ROW: row + 1}


def halo_barrier():
    row, rows, _, pair, above, below = halo_peers()
    barrier = pltpu.get_barrier_semaphore()
    pl.semaphore_signal(barrier, inc=1, device_id=pair, device_id_type=MESH)

    @pl.when(row > 0)
    def _():
        pl.semaphore_signal(barrier, inc=1, device_id=above, device_id_type=MESH)

    @pl.when(row < rows - 1)
    def _():
        pl.semaphore_signal(barrier, inc=1, device_id=below, device_id_type=MESH)

    count = 1 + (row > 0).astype(jnp.int32) + (row < rows - 1).astype(jnp.int32)
    pl.semaphore_wait(barrier, count)


def halo_kernel(pad, reach, h_ref, o_ref, send_sems, recv_sems):
    row, rows, col, pair, above, below = halo_peers()
    tile_rows, tile_cols = h_ref.shape[1], h_ref.shape[2]
    off = pl.multiple_of(HALF * col, HALF)
    spot = pl.multiple_of(2 * HALF * col, HALF)
    own = pl.ds(off, tile_cols)
    mid = pl.ds(HALF, HALF)
    upper = pl.ds(pad - reach, reach)
    lower = pl.ds(pad + tile_rows, reach)
    zero_row = jnp.zeros((h_ref.shape[0],) + o_ref.shape[2:], o_ref.dtype)

    def blank(at):
        for k in range(at.start, at.stop):
            o_ref[:, k] = zero_row

    blank(slice(0, pad - reach))
    blank(slice(pad + tile_rows + reach, 2 * pad + tile_rows))

    @pl.when(row == 0)
    def _():
        blank(slice(pad - reach, pad))

    @pl.when(row == rows - 1)
    def _():
        blank(slice(pad + tile_rows, pad + tile_rows + reach))

    halo_barrier()

    def copy(src, dst, k, device):
        return pltpu.make_async_remote_copy(
            src_ref=src,
            dst_ref=dst,
            send_sem=send_sems.at[k],
            recv_sem=recv_sems.at[k],
            device_id=device,
            device_id_type=MESH,
        )

    to_pair = copy(
        h_ref.at[:, :, pl.ds(pl.multiple_of(HALF * (1 - col), HALF), HALF)],
        o_ref.at[:, pl.ds(pad, tile_rows), pl.ds(spot, HALF)],
        0,
        pair,
    )
    up = copy(h_ref.at[:, pl.ds(0, reach)], o_ref.at[:, lower, own], 1, above)
    down = copy(h_ref.at[:, pl.ds(tile_rows - reach, reach)], o_ref.at[:, upper, own], 2, below)
    from_below = copy(o_ref.at[:, lower, mid], o_ref.at[:, lower, pl.ds(spot, HALF)], 3, pair)
    from_above = copy(o_ref.at[:, upper, mid], o_ref.at[:, upper, pl.ds(spot, HALF)], 4, pair)

    @pl.when(row > 0)
    def _():
        up.start()

    @pl.when(row < rows - 1)
    def _():
        down.start()

    to_pair.start()
    for n in range(h_ref.shape[0]):
        o_ref[n, pl.ds(pad, tile_rows), own, :] = h_ref[n]

    @pl.when(row < rows - 1)
    def _():
        up.wait_recv()
        from_below.start()

    @pl.when(row > 0)
    def _():
        down.wait_recv()
        from_above.start()

    to_pair.wait()

    @pl.when(row < rows - 1)
    def _():
        down.wait_send()
        from_below.wait()

    @pl.when(row > 0)
    def _():
        up.wait_send()
        from_above.wait()


def with_halo(tile, pad, reach):
    images, rows, cols, width = tile.shape
    return pl.pallas_call(
        functools.partial(halo_kernel, pad, reach),
        out_shape=jax.ShapeDtypeStruct((images, rows + 2 * pad, cols + HALF, width), tile.dtype),
        in_specs=[VMEM],
        out_specs=VMEM,
        scratch_shapes=[pltpu.SemaphoreType.DMA((5,)), pltpu.SemaphoreType.DMA((5,))],
        compiler_params=pltpu.CompilerParams(
            collective_id=HALO_CID, has_side_effects=True, vmem_limit_bytes=VMEM_LIMIT
        ),
    )(tile)


BLOCK_ROWS = 8
SPAN = 17
WINDOW = 3 * BLOCK_ROWS


def tap_span(group, cols):
    first = 2 + 2 * group
    start = first * cols // 128 * 128
    stop = -(-(first + SPAN) * cols // 128) * 128
    return first, start, stop


def tap_weights(tap, block, cols, up_ref, left_ref, fr_ref, fc_ref, image=0, lanes=slice(None)):
    up, left, fr, fc = (
        ref[image, tap : tap + 1, lanes] for ref in (up_ref, left_ref, fr_ref, fc_ref)
    )
    up = up - block * BLOCK_ROWS
    pixels = up.shape[1]

    def pair(size, at, frac):
        ids = lax.broadcasted_iota(jnp.int32, (size, pixels), 0)
        first, second = ids == at, ids == at + 1
        value = jnp.where(first, 1.0 - frac, jnp.where(second, frac, 0.0))
        slope = jnp.where(second, 1.0, jnp.where(first, -1.0, 0.0))
        return value, slope

    return pair(WINDOW, up, fr) + pair(cols, left, fc)


def write_table(table, lane, row_w, col_w, group, cols):
    first, start, stop = tap_span(group, cols)
    pixels = row_w.shape[1]
    low = start // cols
    high = -(-stop // cols)
    for r in range(low, min(high, WINDOW)):
        table[r * cols : (r + 1) * cols, lane : lane + pixels] = (
            row_w[r : r + 1, :] * col_w
        ).astype(BF16)


def sample_kernel(rim_ref, w_ref, up_ref, left_ref, fr_ref, fc_ref, s_ref, d_ref, table):
    block = pl.program_id(1)
    width = rim_ref.shape[1]
    cols = table.shape[0] // WINDOW
    base = block * (BLOCK_ROWS * cols)
    for tap in range(9):
        row_w, _, col_w, _ = tap_weights(tap, block, cols, up_ref, left_ref, fr_ref, fc_ref)
        write_table(table, 0, row_w, col_w, tap // 3, cols)
        _, start, stop = tap_span(tap // 3, cols)
        cells = pl.ds(pl.multiple_of(base + start, 128), stop - start)
        value = jnp.dot(rim_ref[0, :, cells], table[start:stop, :], preferred_element_type=F32)
        s_ref[tap * width : (tap + 1) * width, :] = value.astype(BF16)
    d_ref[...] = jnp.dot(w_ref[...], s_ref[...], preferred_element_type=F32)


def sample_forward(rim_t, w_t, up, left, fr, fc, cols):
    images, width, cells = rim_t.shape
    pixels = up.shape[-1]
    blocks = 2
    step = pixels // blocks
    tap_spec = pl.BlockSpec((1, 16, step), lambda i, b: (i, 0, b))
    return pl.pallas_call(
        sample_kernel,
        grid=(images, blocks),
        out_shape=(
            jax.ShapeDtypeStruct((9 * width, images * pixels), BF16),
            jax.ShapeDtypeStruct((width, images * pixels), F32),
        ),
        in_specs=[
            pl.BlockSpec((1, width, cells), lambda i, b: (i, 0, 0)),
            pl.BlockSpec((width, 9 * width), lambda i, b: (0, 0)),
            tap_spec,
            tap_spec,
            tap_spec,
            tap_spec,
        ],
        out_specs=(
            pl.BlockSpec((9 * width, step), lambda i, b: (0, i * blocks + b)),
            pl.BlockSpec((width, step), lambda i, b: (0, i * blocks + b)),
        ),
        scratch_shapes=[pltpu.VMEM((WINDOW * cols, step), BF16)],
        compiler_params=pltpu.CompilerParams(vmem_limit_bytes=VMEM_LIMIT),
    )(rim_t, w_t, up, left, fr, fc)


def build_shifted(rim_ref, shifted):
    images, rows, cols, width = rim_ref.shape
    col = lax.axis_index(COL)
    tile = cols - HALF

    def fill(first):
        def one_row(k, carry):
            for n in range(images):
                line = rim_ref[n, k].astype(F32)
                none = jnp.zeros((2, width), F32)
                for d in range(3):
                    at = first + 2 * (d - 1)
                    if at < 0:
                        part = jnp.concatenate([none, line[: tile - 2]], axis=0)
                    elif at + tile > cols:
                        part = jnp.concatenate([line[at:], none], axis=0)
                    else:
                        part = line[at : at + tile]
                    shifted[n, k, :, d * width : (d + 1) * width] = part.astype(BF16)
            return carry

        lax.fori_loop(0, rows, one_row, 0)

    @pl.when(col == 0)
    def _():
        fill(0)

    @pl.when(col == 1)
    def _():
        fill(HALF)


def conv_product(shifted, w_ref, o_ref):
    images, rows, cols, width3 = shifted.shape
    tile_rows = rows - 4
    pixels = tile_rows * cols
    for n in range(images):
        total = None
        for i in range(3):
            taps = shifted[n, 2 * i : 2 * i + tile_rows].reshape(pixels, width3)
            term = jnp.dot(taps, w_ref[i * width3 : (i + 1) * width3, :], preferred_element_type=F32)
            total = term if total is None else total + term
        o_ref[n * pixels : (n + 1) * pixels, :] = total


def conv_weight_product(turned, shifted, gw_ref, i):
    images, rows, cols, width3 = shifted.shape
    tile_rows = rows - 4
    pixels = tile_rows * cols
    total = None
    for n in range(images):
        taps = shifted[n, 2 * i : 2 * i + tile_rows].reshape(pixels, width3)
        term = jnp.dot(turned[:, n * pixels : (n + 1) * pixels], taps, preferred_element_type=F32)
        total = term if total is None else total + term
    put_lanes(gw_ref, i * width3, total)


def unconv_product(shifted, w_ref, o_ref):
    images, rows, cols, width3 = shifted.shape
    width = width3 // 3
    tile_rows = rows - 4
    pixels = tile_rows * cols
    for n in range(images):
        total = None
        for tap in range(9):
            i, d = 2 - tap // 3, 2 - tap % 3
            grads = shifted[n, 2 * i : 2 * i + tile_rows, :, d * width : (d + 1) * width]
            term = lax.dot_general(
                grads.reshape(pixels, width),
                w_ref[tap * width : (tap + 1) * width, :],
                (((1,), (1,)), ((), ())),
                preferred_element_type=F32,
            )
            total = term if total is None else total + term
        o_ref[n * pixels : (n + 1) * pixels, :] = total


def halves(width):
    first = -(-width // 256) * 128
    return ((0, first), (first, width - first)) if first < width else ((0, width),)


def remote(src, dst, send, recv, device):
    return pltpu.make_async_remote_copy(
        src_ref=src, dst_ref=dst, send_sem=send, recv_sem=recv, device_id=device, device_id_type=MESH
    )


def arrival(ref, sem):
    return pltpu.make_async_copy(ref, ref, sem)


class Plane:
    @staticmethod
    def scratch(shape):
        images, _, rows, width = shape
        count = len(halves(width))
        return [
            pltpu.VMEM((images, 4, rows, width), BF16),
            pltpu.VMEM((images, 2, rows, width), BF16),
            pltpu.SemaphoreType.DMA((count, 3)),
            pltpu.SemaphoreType.DMA((count, 3)),
        ]

    def __init__(self, src, eighth, refs, part):
        half, quarter, send, recv = refs
        lanes = pl.ds(*halves(src.shape[-1])[part])
        self.src, self.half, self.quarter = (
            ref.at[:, :, :, lanes] for ref in (src, half, quarter)
        )
        self.eighth = eighth.at[:, :, lanes]
        self.images = src.shape[0]
        self.send, self.recv = [send.at[part, k] for k in range(3)], [recv.at[part, k] for k in range(3)]
        self.x_first = part == 0
        row, col = lax.axis_index(ROW), lax.axis_index(COL)
        bits = (lax.rem(row, 2), row // 2)
        peers = ({ROW: row + 1 - 2 * bits[0]}, {ROW: row + 2 - 4 * bits[1]})
        order = (0, 1) if self.x_first else (1, 0)
        self.a, self.b = (bits[k] for k in order)
        self.first, self.second = (peers[k] for k in order)
        self.mine, self.pair, self.other = 4 * col, {COL: 1 - col}, 4 * (1 - col)

    def spot(self, bit, free):
        return bit + 2 * free if self.x_first else 2 * bit + free

    def steps(self):
        return [self.to_pair, self.to_first, self.to_second, self.done]

    def to_pair(self):
        src = self.src.at[:, pl.ds(self.other, 4)]
        remote(src, self.half, self.send[0], self.recv[0], self.pair).start()

    def to_first(self):
        arrival(self.half, self.recv[0]).wait()

        def add(i, carry):
            for s in range(4):
                own = self.src[i, self.mine + s].astype(F32)
                self.half[i, s] = (own + self.half[i, s].astype(F32)).astype(BF16)
            return carry

        lax.fori_loop(0, self.images, add, 0)
        for k in range(2):
            src = self.half.at[:, self.spot(1 - self.a, k)]
            remote(src, self.quarter.at[:, k], self.send[1], self.recv[1], self.first).start()

    def to_second(self):
        arrival(self.quarter, self.recv[1]).wait()

        def add(i, carry):
            for k in range(2):
                own = self.half[i, self.spot(self.a, k)].astype(F32)
                self.quarter[i, k] = (own + self.quarter[i, k].astype(F32)).astype(BF16)
            return carry

        lax.fori_loop(0, self.images, add, 0)
        src = self.quarter.at[:, 1 - self.b]
        remote(src, self.eighth, self.send[2], self.recv[2], self.second).start()

    def done(self):
        arrival(self.eighth, self.recv[2]).wait()

        def add(i, carry):
            own = self.quarter[i, self.b].astype(F32)
            self.eighth[i] = (own + self.eighth[i].astype(F32)).astype(BF16)
            return carry

        lax.fori_loop(0, self.images, add, 0)
        arrival(self.half, self.send[0]).wait()
        arrival(self.quarter, self.send[1]).wait()
        arrival(self.eighth, self.send[2]).wait()


class Line:
    @staticmethod
    def scratch(shape):
        images, rows, width = shape
        count = len(halves(width))
        return [
            pltpu.VMEM(shape, BF16),
            pltpu.SemaphoreType.DMA((count, 3)),
            pltpu.SemaphoreType.DMA((count, 3)),
        ]

    def __init__(self, eighth, out, refs, part):
        line, send, recv = refs
        lanes = pl.ds(*halves(eighth.shape[-1])[part])
        self.eighth, self.line, self.out = (ref.at[:, :, lanes] for ref in (eighth, line, out))
        self.images = eighth.shape[0]
        self.send, self.recv = [send.at[part, k] for k in range(3)], [recv.at[part, k] for k in range(3)]
        self.img, self.row, col = (lax.axis_index(a) for a in (IMG, ROW, COL))
        self.mine, self.pair = 4 * col, {COL: 1 - col}

    def steps(self):
        return [self.to_line, self.to_rows, self.to_pair, self.done]

    def arrived(self):
        return self.line.at[pl.ds(1, self.images - 1)]

    def to_line(self):
        for j in range(1, self.images):
            there = lax.rem(self.img + j, self.images)
            src = self.eighth.at[there]
            remote(src, self.line.at[j], self.send[0], self.recv[0], {IMG: there}).start()

    def to_rows(self):
        arrival(self.arrived(), self.recv[0]).wait()
        total = self.eighth[self.img].astype(F32)
        for j in range(1, self.images):
            total = total + self.line[j].astype(F32)
        spot = self.out.at[self.mine + self.row]
        self.out[self.mine + self.row] = total.astype(BF16)
        for j in range(1, 4):
            there = lax.rem(self.row + j, 4)
            remote(spot, spot, self.send[1], self.recv[1], {ROW: there}).start()

    def to_pair(self):
        arrival(self.out.at[pl.ds(0, 3)], self.recv[1]).wait()
        four = self.out.at[pl.ds(self.mine, 4)]
        remote(four, four, self.send[2], self.recv[2], self.pair).start()

    def done(self):
        arrival(self.out.at[pl.ds(0, 4)], self.recv[2]).wait()
        arrival(self.arrived(), self.send[0]).wait()
        arrival(self.out.at[pl.ds(0, 3)], self.send[1]).wait()
        arrival(self.out.at[pl.ds(0, 4)], self.send[2]).wait()


class SmallSum:
    @staticmethod
    def scratch(shape):
        sizes = [lax.axis_size(IMG), lax.axis_size(ROW) * lax.axis_size(COL)]
        return [pltpu.VMEM((size,) + shape[1:], BF16) for size in sizes] + [
            pltpu.SemaphoreType.DMA((2,)),
            pltpu.SemaphoreType.DMA((2,)),
        ]

    def __init__(self, src, out, refs):
        self.src, self.out = src, out
        self.slots1, self.slots2, self.send, self.recv = refs

    def steps(self):
        return [self.to_line, self.to_plane, self.done]

    def to_line(self):
        here, total, _ = group_of(LINE)
        self.slots1[0] = self.src[here]
        for j in range(1, total):
            there = lax.rem(here + j, total)
            remote(
                self.src.at[there], self.slots1.at[j], self.send.at[0], self.recv.at[0], {IMG: there}
            ).start()

    def to_plane(self):
        gather_wait(LINE, self.slots1, self.recv.at[0])
        total = added([p.astype(F32) for p in in_order(LINE, self.slots1)])
        self.slots2[0] = total.astype(BF16)
        gather_start(PLANE, self.slots2, self.send.at[1], self.recv.at[1])

    def done(self):
        gather_wait(PLANE, self.slots2, self.recv.at[1])
        self.out[...] = added([p.astype(F32) for p in in_order(PLANE, self.slots2)])
        gather_wait(LINE, self.slots1, self.send.at[0])
        gather_wait(PLANE, self.slots2, self.send.at[1])


class Jobs:
    def __init__(self):
        self.queue = []

    def add(self, *jobs):
        lists = [job.steps() for job in jobs]
        for k in range(max(len(steps) for steps in lists)):
            self.queue += [steps[k] for steps in lists if k < len(steps)]

    def tick(self, count=1):
        for _ in range(min(count, len(self.queue))):
            self.queue.pop(0)()

    def finish(self):
        self.tick(len(self.queue))


def plane_jobs(src, eighth, refs):
    return [Plane(src, eighth, refs, part) for part in range(len(halves(src.shape[-1])))]


def line_jobs(eighth, out, refs):
    return [Line(eighth, out, refs, part) for part in range(len(halves(out.shape[-1])))]


STEP = 32
PIECE = 256
CHUNK = 256


class Refs:
    def __init__(self):
        self.loads, self.stores = {}, {}

    def ready(self, *refs):
        for ref in refs:
            self.loads.pop(id(ref)).wait()

    def push(self, *refs):
        for ref in refs:
            self.stores[id(ref)].start()

    def flush(self):
        for copy in self.stores.values():
            copy.wait()


def fused(work, cid, ins, staged, outs, pushed, scratch):
    sizes = (len(ins), len(staged), len(outs), len(pushed))

    def kernel(*refs):
        r = Refs()
        refs = list(refs)

        def take(count):
            taken = refs[:count]
            del refs[:count]
            return taken

        in_refs, in_raw, out_refs, out_raw = (take(count) for count in sizes)
        for key, shape in scratch.items():
            setattr(r, key, take(len(shape)) if isinstance(shape, list) else take(1)[0])
        in_bufs, out_bufs = take(sizes[1]), take(sizes[3])
        in_sems, out_sems = take(2)
        for keys, named in ((ins, in_refs), (staged, in_bufs), (outs, out_refs), (pushed, out_bufs)):
            for key, ref in zip(keys, named):
                setattr(r, key, ref)
        for k, (raw, buf) in enumerate(zip(in_raw, in_bufs)):
            r.loads[id(buf)] = pltpu.make_async_copy(raw, buf, in_sems.at[k])
            r.loads[id(buf)].start()
        for k, (raw, buf) in enumerate(zip(out_raw, out_bufs)):
            r.stores[id(buf)] = pltpu.make_async_copy(buf, raw, out_sems.at[k])
        work(r)
        r.flush()

    flat = []
    for shape in scratch.values():
        flat += shape if isinstance(shape, list) else [shape]
    flat += [pltpu.VMEM(a.shape, a.dtype) for a in (*staged.values(), *pushed.values())]
    flat += [pltpu.SemaphoreType.DMA((max(count, 1),)) for count in (sizes[1], sizes[3])]
    anywhere = pl.BlockSpec(memory_space=pl.ANY)
    result = pl.pallas_call(
        kernel,
        out_shape=[*outs.values(), *pushed.values()],
        in_specs=[VMEM] * sizes[0] + [anywhere] * sizes[1],
        out_specs=[VMEM] * sizes[2] + [anywhere] * sizes[3],
        scratch_shapes=flat,
        compiler_params=pltpu.CompilerParams(
            collective_id=cid, has_side_effects=True, vmem_limit_bytes=VMEM_LIMIT
        ),
    )(*ins.values(), *staged.values())
    return types.SimpleNamespace(**dict(zip((*outs, *pushed), result)))


def signal_all():
    barrier = pltpu.get_barrier_semaphore()
    for axes in (PLANE, LINE):
        _, total, device = group_of(axes)
        for step in range(1, total):
            pl.semaphore_signal(barrier, inc=1, device_id=device(step), device_id_type=MESH)


def wait_all():
    count = sum(group_of(axes)[1] - 1 for axes in (PLANE, LINE))
    pl.semaphore_wait(pltpu.get_barrier_semaphore(), count)


def added(parts):
    return functools.reduce(lambda a, b: a + b, parts)


class Exchange:
    @staticmethod
    def scratch(width):
        rows = 2 * width // 128
        sizes = [int(np.prod([lax.axis_size(a) for a in axes])) for axes in (PLANE, LINE)]
        return [
            pltpu.VMEM((sizes[0], rows, 128), F32),
            pltpu.VMEM((sizes[1], rows, 128), F32),
            pltpu.VMEM((rows, 128), F32),
            pltpu.SemaphoreType.DMA((2,)),
            pltpu.SemaphoreType.DMA((2,)),
        ]

    def __init__(self, refs):
        self.slots1, self.slots2, self.out, self.send, self.recv = refs
        self.half = self.out.shape[0] // 2

    def put(self, first, second):
        for k in range(self.half):
            self.slots1[0, k : k + 1, :] = first[:, 128 * k : 128 * (k + 1)]
            self.slots1[0, self.half + k : self.half + k + 1, :] = second[:, 128 * k : 128 * (k + 1)]
        gather_start(PLANE, self.slots1, self.send.at[0], self.recv.at[0])

    def line(self):
        gather_start(LINE, self.slots2, self.send.at[1], self.recv.at[1])

    def middle_sums(self):
        gather_wait(PLANE, self.slots1, self.recv.at[0])
        self.slots2[0] = added(in_order(PLANE, self.slots1))
        self.line()

    def finish_sums(self):
        gather_wait(LINE, self.slots2, self.recv.at[1])
        self.out[...] = added(in_order(LINE, self.slots2))
        self.drain()

    def middle_stats(self, count_ref, plane_count):
        half = self.half
        gather_wait(PLANE, self.slots1, self.recv.at[0])
        parts = in_order(PLANE, self.slots1)
        total = added([p[:half] for p in parts])
        center = total / plane_count
        spread = added([p[half:] for p in parts])
        for spot, part in enumerate(parts):
            count = count_ref[spot : spot + 1, :]
            away = part[:half] / jnp.maximum(count, 1.0) - center
            spread = spread + count * (away * away)
        self.slots2[0, :half] = total
        self.slots2[0, half:] = spread
        self.line()

    def finish_stats(self, plane_count):
        half = self.half
        total_count = plane_count * lax.axis_size(IMG)
        gather_wait(LINE, self.slots2, self.recv.at[1])
        parts = in_order(LINE, self.slots2)
        center = added([p[:half] for p in parts]) / total_count
        spread = added([p[half:] for p in parts])
        for part in parts:
            away = part[:half] / plane_count - center
            spread = spread + plane_count * (away * away)
        self.out[:half] = center
        self.out[half:] = spread / total_count
        self.drain()

    def drain(self):
        gather_wait(PLANE, self.slots1, self.send.at[0])
        gather_wait(LINE, self.slots2, self.send.at[1])

    def rows(self):
        out = self.out[...]
        first = [out[k : k + 1] for k in range(self.half)]
        second = [out[self.half + k : self.half + k + 1] for k in range(self.half)]
        return jnp.concatenate(first, axis=1), jnp.concatenate(second, axis=1)


class Halo:
    scratch = [pltpu.SemaphoreType.DMA((5,)), pltpu.SemaphoreType.DMA((5,))]

    def __init__(self, pad, reach, tile, window, sems):
        self.row, self.rows, col, pair, above, below = halo_peers()
        self.pad, self.reach, self.tile, self.window = pad, reach, tile, window
        self.tile_rows, self.tile_cols = tile.shape[1], tile.shape[2]
        self.own = own = pl.ds(pl.multiple_of(HALF * col, HALF), self.tile_cols)
        spot = pl.ds(pl.multiple_of(2 * HALF * col, HALF), HALF)
        side = pl.ds(pl.multiple_of(HALF * (1 - col), HALF), HALF)
        mid = pl.ds(HALF, HALF)
        upper = pl.ds(pad - reach, reach)
        lower = pl.ds(pad + self.tile_rows, reach)
        send, recv = sems

        def copy(src, dst, k, device):
            return pltpu.make_async_remote_copy(
                src_ref=src,
                dst_ref=dst,
                send_sem=send.at[k],
                recv_sem=recv.at[k],
                device_id=device,
                device_id_type=MESH,
            )

        w = window
        self.to_pair = copy(
            tile.at[:, :, side], w.at[:, pl.ds(pad, self.tile_rows), spot], 0, pair
        )
        self.up = copy(tile.at[:, pl.ds(0, reach)], w.at[:, lower, own], 1, above)
        self.down = copy(
            tile.at[:, pl.ds(self.tile_rows - reach, reach)], w.at[:, upper, own], 2, below
        )
        self.from_below = copy(w.at[:, lower, mid], w.at[:, lower, spot], 3, pair)
        self.from_above = copy(w.at[:, upper, mid], w.at[:, upper, spot], 4, pair)

    def blank(self):
        window, pad, reach, tile_rows = self.window, self.pad, self.reach, self.tile_rows
        zero = jnp.zeros((window.shape[0],) + window.shape[2:], window.dtype)

        def fill(first, last):
            for k in range(first, last):
                window[:, k] = zero

        fill(0, pad - reach)
        fill(pad + tile_rows + reach, 2 * pad + tile_rows)

        @pl.when(self.row == 0)
        def _():
            fill(pad - reach, pad)

        @pl.when(self.row == self.rows - 1)
        def _():
            fill(pad + tile_rows, pad + tile_rows + reach)

    def start(self):
        @pl.when(self.row > 0)
        def _():
            self.up.start()

        @pl.when(self.row < self.rows - 1)
        def _():
            self.down.start()

        self.to_pair.start()
        for n in range(self.tile.shape[0]):
            self.window[n, pl.ds(self.pad, self.tile_rows), self.own, :] = self.tile[n]

    def middle(self):
        @pl.when(self.row < self.rows - 1)
        def _():
            self.up.wait_recv()
            self.from_below.start()

        @pl.when(self.row > 0)
        def _():
            self.down.wait_recv()
            self.from_above.start()

    def finish(self):
        self.to_pair.wait()

        @pl.when(self.row < self.rows - 1)
        def _():
            self.down.wait_send()
            self.from_below.wait()

        @pl.when(self.row > 0)
        def _():
            self.up.wait_send()
            self.from_above.wait()


def gauss(x):
    bell = jnp.exp(-0.5 * x * x)
    t = 1.0 / (1.0 + (0.3275911 * 0.7071067811865476) * jnp.abs(x))
    poly = 1.061405429 * t - 1.453152027
    poly = poly * t + 1.421413741
    poly = poly * t - 0.284496736
    poly = poly * t + 0.254829592
    tail = 0.5 * poly * t * bell
    return jnp.where(x < 0, tail, 1.0 - tail), bell * 0.3989422804014327


def wide(mask, width):
    return jnp.concatenate([mask] * (width // 128), axis=1)


def place(ref, i, lanes):
    if len(ref.shape) == 4:
        return (i // ref.shape[1], lax.rem(i, ref.shape[1]), slice(None), lanes)
    return (pl.ds(pl.multiple_of(i * STEP, STEP), STEP), lanes)


def by_rows(pixels, width, work, sums=0):
    pieces = [slice(l, l + PIECE) for l in range(0, width, PIECE)]

    def one(i, carry):
        out = []
        for k, lanes in enumerate(pieces):
            got = work(i, lanes)
            for j in range(sums):
                folded = jnp.sum(got[j].reshape(STEP // 8, 8, PIECE), axis=0)
                out.append(carry[k * sums + j] + folded)
        return tuple(out)

    start = tuple(jnp.zeros((8, PIECE), F32) for _ in range(sums * len(pieces)))
    final = lax.fori_loop(0, pixels // STEP, one, start)
    rows = []
    for j in range(sums):
        parts = [jnp.sum(final[k * sums + j], axis=0, keepdims=True) for k in range(len(pieces))]
        rows.append(jnp.concatenate(parts, axis=1))
    return rows


NORM_ROWS = 8


def norm_table(exchange, gain_ref, shift_ref, out_ref):
    mean, var = exchange.rows()
    inv = lax.rsqrt(var + EPSILON)
    out_ref[...] = jnp.zeros_like(out_ref)
    out_ref[0:1, :] = mean
    out_ref[1:2, :] = inv
    out_ref[2:3, :] = inv * gain_ref[...]
    out_ref[3:4, :] = shift_ref[...]
    out_ref[4:5, :] = var


def normed(u_ref, norm, i, lanes):
    away = u_ref[place(u_ref, i, lanes)].astype(F32) - norm[0:1, lanes]
    return away * norm[2:3, lanes] + norm[3:4, lanes], away


def activate(u_ref, norm, mask, h_ref, residual=None, slope=None, keep=None):
    def work(i, lanes):
        x, _ = normed(u_ref, norm, i, lanes)
        if residual is not None:
            x = x + residual[place(residual, i, lanes)].astype(F32)
        below, bell = gauss(x)
        m = wide(mask[place(mask, i, slice(None))], PIECE)
        h_ref[place(h_ref, i, lanes)] = (x * below * m).astype(BF16)
        if slope is not None:
            slope[place(slope, i, lanes)] = ((below + x * bell) * m).astype(BF16)
        if keep is not None:
            keep[place(keep, i, lanes)] = u_ref[place(u_ref, i, lanes)].astype(BF16)

    by_rows(mask.shape[0], norm.shape[1], work)


def device_stats(u_ref, mask, count):
    pixels, width = u_ref.shape

    def total_of(i, lanes):
        m = wide(mask[place(mask, i, slice(None))], PIECE)
        return (u_ref[place(u_ref, i, lanes)] * m,)

    (total,) = by_rows(pixels, width, total_of, 1)
    center = total / jnp.maximum(wide(count, width), 1.0)

    def spread_of(i, lanes):
        m = wide(mask[place(mask, i, slice(None))], PIECE)
        away = u_ref[place(u_ref, i, lanes)] - center[:, lanes]
        return (away * away * m,)

    (spread,) = by_rows(pixels, width, spread_of, 1)
    return total, spread


def product(a_ref, w_ref, o_ref, turned=False):
    dims = (((1,), (1 if turned else 0,)), ((), ()))

    def one(i, carry):
        rows = pl.ds(pl.multiple_of(i * CHUNK, CHUNK), CHUNK)
        o_ref[rows, :] = lax.dot_general(
            a_ref[rows, :], w_ref[...], dims, preferred_element_type=F32
        )
        return carry

    lax.fori_loop(0, a_ref.shape[0] // CHUNK, one, 0)


def turn(a_ref, t_ref):
    def one(i, carry):
        rows = pl.ds(pl.multiple_of(i * CHUNK, CHUNK), CHUNK)
        t_ref[:, rows] = a_ref[rows, :].T
        return carry

    lax.fori_loop(0, a_ref.shape[0] // CHUNK, one, 0)


def put_lanes(ref, first, value):
    width = ref.shape[-1]
    at, stop = first, first + value.shape[1]
    while at < stop:
        cut = at // width
        until = min(stop, (cut + 1) * width)
        part = value[:, at - first : until - first].astype(ref.dtype)
        lanes = slice(at - cut * width, until - cut * width)
        if len(ref.shape) == 4:
            ref[cut, :, :, lanes] = part.reshape(ref.shape[1:3] + part.shape[1:])
        else:
            ref[cut, :, lanes] = part
        at = until


def weight_product(t_ref, b_ref, gw_ref):
    channels = b_ref.shape[1]
    for first in range(0, channels, 512):
        value = jnp.dot(t_ref[...], b_ref[:, first : first + 512], preferred_element_type=F32)
        put_lanes(gw_ref, first, value)


def norm_back(e_ref, u_ref, norm, sums, pixel_count, mask, out_ref):
    sum_grad, sum_unit = (s * (1.0 / pixel_count) for s in sums)

    def work(i, lanes):
        away = u_ref[place(u_ref, i, lanes)].astype(F32) - norm[0:1, lanes]
        unit = away * norm[1:2, lanes]
        e = e_ref[place(e_ref, i, lanes)].astype(F32)
        m = wide(mask[place(mask, i, slice(None))], PIECE)
        grad = norm[2:3, lanes] * (e - sum_grad[:, lanes] - unit * sum_unit[:, lanes]) * m
        out_ref[place(out_ref, i, lanes)] = grad.astype(BF16)

    by_rows(mask.shape[0], norm.shape[1], work)


def gelu_grad(e_ref, u_ref, norm, mask):
    def work(i, lanes):
        x, away = normed(u_ref, norm, i, lanes)
        below, bell = gauss(x)
        m = wide(mask[place(mask, i, slice(None))], PIECE)
        e = e_ref[place(e_ref, i, lanes)] * (below + x * bell) * m
        e_ref[place(e_ref, i, lanes)] = e
        return e, e * (away * norm[1:2, lanes])

    return by_rows(mask.shape[0], norm.shape[1], work, 2)


def put_sums(exchange, out_ref):
    first, second = exchange.rows()
    out_ref[...] = jnp.zeros_like(out_ref)
    out_ref[0:1, :] = first
    out_ref[1:2, :] = second
    return first, second


def forward_a(plane_count, r):
    signal_all()
    ex3, ex1 = Exchange(r.ex3), Exchange(r.ex1)
    halo = Halo(2, 2, r.tile, r.rim_b, r.halo)
    halo.blank()
    r.ready(r.u_a2)
    activate(r.u_a2, r.norm_a2, r.mask, r.h2_a)
    r.push(r.h2_a)
    r.ready(r.w_expand)
    product(r.h2_a, r.w_expand, r.wide)
    count = r.counts[8:9, :]
    total, spread = device_stats(r.wide, r.mask, count)
    wait_all()
    ex3.put(total, spread)
    r.ready(r.feature, r.w_reduce)
    ex3.middle_stats(r.counts, plane_count)
    ex3.finish_stats(plane_count)
    norm_table(ex3, r.gain_a3, r.shift_a3, r.norm_a3)
    activate(r.wide, r.norm_a3, r.mask, r.middle, r.feature, r.slope_a, r.u_a3)
    r.push(r.middle, r.slope_a, r.u_a3)
    product(r.middle, r.w_reduce, r.u_b1)
    r.push(r.u_b1)
    total, spread = device_stats(r.u_b1, r.mask, count)
    ex1.put(total, spread)
    ex1.middle_stats(r.counts, plane_count)
    ex1.finish_stats(plane_count)
    norm_table(ex1, r.gain_b1, r.shift_b1, r.norm_b1)
    activate(r.u_b1, r.norm_b1, r.mask, r.tile)
    halo.start()
    halo.middle()
    halo.finish()
    r.push(r.rim_b)


def forward_b(plane_count, r):
    signal_all()
    ex2, ex3, ex4 = Exchange(r.ex2), Exchange(r.ex3), Exchange(r.ex4)
    count = r.counts[8:9, :]
    r.ready(r.rim_b)
    build_shifted(r.rim_b, r.shifted)
    r.ready(r.w_conv)
    conv_product(r.shifted, r.w_conv, r.u_b2)
    r.push(r.u_b2)
    total, spread = device_stats(r.u_b2, r.mask, count)
    wait_all()
    ex2.put(total, spread)
    ex2.middle_stats(r.counts, plane_count)
    ex2.finish_stats(plane_count)
    norm_table(ex2, r.gain_b2, r.shift_b2, r.norm_b2)
    activate(r.u_b2, r.norm_b2, r.mask, r.h2_b)
    r.push(r.h2_b)
    r.ready(r.w_expand)
    product(r.h2_b, r.w_expand, r.wide)
    total, spread = device_stats(r.wide, r.mask, count)
    ex3.put(total, spread)
    r.ready(r.middle, r.cotangent)
    ex3.middle_stats(r.counts, plane_count)
    ex3.finish_stats(plane_count)
    norm = r.norm_b3
    norm_table(ex3, r.gain_b3, r.shift_b3, norm)

    def work(i, lanes):
        x, away = normed(r.wide, norm, i, lanes)
        at = place(r.wide, i, lanes)
        r.u_b3[at] = r.wide[at].astype(BF16)
        x = x + r.middle[at].astype(F32)
        below, bell = gauss(x)
        m = wide(r.mask[place(r.mask, i, slice(None))], PIECE)
        r.feature_out[at] = (x * below * m).astype(BF16)
        e = (below + x * bell) * r.cotangent[at].astype(F32) * m
        r.e_b3[at] = e.astype(BF16)
        return e, e * (away * norm[1:2, lanes])

    sums = by_rows(r.wide.shape[0], r.wide.shape[1], work, 2)
    ex4.put(*sums)
    r.push(r.feature_out, r.e_b3, r.u_b3)
    ex4.middle_sums()
    ex4.finish_sums()
    put_sums(ex4, r.sums_b3)


def backward_b(pixel_count, r):
    signal_all()
    ex2, ex1 = Exchange(r.ex2), Exchange(r.ex1)
    halo = Halo(2, 2, r.tile, r.back_rim, r.halo)
    halo.blank()
    r.ready(r.e_b3, r.u_b3)
    sums = (r.sums_b3[0:1, :], r.sums_b3[1:2, :])
    norm_back(r.e_b3, r.u_b3, r.norm_b3, sums, pixel_count, r.mask, r.geo)
    r.ready(r.w_expand)
    product(r.geo, r.w_expand, r.grad, turned=True)
    r.ready(r.u_b2)
    sums = gelu_grad(r.grad, r.u_b2, r.norm_b2, r.mask)
    wait_all()
    ex2.put(*sums)
    r.ready(r.h2_b)
    turn(r.h2_b, r.turned)
    ex2.middle_sums()
    weight_product(r.turned, r.geo, r.gw_expand)
    r.push(r.gw_expand)
    ex2.finish_sums()
    sums = put_sums(ex2, r.sums_b2)
    norm_back(r.grad, r.u_b2, r.norm_b2, sums, pixel_count, r.mask, r.tile)
    halo.start()
    tile_rows, tile_cols, width = r.tile.shape[1:]
    pixels = tile_rows * tile_cols
    for n in range(r.tile.shape[0]):
        for k in range(0, tile_rows, 8):
            at = n * pixels + k * tile_cols
            block = r.tile[n, k : k + 8].reshape(8 * tile_cols, width)
            r.turned[:, at : at + 8 * tile_cols] = block.T
    r.ready(r.rim_b)
    build_shifted(r.rim_b, r.shifted)
    conv_weight_product(r.turned, r.shifted, r.gw_conv, 0)
    halo.middle()
    conv_weight_product(r.turned, r.shifted, r.gw_conv, 1)
    halo.finish()
    build_shifted(r.back_rim, r.back_shifted)
    r.ready(r.w_conv)
    unconv_product(r.back_shifted, r.w_conv, r.grad)
    r.ready(r.u_b1)
    sums = gelu_grad(r.grad, r.u_b1, r.norm_b1, r.mask)
    ex1.put(*sums)
    ex1.middle_sums()
    conv_weight_product(r.turned, r.shifted, r.gw_conv, 2)
    r.push(r.gw_conv)
    ex1.finish_sums()
    sums = put_sums(ex1, r.sums_b1)
    norm_back(r.grad, r.u_b1, r.norm_b1, sums, pixel_count, r.mask, r.gro_b)


def backward_a(pixel_count, direct, r):
    signal_all()
    ex3, ex2 = Exchange(r.ex3), Exchange(r.ex2)
    jobs = Jobs()
    wait_all()
    if direct:
        r.ready(r.src_conv_b, r.src_expand_b)
        jobs.add(
            *plane_jobs(r.src_conv_b, r.eighth_conv_b, r.plane_conv_b),
            *plane_jobs(r.src_expand_b, r.eighth_expand_b, r.plane_expand_b),
        )
    jobs.tick(4)
    r.ready(r.gro_b, r.w_reduce)
    product(r.gro_b, r.w_reduce, r.wide, turned=True)
    r.ready(r.e_b3, r.slope_a, r.u_a3)
    norm = r.norm_a3

    def work(i, lanes):
        at = place(r.wide, i, lanes)
        e = (r.wide[at] + r.e_b3[at].astype(F32)) * r.slope_a[at].astype(F32)
        r.e_a3[at] = e.astype(BF16)
        away = r.u_a3[at].astype(F32) - norm[0:1, lanes]
        return e, e * (away * norm[1:2, lanes])

    sums = by_rows(r.wide.shape[0], r.wide.shape[1], work, 2)
    ex3.put(*sums)
    jobs.tick(4)
    r.push(r.e_a3)
    turn(r.gro_b, r.turned)
    ex3.middle_sums()
    r.ready(r.middle)
    weight_product(r.turned, r.middle, r.gw_reduce)
    r.push(r.gw_reduce)
    ex3.finish_sums()
    sums = put_sums(ex3, r.sums_a3)
    norm_back(r.e_a3, r.u_a3, norm, sums, pixel_count, r.mask, r.e_b3)
    r.ready(r.w_expand)
    product(r.e_b3, r.w_expand, r.grad, turned=True)
    r.ready(r.u_a2)
    sums = gelu_grad(r.grad, r.u_a2, r.norm_a2, r.mask)
    ex2.put(*sums)
    r.ready(r.h2_a)
    turn(r.h2_a, r.turned)
    ex2.middle_sums()
    weight_product(r.turned, r.e_b3, r.gw_expand)
    r.push(r.gw_expand)
    jobs.tick(4)
    ex2.finish_sums()
    sums = put_sums(ex2, r.sums_a2)
    norm_back(r.grad, r.u_a2, r.norm_a2, sums, pixel_count, r.mask, r.gd)
    jobs.finish()
    if direct:
        r.push(r.eighth_conv_b, r.eighth_expand_b)


def unsample(r, plan):
    width = r.rim.shape[2]
    cols = r.table.shape[0] // WINDOW
    pixels = r.up.shape[2] // 2
    r.spill[...] = jnp.zeros_like(r.spill)
    r.grad_row[...] = jnp.zeros_like(r.grad_row)
    r.grad_col[...] = jnp.zeros_like(r.grad_col)

    def unit(step, carry):
        n, block = step // 2, lax.rem(step, 2)
        lanes = pl.ds(pl.multiple_of(block * pixels, pixels), pixels)
        base = block * (BLOCK_ROWS * cols)
        grad_in = r.turned[:, pl.ds(pl.multiple_of(step * pixels, pixels), pixels)]
        for group in range(3):
            first, start, stop = tap_span(group, cols)
            cells = pl.ds(pl.multiple_of(base + start, 128), stop - start)
            for j in range(3):
                tap = 3 * group + j
                spot = slice(j * pixels, (j + 1) * pixels)
                row_w, row_s, col_w, col_s = tap_weights(
                    tap, block, cols, r.up, r.left, r.fr, r.fc, n, lanes
                )
                write_table(r.table, j * pixels, row_w, col_w, group, cols)
                grad = jnp.dot(
                    r.w_deform[tap * width : (tap + 1) * width, :],
                    grad_in,
                    preferred_element_type=F32,
                ).astype(BF16)
                r.grads[:, spot] = grad
                scores = jnp.dot(r.rim[n, cells, :], grad, preferred_element_type=F32)
                by_value = jnp.zeros((cols, pixels), F32)
                by_slope = jnp.zeros((cols, pixels), F32)
                for k in range(first, first + SPAN):
                    line = scores[k * cols - start : (k + 1) * cols - start]
                    by_value = by_value + line * row_w[k : k + 1, :]
                    by_slope = by_slope + line * row_s[k : k + 1, :]
                r.grad_row[n, tap : tap + 1, lanes] = jnp.sum(
                    by_slope * col_w, axis=0, keepdims=True
                )
                r.grad_col[n, tap : tap + 1, lanes] = jnp.sum(
                    by_value * col_s, axis=0, keepdims=True
                )
            r.spill[n, cells, :] += lax.dot_general(
                r.table[start:stop, :],
                r.grads[...],
                (((1,), (1,)), ((), ())),
                preferred_element_type=F32,
            )
            for turn_at in range(4):
                if 3 * turn_at + group in plan:

                    @pl.when(step == turn_at)
                    def _(slot=3 * turn_at + group):
                        plan[slot]()

        return carry

    lax.fori_loop(0, 4, unit, 0)


def select_cells(r, cols):
    off = HALF * lax.axis_index(COL)
    cells = r.select.shape[1]

    def fill(i, carry):
        ids = lax.broadcasted_iota(jnp.int32, (STEP, cells), 1)
        pixel = lax.broadcasted_iota(jnp.int32, (STEP, cells), 0)
        hit = ids == pixel + (i + PAD) * cols + off
        r.select[pl.ds(pl.multiple_of(i * STEP, STEP), STEP), :] = jnp.where(hit, 1.0, 0.0).astype(
            BF16
        )
        return carry

    lax.fori_loop(0, r.select.shape[0] // STEP, fill, 0)


def unoffset(r):
    images, cells, width = r.rim.shape
    cols = r.table.shape[0] // WINDOW
    select_cells(r, cols)
    column = lax.rem(lax.broadcasted_iota(jnp.int32, (32, cells), 1), cols)
    for n in range(images):
        parts = []
        for grad, frac in ((r.grad_row, r.fr), (r.grad_col, r.fc)):
            f = frac[n]
            parts.append(grad[n] * f * (1.0 - f))
        go = jnp.concatenate(parts, axis=0).astype(BF16)
        on_tile = jnp.dot(go, r.select[...], preferred_element_type=F32)
        for tap in range(9):
            i, j = 2 * (tap // 3 - 1), 2 * (tap % 3 - 1)
            kept = on_tile
            if j < 0:
                kept = jnp.where(column >= -j, on_tile, 0.0)
            if j > 0:
                kept = jnp.where(column < cols - j, on_tile, 0.0)
            shift = (i * cols + j) % cells
            if shift:
                kept = pltpu.roll(kept, shift, axis=1)
            r.on_cells[32 * tap : 32 * tap + 32, :] = kept.astype(BF16)
        grad = jnp.dot(r.on_cells[...], r.rim[n], preferred_element_type=F32)
        if n == 0:
            r.gw_off_sum[...] = grad
        else:
            r.gw_off_sum[...] += grad
        for first in range(0, cells, 512):
            r.spill[n, first : first + 512, :] += lax.dot_general(
                r.on_cells[:, first : first + 512],
                r.w_off[...],
                (((0,), (0,)), ((), ())),
                preferred_element_type=F32,
            )
    for tap in range(9):
        put_lanes(r.gw_off, tap * width, r.gw_off_sum[32 * tap : 32 * tap + 32, :])


class Spill:
    @staticmethod
    def scratch(images, tile_rows, tile_cols, width):
        side = pltpu.VMEM((images, tile_rows + 2 * PAD, HALF, width), BF16)
        strip = pltpu.VMEM((images, REACH, tile_cols, width), BF16)
        sems = pltpu.SemaphoreType.DMA((3,))
        return [side, side, strip, strip, strip, strip, sems, sems]

    def __init__(self, spill, grad, cols, refs):
        self.spill, self.grad, self.cols = spill, grad, cols
        self.side_out, self.side_in, self.up_out, self.down_out, self.up_in, self.down_in = refs[:6]
        send, recv = refs[6:]
        self.row, self.rows, col, pair, above, below = halo_peers()
        self.images, self.all_rows = self.side_out.shape[:2]
        self.tile_rows, self.tile_cols = self.all_rows - 2 * PAD, self.up_out.shape[2]
        self.off, self.away, self.near = HALF * col, 2 * HALF * (1 - col), HALF * (1 - col)
        self.side = remote(self.side_out, self.side_in, send.at[0], recv.at[0], pair)
        self.up = remote(self.up_out, self.down_in, send.at[1], recv.at[1], above)
        self.down = remote(self.down_out, self.up_in, send.at[2], recv.at[2], below)

    def cells(self, k, first, count):
        return pl.ds(pl.multiple_of(k * self.cols + first, HALF), count)

    def start(self):
        def cast(k, carry):
            for n in range(self.images):
                self.side_out[n, k] = self.spill[n, self.cells(k, self.away, HALF), :].astype(BF16)
            return carry

        lax.fori_loop(0, self.all_rows, cast, 0)
        self.side.start()

    def edge(self, buffer, first):
        near = pl.ds(pl.multiple_of(self.near, HALF), HALF)

        def one(k, carry):
            for n in range(self.images):
                at = first + k
                buffer[n, k] = self.spill[n, self.cells(at, self.off, self.tile_cols), :].astype(BF16)
                part = self.spill[n, self.cells(at, HALF, HALF), :]
                buffer[n, k, near, :] = (part + self.side_in[n, at].astype(F32)).astype(BF16)
            return carry

        lax.fori_loop(0, REACH, one, 0)

    def middle(self):
        self.side.wait_recv()

        @pl.when(self.row > 0)
        def _():
            self.edge(self.up_out, PAD - REACH)
            self.up.start()

        @pl.when(self.row < self.rows - 1)
        def _():
            self.edge(self.down_out, PAD + self.tile_rows)
            self.down.start()

    def pixels(self, n, k, first, count):
        at = (n * self.tile_rows + k) * self.tile_cols + first
        return pl.ds(pl.multiple_of(at, HALF), count)

    def own(self):
        def fill(k, carry):
            for n in range(self.images):
                home = self.spill[n, self.cells(PAD + k, self.off, self.tile_cols), :]
                self.grad[self.pixels(n, k, 0, self.tile_cols), :] = home
                self.grad[self.pixels(n, k, self.near, HALF), :] += self.side_in[n, PAD + k].astype(F32)
            return carry

        lax.fori_loop(0, self.tile_rows, fill, 0)

    def finish(self):
        def arrive(buffer, first):
            def one(k, carry):
                for n in range(self.images):
                    at = self.pixels(n, first + k, 0, self.tile_cols)
                    self.grad[at, :] += buffer[n, k].astype(F32)
                return carry

            lax.fori_loop(0, REACH, one, 0)

        @pl.when(self.row > 0)
        def _():
            self.down.wait_recv()
            arrive(self.up_in, 0)
            self.up.wait_send()

        @pl.when(self.row < self.rows - 1)
        def _():
            self.up.wait_recv()
            arrive(self.down_in, self.tile_rows - REACH)
            self.down.wait_send()

        self.side.wait_send()


def backward_s(pixel_count, direct, r):
    signal_all()
    ex = Exchange(r.ex1)
    cols = r.table.shape[0] // WINDOW
    spill = Spill(r.spill, r.grad, cols, r.strips)
    wait_all()

    def nothing():
        pass

    first_jobs, second, third, plan = Jobs(), Jobs(), Jobs(), {}
    if direct:
        lines = Jobs()
        lines.add(
            *line_jobs(r.eighth_conv_b, r.sum_conv_b, r.line_conv_b),
            *line_jobs(r.eighth_expand_b, r.sum_expand_b, r.line_expand_b),
        )
        planes = Jobs()
        planes.add(
            *plane_jobs(r.src_reduce_b, r.eighth_reduce_b, r.plane_reduce_b),
            *plane_jobs(r.src_expand_a, r.eighth_expand_a, r.plane_expand_a),
        )
        deform = Jobs()
        deform.add(*plane_jobs(r.src_deform, r.eighth_deform, r.plane_deform))
        later = Jobs()
        later.add(
            *line_jobs(r.eighth_reduce_b, r.sum_reduce_b, r.line_reduce_b),
            *line_jobs(r.eighth_expand_a, r.sum_expand_a, r.line_expand_a),
        )
        r.ready(r.src_reduce_b, r.src_expand_a)
        planes.tick(4)
        r.ready(r.eighth_conv_b, r.eighth_expand_b)
        lines.tick(4)
        r.ready(r.src_deform)
        deform.tick(2)
        q1, q2, q3, q4 = planes.queue, lines.queue, deform.queue, later.queue
        slots = {
            2: q1[0:4],
            4: q3[0:2],
            7: q1[4:8] + q2[0:4],
            10: q1[8:12] + q4[0:4],
            11: q3[2:4] + q2[4:8],
        }

        def run(queue):
            def call():
                for step in queue:
                    step()

            return call

        plan = {slot: run(queue) for slot, queue in slots.items()}
        first_jobs.queue = q2[8:12]
        second.queue = q4[4:8]
        third.queue = q3[4:6] + q4[8:16]
    r.ready(r.gd, r.rim, r.w_deform)
    turn(r.gd, r.turned)
    unsample(r, plan)
    r.ready(r.w_off)
    unoffset(r)
    spill.start()
    r.push(r.gw_off)
    first_jobs.finish()
    spill.middle()
    spill.own()
    second.finish()
    r.ready(r.u_a1)
    spill.finish()
    sums = gelu_grad(r.grad, r.u_a1, r.norm_a1, r.mask)
    ex.put(*sums)
    third.tick(6)
    ex.middle_sums()
    ex.finish_sums()
    sums = put_sums(ex, r.sums_a1)
    norm_back(r.grad, r.u_a1, r.norm_a1, sums, pixel_count, r.mask, r.gr_a)
    third.finish()
    if direct:
        r.push(r.sum_conv_b, r.sum_expand_b, r.sum_reduce_b, r.sum_expand_a, r.eighth_deform)


def last(direct, r):
    signal_all()
    wait_all()
    jobs, plane = Jobs(), Jobs()
    if direct:
        r.ready(r.eighth_deform, r.gw_off)
        small = SmallSum(r.gw_off, r.sum_off, r.small)
        jobs.add(*line_jobs(r.eighth_deform, r.sum_deform, r.line_deform), small)
        jobs.tick(3)
    r.ready(r.gr_a, r.feature)
    turn(r.gr_a, r.turned)
    weight_product(r.turned, r.feature, r.gw_reduce)
    if direct:
        plane.add(*plane_jobs(r.gw_reduce, r.eighth_reduce_a, r.plane_reduce_a))
        plane.add(*line_jobs(r.eighth_reduce_a, r.sum_reduce_a, r.line_reduce_a))
    else:
        r.push(r.gw_reduce)
    plane.tick(2)
    r.ready(r.w_reduce, r.e_a3)

    def chunk(i, carry):
        rows = pl.ds(pl.multiple_of(i * CHUNK, CHUNK), CHUNK)
        for first in range(0, r.feature.shape[1], 512):
            lanes = slice(first, first + 512)
            grad = lax.dot_general(
                r.gr_a[rows, :],
                r.w_reduce[lanes, :],
                (((1,), (1,)), ((), ())),
                preferred_element_type=F32,
            )
            r.grad_in[rows, lanes] = (grad + r.e_a3[rows, lanes].astype(F32)).astype(BF16)
        return carry

    half = r.feature.shape[0] // CHUNK // 2
    lax.fori_loop(0, half, chunk, 0)
    plane.tick(2)
    lax.fori_loop(half, 2 * half, chunk, 0)
    r.push(r.grad_in)
    jobs.tick(3)
    plane.tick(2)
    jobs.tick(3)
    plane.tick(4)
    jobs.finish()
    plane.finish()
    if direct:
        r.push(r.sum_deform, r.sum_reduce_a)


def local_stats(values, weight_col, count):
    total = jnp.sum(values * weight_col, axis=0)
    away = values - total / jnp.maximum(count, 1.0)
    return total, jnp.sum(away * away * weight_col, axis=0)


def norm_forward(pre_norm, weight_col, norm_gain, norm_shift, counts):
    own_count, all_counts, plane_count = counts
    total, spread = local_stats(pre_norm, weight_col, own_count)
    batch_mean, spread = stats_over_devices(total, spread, all_counts, plane_count)
    inv_std = lax.rsqrt(spread + EPSILON)
    unit_value = (pre_norm - batch_mean) * inv_std
    return (unit_value * norm_gain + norm_shift, unit_value, inv_std, batch_mean, spread)


def inside_counts(orientation, tile_rows, tile_cols):
    rows, cols = lax.axis_size(ROW), lax.axis_size(COL)
    tall = np.clip(SHORT - np.arange(rows) * tile_rows, 0, tile_rows)[:, None] * tile_cols
    wide = np.clip(SHORT - np.arange(cols) * tile_cols, 0, tile_cols)[None, :] * tile_rows
    tall = jnp.asarray(np.broadcast_to(tall, (rows, cols)).reshape(-1), F32)
    wide = jnp.asarray(np.broadcast_to(wide, (rows, cols)).reshape(-1), F32)
    flat = (orientation == 0).astype(F32)[:, None]
    each = jnp.sum(flat * tall + (1.0 - flat) * wide, axis=0)
    place = lax.axis_index(ROW) * cols + lax.axis_index(COL)
    own = lax.dynamic_index_in_dim(each, place, keepdims=False)
    return own, jnp.broadcast_to(each[:, None], (rows * cols, 128))


def body(
    feature_in,
    orientation,
    offset_base,
    w_reduce_a,
    w_offset_a,
    w_deform_a,
    w_expand_a,
    scale_a,
    shift_a,
    w_reduce_b,
    w_conv_b,
    w_expand_b,
    scale_b,
    shift_b,
    cotangent,
):
    images, tile_rows, tile_cols, channels = feature_in.shape
    inner_width = w_reduce_a.shape[1]
    second_cut = 2 * inner_width
    tile_pixels = tile_rows * tile_cols
    win_cols = tile_cols + HALF
    win_rows = tile_rows + 2 * PAD
    plane_count = 1.0 * images * LONG * SHORT
    pixel_count = plane_count * lax.axis_size(IMG)
    unbias = pixel_count / (pixel_count - 1.0)
    col_at = lax.axis_index(COL)
    row_ids = lax.axis_index(ROW) * tile_rows + jnp.arange(tile_rows, dtype=jnp.int32)
    col_ids = col_at * tile_cols + jnp.arange(tile_cols, dtype=jnp.int32)
    landscape = jnp.broadcast_to((row_ids < SHORT)[:, None], (tile_rows, tile_cols))
    portrait = jnp.broadcast_to((col_ids < SHORT)[None, :], (tile_rows, tile_cols))
    inside = jnp.where(orientation[:, None, None] == 0, landscape[None], portrait[None]).astype(F32)
    weight_col = inside.reshape(-1, 1)
    pixels = weight_col.shape[0]
    own_count, all_counts = inside_counts(orientation, tile_rows, tile_cols)
    counts = (own_count, all_counts, plane_count)
    block_in = (
        (feature_in.astype(F32) * inside[..., None]).astype(BF16).reshape(pixels, channels)
    )
    reduced_a = jnp.dot(block_in, w_reduce_a, preferred_element_type=F32)
    normed_a1, unit_a1, inv_a1, mean_a1, spread_a1 = norm_forward(
        reduced_a, weight_col, scale_a[:inner_width], shift_a[:inner_width], counts
    )
    hidden_a = (gelu_exact(normed_a1) * weight_col).astype(BF16)
    rim_a = with_halo(
        hidden_a.reshape(images, tile_rows, tile_cols, inner_width), PAD, REACH
    )
    rim_flat = rim_a.reshape(images, -1, inner_width)
    own_at = HALF * col_at
    w_off = w_offset_a.reshape(9, inner_width, 18).transpose(1, 0, 2).reshape(inner_width, 162)
    spread_taps = jnp.dot(
        rim_flat.reshape(-1, inner_width), w_off, preferred_element_type=F32
    ).reshape(images, win_rows, win_cols, 162)
    spread_taps = jnp.pad(spread_taps, ((0, 0), (0, 0), (2, 2), (0, 0)))
    spread_taps = lax.dynamic_slice_in_dim(spread_taps, own_at, tile_cols + 4, axis=2)
    offsets = 0.0
    for tap in range(9):
        i, j = 2 * (tap // 3), 2 * (tap % 3)
        offsets = offsets + spread_taps[
            :, PAD - 2 + i : PAD - 2 + i + tile_rows, j : j + tile_cols, 18 * tap : 18 * tap + 18
        ]
    pad_taps = ((0, 0), (0, 16 - 9), (0, 0))
    fraction = jax.nn.sigmoid(offsets).reshape(images, tile_pixels, 18).transpose(0, 2, 1)
    frac_row, frac_col = (jnp.pad(fraction[:, k::2], pad_taps) for k in range(2))
    base = offset_base.reshape(images, tile_pixels, 18).transpose(0, 2, 1)
    cell = np.arange(tile_pixels)
    tap_row = np.array([2 * (tap // 3 - 1) for tap in range(9)])[:, None]
    tap_col = np.array([2 * (tap % 3 - 1) for tap in range(9)])[:, None]
    upper = base[:, 0::2] + jnp.asarray(cell // tile_cols + PAD + tap_row, jnp.int32)
    left = base[:, 1::2] + jnp.asarray(cell % tile_cols + tap_col, jnp.int32) + own_at
    upper, left = jnp.pad(upper, pad_taps), jnp.pad(left, pad_taps)
    samples, deformed = sample_forward(
        rim_flat.transpose(0, 2, 1), w_deform_a.T, upper, left, frac_row, frac_col, win_cols
    )
    deformed = deformed.T
    total, spread = local_stats(deformed, weight_col, own_count)
    mean_a2, spread_a2 = stats_over_devices(total, spread, all_counts, plane_count)
    one, two, three = slice(0, inner_width), slice(inner_width, second_cut), slice(second_cut, None)

    def norm_rows(mean, var, part):
        inv = lax.rsqrt(var + EPSILON)
        rows = jnp.stack([mean, inv, inv * scale_a[part], shift_a[part], var])
        return jnp.pad(rows, ((0, NORM_ROWS - 5), (0, 0)))

    norm_a1 = norm_rows(mean_a1, spread_a1, one)
    norm_a2 = norm_rows(mean_a2, spread_a2, two)
    mask = jnp.broadcast_to(weight_col, (pixels, 128))
    own_counts = jnp.broadcast_to(own_count, (8, 128))
    count_rows = jnp.concatenate([all_counts, own_counts], axis=0)

    def array(*shape, dtype=BF16):
        return jax.ShapeDtypeStruct(shape, dtype)

    def table(width):
        return array(NORM_ROWS, width, dtype=F32)

    small = (pixels, inner_width)
    big = (pixels, channels)
    window_b = (images, tile_rows + 4, win_cols, inner_width)
    shifted = pltpu.VMEM((images, tile_rows + 4, tile_cols, 3 * inner_width), BF16)
    tile = pltpu.VMEM((images, tile_rows, tile_cols, inner_width), BF16)
    turned = pltpu.VMEM((inner_width, pixels), BF16)
    images_axis = lax.axis_size(IMG)
    direct = inner_width % (images_axis * 8 * 16) == 0
    cuts = images_axis if direct else 1
    feature = feature_in.reshape(big)
    fwd_a = fused(
        functools.partial(forward_a, plane_count),
        FORWARD_A_CID,
        ins=dict(
            norm_a2=norm_a2,
            mask=mask,
            counts=count_rows,
            gain_a3=scale_a[None, three],
            shift_a3=shift_a[None, three],
            gain_b1=scale_b[None, one],
            shift_b1=shift_b[None, one],
        ),
        staged=dict(u_a2=deformed, w_expand=w_expand_a, feature=feature, w_reduce=w_reduce_b),
        outs=dict(norm_a3=table(channels), norm_b1=table(inner_width)),
        pushed=dict(
            h2_a=array(*small),
            middle=array(*big),
            slope_a=array(*big),
            u_a3=array(*big),
            u_b1=array(*small, dtype=F32),
            rim_b=array(*window_b),
        ),
        scratch=dict(
            ex3=Exchange.scratch(channels),
            ex1=Exchange.scratch(inner_width),
            halo=Halo.scratch,
            wide=pltpu.VMEM(big, F32),
            tile=tile,
        ),
    )
    fwd_b = fused(
        functools.partial(forward_b, plane_count),
        FORWARD_B_CID,
        ins=dict(
            mask=mask,
            counts=count_rows,
            gain_b2=scale_b[None, two],
            shift_b2=shift_b[None, two],
            gain_b3=scale_b[None, three],
            shift_b3=shift_b[None, three],
        ),
        staged=dict(
            rim_b=fwd_a.rim_b,
            w_conv=w_conv_b,
            w_expand=w_expand_b,
            middle=fwd_a.middle,
            cotangent=cotangent.reshape(big),
        ),
        outs=dict(norm_b2=table(inner_width), norm_b3=table(channels), sums_b3=table(channels)),
        pushed=dict(
            u_b2=array(*small, dtype=F32),
            h2_b=array(*small),
            u_b3=array(*big),
            feature_out=array(*big),
            e_b3=array(*big),
        ),
        scratch=dict(
            ex2=Exchange.scratch(inner_width),
            ex3=Exchange.scratch(channels),
            ex4=Exchange.scratch(channels),
            wide=pltpu.VMEM(big, F32),
            shifted=shifted,
        ),
    )
    bwd_b = fused(
        functools.partial(backward_b, pixel_count),
        BACKWARD_B_CID,
        ins=dict(
            mask=mask,
            norm_b3=fwd_b.norm_b3,
            sums_b3=fwd_b.sums_b3,
            norm_b2=fwd_b.norm_b2,
            norm_b1=fwd_a.norm_b1,
        ),
        staged=dict(
            e_b3=fwd_b.e_b3,
            u_b3=fwd_b.u_b3,
            w_expand=w_expand_b,
            u_b2=fwd_b.u_b2,
            h2_b=fwd_b.h2_b,
            rim_b=fwd_a.rim_b,
            w_conv=w_conv_b,
            u_b1=fwd_a.u_b1,
        ),
        outs=dict(gro_b=array(*small), sums_b2=table(inner_width), sums_b1=table(inner_width)),
        pushed=dict(
            gw_expand=array(1, inner_width, channels),
            gw_conv=array(cuts, inner_width, 9 * inner_width // cuts),
        ),
        scratch=dict(
            ex2=Exchange.scratch(inner_width),
            ex1=Exchange.scratch(inner_width),
            halo=Halo.scratch,
            geo=pltpu.VMEM(big, BF16),
            grad=pltpu.VMEM(small, F32),
            tile=tile,
            turned=turned,
            back_rim=pltpu.VMEM(window_b, BF16),
            shifted=shifted,
            back_shifted=shifted,
        ),
    )

    def eighths(grad):
        return grad.reshape(images_axis, 8, -1, grad.shape[-1])

    def eighth_of(src):
        return array(images_axis, *src.shape[2:])

    def sum_of(src):
        return array(*src.shape[1:])

    def vmem(struct):
        return pltpu.VMEM(struct.shape, struct.dtype)

    staged_a, pushed_a, scratch_a = {}, {}, {}
    if direct:
        conv_b, expand_b = eighths(bwd_b.gw_conv), eighths(bwd_b.gw_expand)
        staged_a = dict(src_conv_b=conv_b, src_expand_b=expand_b)
        pushed_a = dict(eighth_conv_b=eighth_of(conv_b), eighth_expand_b=eighth_of(expand_b))
        scratch_a = dict(
            plane_conv_b=Plane.scratch(conv_b.shape), plane_expand_b=Plane.scratch(expand_b.shape)
        )
    bwd_a = fused(
        functools.partial(backward_a, pixel_count, direct),
        BACKWARD_A_CID,
        ins=dict(mask=mask, norm_a3=fwd_a.norm_a3, norm_a2=norm_a2),
        staged=dict(
            **staged_a,
            gro_b=bwd_b.gro_b,
            w_reduce=w_reduce_b,
            e_b3=fwd_b.e_b3,
            slope_a=fwd_a.slope_a,
            u_a3=fwd_a.u_a3,
            middle=fwd_a.middle,
            w_expand=w_expand_a,
            u_a2=deformed,
            h2_a=fwd_a.h2_a,
        ),
        outs=dict(gd=array(*small), sums_a3=table(channels), sums_a2=table(inner_width)),
        pushed=dict(
            **pushed_a,
            gw_reduce=array(cuts, inner_width, channels // cuts),
            gw_expand=array(1, inner_width, channels),
            e_a3=array(*big),
        ),
        scratch=dict(
            **scratch_a,
            ex3=Exchange.scratch(channels),
            ex2=Exchange.scratch(inner_width),
            wide=pltpu.VMEM(big, F32),
            grad=pltpu.VMEM(small, F32),
            turned=turned,
        ),
    )
    feature_out = fwd_b.feature_out.reshape(feature_in.shape)
    gw_deform = jnp.dot(samples, bwd_a.gd, preferred_element_type=F32).astype(BF16)
    w_off_rows = w_offset_a.reshape(9, inner_width, 9, 2).transpose(0, 3, 2, 1)
    w_off_rows = jnp.pad(w_off_rows, ((0, 0), (0, 0), (0, 7), (0, 0))).reshape(288, inner_width)
    staged_s, pushed_s, scratch_s = {}, {}, {}
    if direct:
        reduce_b, expand_a = eighths(bwd_a.gw_reduce), eighths(bwd_a.gw_expand)
        deform = eighths(gw_deform)
        staged_s = dict(
            eighth_conv_b=bwd_a.eighth_conv_b,
            eighth_expand_b=bwd_a.eighth_expand_b,
            src_reduce_b=reduce_b,
            src_expand_a=expand_a,
            src_deform=deform,
        )
        pushed_s = dict(
            sum_conv_b=sum_of(conv_b),
            sum_expand_b=sum_of(expand_b),
            sum_reduce_b=sum_of(reduce_b),
            sum_expand_a=sum_of(expand_a),
            eighth_deform=eighth_of(deform),
        )
        scratch_s = dict(
            line_conv_b=Line.scratch(bwd_a.eighth_conv_b.shape),
            line_expand_b=Line.scratch(bwd_a.eighth_expand_b.shape),
            plane_reduce_b=Plane.scratch(reduce_b.shape),
            plane_expand_a=Plane.scratch(expand_a.shape),
            plane_deform=Plane.scratch(deform.shape),
            eighth_reduce_b=vmem(eighth_of(reduce_b)),
            eighth_expand_a=vmem(eighth_of(expand_a)),
            line_reduce_b=Line.scratch(eighth_of(reduce_b).shape),
            line_expand_a=Line.scratch(eighth_of(expand_a).shape),
        )
    cells = win_rows * win_cols
    taps_shape = (images, 16, tile_pixels)
    block = tile_pixels // 2
    bwd_s = fused(
        functools.partial(backward_s, pixel_count, direct),
        BACKWARD_S_CID,
        ins=dict(mask=mask, norm_a1=norm_a1, up=upper, left=left, fr=frac_row, fc=frac_col),
        staged=dict(
            **staged_s,
            gd=bwd_a.gd,
            rim=rim_flat,
            w_deform=w_deform_a,
            w_off=w_off_rows,
            u_a1=reduced_a,
        ),
        outs=dict(gr_a=array(*small), sums_a1=table(inner_width)),
        pushed=dict(**pushed_s, gw_off=array(cuts, 32, 9 * inner_width // cuts)),
        scratch=dict(
            **scratch_s,
            ex1=Exchange.scratch(inner_width),
            strips=Spill.scratch(images, tile_rows, tile_cols, inner_width),
            spill=pltpu.VMEM((images, cells, inner_width), F32),
            table=pltpu.VMEM((WINDOW * win_cols, 3 * block), BF16),
            grads=pltpu.VMEM((inner_width, 3 * block), BF16),
            turned=turned,
            grad_row=pltpu.VMEM(taps_shape, F32),
            grad_col=pltpu.VMEM(taps_shape, F32),
            select=pltpu.VMEM((tile_pixels, cells), BF16),
            on_cells=pltpu.VMEM((288, cells), BF16),
            gw_off_sum=pltpu.VMEM((288, inner_width), F32),
            grad=pltpu.VMEM(small, F32),
        ),
    )
    staged_l, pushed_l, scratch_l = {}, {}, {}
    if direct:
        reduce_a = array(images_axis, 8, inner_width // 8, channels // cuts)
        staged_l = dict(eighth_deform=bwd_s.eighth_deform, gw_off=bwd_s.gw_off)
        pushed_l = dict(sum_deform=sum_of(deform), sum_reduce_a=sum_of(reduce_a))
        scratch_l = dict(
            gw_reduce=vmem(reduce_a),
            small=SmallSum.scratch(bwd_s.gw_off.shape),
            line_deform=Line.scratch(bwd_s.eighth_deform.shape),
            plane_reduce_a=Plane.scratch(reduce_a.shape),
            eighth_reduce_a=vmem(eighth_of(reduce_a)),
            line_reduce_a=Line.scratch(eighth_of(reduce_a).shape),
        )
        outs_l = dict(sum_off=array(*bwd_s.gw_off.shape[1:], dtype=F32))
    else:
        pushed_l = dict(gw_reduce=array(cuts, inner_width, channels // cuts))
        outs_l = {}
    end = fused(
        functools.partial(last, direct),
        LAST_CID,
        ins={},
        staged=dict(
            **staged_l, gr_a=bwd_s.gr_a, feature=feature, w_reduce=w_reduce_a, e_a3=bwd_a.e_a3
        ),
        outs=outs_l,
        pushed=dict(**pushed_l, grad_in=array(*big)),
        scratch=dict(**scratch_l, turned=turned),
    )
    if direct:

        def rows_of(grad):
            return grad.reshape(-1, grad.shape[-1]).astype(F32)

        gw_expand_b, gw_expand_a = rows_of(bwd_s.sum_expand_b), rows_of(bwd_s.sum_expand_a)
        gw_conv_b, gw_reduce_b = rows_of(bwd_s.sum_conv_b).T, rows_of(bwd_s.sum_reduce_b).T
        gw_deform_a, gw_reduce_a = rows_of(end.sum_deform), rows_of(end.sum_reduce_a).T
        gw_off = end.sum_off
    else:

        def over_devices(grad, dim):
            part = lax.psum_scatter(grad, IMG, scatter_dimension=dim, tiled=True)
            return lax.psum(part, (ROW, COL)).astype(F32)

        gw_expand_b, gw_expand_a = (
            over_devices(g[0], 0) for g in (bwd_b.gw_expand, bwd_a.gw_expand)
        )
        gw_conv_b, gw_reduce_b, gw_reduce_a, gw_off_t = (
            over_devices(g[0], 1).T
            for g in (bwd_b.gw_conv, bwd_a.gw_reduce, end.gw_reduce, bwd_s.gw_off)
        )
        gw_deform_a = over_devices(gw_deform, 0)
        gw_off = gw_off_t.T
    gw_offset_a = gw_off.reshape(2, 16, -1)[:, :9].transpose(2, 1, 0).reshape(-1, 18)
    sums_a = [bwd_s.sums_a1, bwd_a.sums_a2, bwd_a.sums_a3]
    sums_b = [bwd_b.sums_b1, bwd_b.sums_b2, fwd_b.sums_b3]
    norms_a = [norm_a1, norm_a2, fwd_a.norm_a3]
    norms_b = [fwd_a.norm_b1, fwd_b.norm_b2, fwd_b.norm_b3]

    def join(tables, row):
        return jnp.concatenate([t[row] for t in tables])

    return (
        feature_out,
        end.grad_in.reshape(feature_in.shape),
        gw_reduce_a,
        gw_offset_a,
        gw_deform_a,
        gw_expand_a,
        join(sums_a, 1),
        join(sums_a, 0),
        join(norms_a, 0),
        join(norms_a, 4) * unbias,
        gw_reduce_b,
        gw_conv_b,
        gw_expand_b,
        join(sums_b, 1),
        join(sums_b, 0),
        join(norms_b, 0),
        join(norms_b, 4) * unbias,
    )


def solution(mesh):
    tiles = P(IMG, ROW, COL, None)
    in_specs = (tiles, P(IMG), tiles) + (P(),) * 11 + (tiles,)
    shares = P(IMG, None)
    out_specs = (tiles, tiles) + (shares,) * 4 + (P(),) * 4 + (shares,) * 3 + (P(),) * 4
    return jax.shard_map(body, mesh=mesh, in_specs=in_specs, out_specs=out_specs, check_vma=False)
```

time: 998 us -> 524 us (0.53)
  waiting for transfers between devices: 302 us -> 0 us
  other arithmetic: 166 us -> 31.1 us
  Pallas kernels: 289 us -> 417 us
  matrix products: 106 us -> 14.4 us
  local copies, waits for them, and re-layouts: 83.6 us -> 54.4 us
  blocking collectives: 25.9 us -> 0 us
  between operations: 16.1 us -> 1.9 us
    reduce_scatter x5 -> x0, waiting for transfers between devices: 223 us -> none  [over_devices(): lax.psum_scatter(grad.astype(BF16), 'img', scatter_dimension=dim, tiled=T...]
    pallas_call x16 -> x8, Pallas kernels: 229 us -> 377 us  [the longest x6 346 us: fused(): pl.pallas_call(kernel, out_shape=[*outs.values(), *pushed.values()], in_s...]
    dot_general x14 -> x1, matrix products: 97.7 us -> 9.39 us  [body(): jnp.dot(samples, bwd_a.gd, preferred_element_type=F32).astype(BF16)]
    convert_element_type x14 -> x2, other arithmetic: 89.6 us -> 3.44 us  [rows_of(): return grad.reshape(-1, grad.shape[-1]).astype(F32)]
    psum x1 -> x0, waiting for transfers between devices: 60.6 us -> none  [over_devices(): return lax.psum(part, ('row', 'col'))]
    reduce_sum x3 -> x0, other arithmetic: 35.5 us -> none  [norm_backward(): jnp.sum(grad_normed, axis=0)]
    psum x1 -> x0, blocking collectives: 25.9 us -> none  [over_devices(): return lax.psum(part, ('row', 'col'))]
    pallas_call x3 -> x1, Pallas kernels: 38.9 us -> 18.5 us  [with_halo(): pl.pallas_call(functools.partial(halo_kernel, pad, reach), out_shape=jax....]
  transfers between devices with their start and end apart: 8 -> 0, of which waited for: 6 -> 0; matrix products, arithmetic and copies ran while one was open for 15% -> 0% of each run, Pallas kernels for 11% -> 0%
where the time goes in v3:
time: 524 us; the launch traced here: 518 us
  Pallas kernels  417 us (80%)
  local copies, waits for them, and re-layouts  54.4 us (10%)
  other arithmetic  31.1 us (6%)
  matrix products  14.4 us (3%)
    pallas_call x6, Pallas kernels, fused(): pl.pallas_call(kernel, out_shape=[*outs.values(), *pushed.values()], in_s...  346 us
    pallas_call x2, Pallas kernels, stats_over_devices(): pl.pallas_call(functools.partial(stats_kernel, plane_count), out_shape=ja...  30.8 us
    pallas_call x1, Pallas kernels, sample_forward(): pl.pallas_call(sample_kernel, grid=(images, blocks), out_shape=(jax.Shape...  21.1 us
    pallas_call x1, Pallas kernels, with_halo(): pl.pallas_call(functools.partial(halo_kernel, pad, reach), out_shape=jax....  18.5 us
    unnamed x44, local copies, waits for them, and re-layouts  14.7 us

profile of v3, /device:TPU:0, one launch (start us, length us, event | category | flops | bytes accessed | tf_op | source)
XLA Modules:
  0.0 518.3 jit_solution(14295302090866071651)
XLA Ops:
  11.1 3.1 multiply_convert_fusion
  14.2 2.3 multiply_reduce_fusion.3
  19.5 12.7 %shard_map.314 = f32[8,128]{1,0:T(8,128)} custom-call(f32[8,128]{1,0:T(8,128)} %pad_maximum_fusion.6.x_ref, f32[8,128]{1,0:T(8,128)} %copy-done.13), custom_call_target="tpu_custom_call" | custom-call | tf_op jit(solution)/shard_map/pallas_call | solution.py:130
  34.9 6.3 %fusion.3 = bf16[1024,512]{1,0:T(8,128)(2,1)} fusion(f32[1024,512]{1,0:T(8,128)S(1)} %get-tuple-element.143.refs_15_, f32[512]{0:T(512)S(1)} %get-tuple-element.130, f32[512]{0:T(512)S(1)} %get-tuple-element.124, f32[512]{0:T(512)S(1)} %get-tuple-element.139, f32[512]{0:T(512)S(1)} %get-tuple-element.132, f32[1024]{0:T(1024)S(1)} %reshape.225), kind=kLoop, calls=%fused_computation.15 | loop fusion | flops 36700160 | bytes 3158016 | tf_op jit(solution)/shard_map/convert_element_type | solution.py:1664
  41.2 18.5 %shard_map.315 = bf16[2,32,48,512]{3,2,1,0:T(8,128)(2,1)} custom-call(bf16[2,16,32,512]{3,2,1,0:T(8,128)(2,1)} %bitcast.133), custom_call_target="tpu_custom_call" | custom-call | tf_op jit(solution)/shard_map/pallas_call | solution.py:250
  59.7 4.6 copy.77.rim_ref
  64.3 6.9 %copy.71 = bf16[4608,512]{0,1:T(8,128)(2,1)} copy(bf16[4608,512]{1,0:T(8,128)(2,1)} %refs_13_.1) | data formatting | bytes 9437184 | tf_op args[5]
  77.0 2.7 fusion.23
  79.7 5.2 %fusion.15 = f32[2,16,32,18]{3,2,1,0:T(8,128)S(1)} fusion(s32[]{:T(128)S(6)} %add.170, s32[]{:T(128)S(6)} %add.160, s32[]{:T(128)S(6)} %add.177, f32[2,32,48,162]{3,2,1,0:T(8,128)} %fusion.23, s32[]{:T(128)S(6)} %add.155, s32[]{:T(128)S(6)} %select_n.22, s32[]{:T(128)S(6)} %add.157, s32[]{:T(128)S(6)} %add.158, s32[]{:T(128)S(6)} %add.161, s32[]{:T(128)S(6)} %add.162, ...), kind=kLoop, calls=%fused_computation.42 | loop fusion | flops 202752 | bytes 2064440 | tf_op jit(solution)/shard_map/div | solution.py:1683
  86.4 21.1 %shard_map.316 = (bf16[4608,1024]{1,0:T(8,128)(2,1)}, f32[512,1024]{1,0:T(8,128)}) custom-call(bf16[2,512,1536]{2,1,0:T(8,128)(2,1)} %copy.77.rim_ref, bf16[512,4608]{1,0:T(8,128)(2,1)} %bitcast.127, s32[2,16,512]{2,1,0:T(8,128)} %pad.30.up_ref.refs_2_, s32[2,16,512]{2,1,0:T(8,128)} %pad.31.left_ref.refs_3_, f32[2,16,512]{2,1,0:T(8,128)} %pad.33.fr_ref.refs_4_, ...), custom_call_target="tpu_custom_call" | custom-call | tf_op jit(solution)/shard_map/pallas_call | solution.py:323
  107.6 1.9 copy.78
  111.4 18.1 %shard_map.317 = f32[8,128]{1,0:T(8,128)} custom-call(f32[8,128]{1,0:T(8,128)} %pad_maximum_fusion.7.x_ref, f32[8,128]{1,0:T(8,128)} %copy-done.13), custom_call_target="tpu_custom_call" | custom-call | tf_op jit(solution)/shard_map/pallas_call | solution.py:130
  132.9 48.3 %shard_map.318 = (f32[8,2048]{1,0:T(8,128)}, f32[8,512]{1,0:T(8,128)}, bf16[1024,512]{1,0:T(8,128)(2,1)}, bf16[1024,2048]{1,0:T(8,128)(2,1)}, bf16[1024,2048]{1,...) custom-call(f32[8,512]{1,0:T(8,128)} %pad.35.refs_0_.refs_2_, ...), custom_call_target="tpu_custom_call" | custom-call | tf_op jit(solution)/shard_map/pallas_call | solution.py:694
  181.2 52.4 %shard_map.319 = (f32[8,512]{1,0:T(8,128)}, f32[8,2048]{1,0:T(8,128)}, f32[8,2048]{1,0:T(8,128)}, f32[1024,512]{1,0:T(8,128)}, bf16[1024,512]{1,0:T(8,128)(2,1)}...) custom-call(f32[1024,128]{1,0:T(8,128)} %broadcast_in_dim.79.refs_1_.refs_0_, ...), custom_call_target="tpu_custom_call" | custom-call | tf_op jit(solution)/shard_map/pallas_call | solution.py:694
  234.3 47.0 %shard_map.320 = (bf16[1024,512]{1,0:T(8,128)(2,1)}, f32[8,512]{1,0:T(8,128)}, f32[8,512]{1,0:T(8,128)}, bf16[1,512,2048]{2,1,0:T(8,128)(2,1)}, bf16[4,512,1152]{2,1,0:T(8,128)(2,1)}) custom-call(f32[1024,128]{1,0:T(8,128)} %broadcast_in_dim.79.refs_1_.refs_0_, f32[8,2048]{1,0:T(8,128)} %get-tuple-element.65.refs_1_, f32[8,2048]{1,0:T(8,128)} %get-tuple-element.66.refs_2_, ...), custom_call_target="tpu_custom_call" | custom-call | tf_op jit(solution)/shard_map/pallas_call | solution.py:694
  281.4 52.0 %shard_map.321 = (bf16[1024,512]{1,0:T(8,128)(2,1)}, f32[8,2048]{1,0:T(8,128)}, f32[8,512]{1,0:T(8,128)}, bf16[4,64,1152]{2,1,0:T(8,128)(2,1)}, bf16[4,16,2048]{...) custom-call(f32[1024,128]{1,0:T(8,128)} %broadcast_in_dim.79.refs_1_.re, ...), custom_call_target="tpu_custom_call" | custom-call | tf_op jit(solution)/shard_map/pallas_call | solution.py:694
  333.4 9.4 %convolution_convert_fusion = bf16[4608,512]{1,0:T(8,128)(2,1)} fusion(bf16[4608,1024]{1,0:T(8,128)(2,1)} %get-tuple-element.84, bf16[1024,512]{1,0:T(8,128)(2,1)} %get-tuple-element.85.refs_11_), kind=kOutput, calls=%fused_computation.1 | convolution fusion | flops 4834197504 | bytes 15204352 | tf_op jit(solution)/shard_map/dot_general | solution.py:1883
  343.8 99.8 %shard_map.322 = (bf16[1024,512]{1,0:T(8,128)(2,1)}, f32[8,512]{1,0:T(8,128)}, bf16[8,64,1152]{2,1,0:T(8,128)(2,1)}, bf16[8,16,2048]{2,1,0:T(8,128)(2,1)}, bf16[...) custom-call(f32[1024,128]{1,0:T(8,128)} %broadcast_in_dim.79.refs_1_, ...), custom_call_target="tpu_custom_call" | custom-call | tf_op jit(solution)/shard_map/pallas_call | solution.py:694
  443.5 46.5 %shard_map.323 = (f32[32,1152]{1,0:T(8,128)}, bf16[8,144,512]{2,1,0:T(8,128)(2,1)}, bf16[8,64,512]{2,1,0:T(8,128)(2,1)}, bf16[1024,2048]{1,0:T(8,128)(2,1)}) custom-call(bf16[4,144,512]{2,1,0:T(8,128)(2,1)} %get-tuple-element.86.refs_0_, bf16[4,32,1152]{2,1,0:T(8,128)(2,1)} %get-tuple-element.87.refs_1_, bf16[1024,512]{1,0:T(8,128)(2,1)} %get-tuple-element.88.refs_2_, ...), custom_call_target="tpu_custom_call" | custom-call | tf_op jit(solution)/shard_map/pallas_call | solution.py:694
  493.5 1.8 bitcast_convert_fusion.1
  495.3 1.6 bitcast_convert_fusion.2
  503.4 2.0 copy.83
  511.1 4.9 copy.91
  516.1 2.0 copy.92
  (115 shorter events, 45.1 us)
Async XLA Ops:
  4.0 10.2 %copy-start.13 = (f32[8,128]{1,0:T(8,128)}, f32[8,128]{1,0:T(8,128)S(1)}, u32[]{:S(2)}) copy-start(f32[8,128]{1,0:T(8,128)S(1)} %broadcast_in_dim.80.count_ref) | copy-start | bytes 12292
  11.1 3.1 copy-start.4
  16.6 24.6 %copy-start.2 = (f32[1024,512]{1,0:T(8,128)}, f32[1024,512]{1,0:T(8,128)S(1)}, u32[]{:S(2)}) copy-start(f32[1024,512]{1,0:T(8,128)S(1)} %get-tuple-element.143.refs_15_) | copy-start | bytes 6291460
  64.3 6.9 %copy-start.11 = (s32[2,16,32,18]{2,1,3,0:T(8,128)S(1)}, s32[2,16,32,18]{2,1,3,0:T(8,128)}, u32[]{:S(2)}) copy-start(s32[2,16,32,18]{2,1,3,0:T(8,128)} %param.21) | copy-start | bytes 221188
  64.3 12.7 %copy-start.1 = (bf16[2,32,48,512]{3,2,1,0:T(8,128)(2,1)S(1)}, bf16[2,32,48,512]{3,2,1,0:T(8,128)(2,1)}, u32[]{:S(2)}) copy-start(bf16[2,32,48,512]{3,2,1,0:T(8,128)(2,1)} %shard_map.315) | copy-start | bytes 9437188
  109.5 1.3 copy-start
  109.5 20.8 %copy-start.14 = (f32[3072]{0:T(1024)S(1)}, f32[3072]{0:T(1024)}, u32[]{:S(2)}) copy-start(f32[3072]{0:T(1024)} %param.26) | copy-start | bytes 36868
  109.5 21.5 %copy-start.19 = (f32[512]{0:T(512)S(1)}, f32[512]{0:T(512)}, u32[]{:S(2)}) copy-start(f32[512]{0:T(512)} %get-tuple-element.129) | copy-start | bytes 6148
  109.5 22.7 %copy-start.15 = (f32[3072]{0:T(1024)S(1)}, f32[3072]{0:T(1024)}, u32[]{:S(2)}) copy-start(f32[3072]{0:T(1024)} %param.27) | copy-start | bytes 36868
  181.1 52.5 %copy-start.17 = (f32[512]{0:T(512)S(1)}, f32[512]{0:T(512)}, u32[]{:S(2)}) copy-start(f32[512]{0:T(512)} %get-tuple-element.123) | copy-start | bytes 6148
  181.2 52.5 %copy-start.18 = (f32[4,128]{1,0:T(4,128)S(1)}, f32[4,128]{1,0:T(4,128)}, u32[]{:S(2)}) copy-start(f32[4,128]{1,0:T(4,128)} %get-tuple-element.134) | copy-start | bytes 6148
  333.4 9.4 %copy-start.7 = (bf16[4608,18]{0,1:T(8,128)(2,1)S(1)}, bf16[4608,18]{0,1:T(8,128)(2,1)}, u32[]{:S(2)}) copy-start(bf16[4608,18]{0,1:T(8,128)(2,1)} %param.23) | copy-start | bytes 497668
  490.1 2.6 copy-start.12
  490.1 3.4 copy-start.6
  492.7 2.6 copy-start.9
  492.7 2.6 copy-start.10
  495.3 5.8 %copy-start.16 = (f32[512]{0:T(512)S(1)}, f32[512]{0:T(512)}, u32[]{:S(2)}) copy-start(f32[512]{0:T(512)} %get-tuple-element.131) | copy-start | bytes 6148
  495.3 6.4 %copy-start.8 = (bf16[8,64,512]{2,1,0:T(8,128)(2,1)S(1)}, bf16[8,64,512]{2,1,0:T(8,128)(2,1)}, u32[]{:S(2)}) copy-start(bf16[8,64,512]{2,1,0:T(8,128)(2,1)} %get-tuple-element.98) | copy-start | bytes 1572868
  496.9 6.2 %copy-start.5 = (bf16[8,64,1152]{2,1,0:T(8,128)(2,1)S(1)}, bf16[8,64,1152]{2,1,0:T(8,128)(2,1)}, u32[]{:S(2)}) copy-start(bf16[8,64,1152]{2,1,0:T(8,128)(2,1)} %get-tuple-element.99) | copy-start | bytes 3538948
  511.1 4.9 copy-start.3

commit v4 on v3

--- a/solution.py
+++ b/solution.py
@@ -22,12 +22,8 @@
 REACH = BOUND + 3
 PAD = 8
 HALF = 16
-STATS_CID, HALO_CID, FORWARD_A_CID, FORWARD_B_CID = 0, 1, 2, 3
+FIRST_CID, SAMPLE_CID, FORWARD_A_CID, FORWARD_B_CID = 0, 1, 2, 3
 BACKWARD_B_CID, BACKWARD_A_CID, BACKWARD_S_CID, LAST_CID = 4, 5, 6, 7
-
-
-def gelu_exact(values):
-    return jax.nn.gelu(values, approximate=False)
 
 
 def group_of(axes):
@@ -50,17 +46,6 @@
 
 PLANE = (ROW, COL)
 LINE = (IMG,)
-
-
-def entry_barrier(groups):
-    barrier = pltpu.get_barrier_semaphore()
-    count = 0
-    for axes in groups:
-        _, total, device = group_of(axes)
-        for step in range(1, total):
-            pl.semaphore_signal(barrier, inc=1, device_id=device(step), device_id_type=MESH)
-        count += total - 1
-    pl.semaphore_wait(barrier, count)
 
 
 def gather_start(axes, slots, send_sem, recv_sem):
@@ -87,176 +72,9 @@
     return [slots[lax.rem(place - spot + total, total)] for spot in range(total)]
 
 
-def stats_kernel(plane_count, x_ref, count_ref, o_ref, slots1, slots2, send_sems, recv_sems):
-    entry_barrier((PLANE, LINE))
-    half = x_ref.shape[0] // 2
-    total_count = plane_count * lax.axis_size(IMG)
-    slots1[0] = x_ref[...]
-    gather_start(PLANE, slots1, send_sems.at[0], recv_sems.at[0])
-    gather_wait(PLANE, slots1, recv_sems.at[0])
-    parts = in_order(PLANE, slots1)
-    total = functools.reduce(lambda a, b: a + b, [p[:half] for p in parts])
-    center = total / plane_count
-    spread = functools.reduce(lambda a, b: a + b, [p[half:] for p in parts])
-    for spot, part in enumerate(parts):
-        count = count_ref[spot : spot + 1, :]
-        away = part[:half] / jnp.maximum(count, 1.0) - center
-        spread = spread + count * (away * away)
-    slots2[0, :half] = total
-    slots2[0, half:] = spread
-    gather_start(LINE, slots2, send_sems.at[1], recv_sems.at[1])
-    gather_wait(LINE, slots2, recv_sems.at[1])
-    parts = in_order(LINE, slots2)
-    center = functools.reduce(lambda a, b: a + b, [p[:half] for p in parts]) / total_count
-    spread = functools.reduce(lambda a, b: a + b, [p[half:] for p in parts])
-    for part in parts:
-        away = part[:half] / plane_count - center
-        spread = spread + plane_count * (away * away)
-    o_ref[:half] = center
-    o_ref[half:] = spread / total_count
-    gather_wait(PLANE, slots1, send_sems.at[0])
-    gather_wait(LINE, slots2, send_sems.at[1])
-
-
-def stats_over_devices(total, spread, counts, plane_count):
-    width = total.shape[0]
-    both = jnp.concatenate([total, spread]).reshape(-1, 128)
-    rows = both.shape[0]
-    scratch = []
-    for axes in (PLANE, LINE):
-        size = int(np.prod([lax.axis_size(a) for a in axes]))
-        scratch.append(pltpu.VMEM((size, rows, 128), F32))
-    scratch += [pltpu.SemaphoreType.DMA((2,)), pltpu.SemaphoreType.DMA((2,))]
-    out = pl.pallas_call(
-        functools.partial(stats_kernel, plane_count),
-        out_shape=jax.ShapeDtypeStruct((rows, 128), F32),
-        in_specs=[VMEM, VMEM],
-        out_specs=VMEM,
-        scratch_shapes=scratch,
-        compiler_params=pltpu.CompilerParams(collective_id=STATS_CID, has_side_effects=True),
-    )(both, counts)
-    out = out.reshape(2, width)
-    return out[0], out[1]
-
-
 def halo_peers():
     row, rows, col = lax.axis_index(ROW), lax.axis_size(ROW), lax.axis_index(COL)
     return row, rows, col, {COL: 1 - col}, {ROW: row - 1}, {ROW: row + 1}
-
-
-def halo_barrier():
-    row, rows, _, pair, above, below = halo_peers()
-    barrier = pltpu.get_barrier_semaphore()
-    pl.semaphore_signal(barrier, inc=1, device_id=pair, device_id_type=MESH)
-
-    @pl.when(row > 0)
-    def _():
-        pl.semaphore_signal(barrier, inc=1, device_id=above, device_id_type=MESH)
-
-    @pl.when(row < rows - 1)
-    def _():
-        pl.semaphore_signal(barrier, inc=1, device_id=below, device_id_type=MESH)
-
-    count = 1 + (row > 0).astype(jnp.int32) + (row < rows - 1).astype(jnp.int32)
-    pl.semaphore_wait(barrier, count)
-
-
-def halo_kernel(pad, reach, h_ref, o_ref, send_sems, recv_sems):
-    row, rows, col, pair, above, below = halo_peers()
-    tile_rows, tile_cols = h_ref.shape[1], h_ref.shape[2]
-    off = pl.multiple_of(HALF * col, HALF)
-    spot = pl.multiple_of(2 * HALF * col, HALF)
-    own = pl.ds(off, tile_cols)
-    mid = pl.ds(HALF, HALF)
-    upper = pl.ds(pad - reach, reach)
-    lower = pl.ds(pad + tile_rows, reach)
-    zero_row = jnp.zeros((h_ref.shape[0],) + o_ref.shape[2:], o_ref.dtype)
-
-    def blank(at):
-        for k in range(at.start, at.stop):
-            o_ref[:, k] = zero_row
-
-    blank(slice(0, pad - reach))
-    blank(slice(pad + tile_rows + reach, 2 * pad + tile_rows))
-
-    @pl.when(row == 0)
-    def _():
-        blank(slice(pad - reach, pad))
-
-    @pl.when(row == rows - 1)
-    def _():
-        blank(slice(pad + tile_rows, pad + tile_rows + reach))
-
-    halo_barrier()
-
-    def copy(src, dst, k, device):
-        return pltpu.make_async_remote_copy(
-            src_ref=src,
-            dst_ref=dst,
-            send_sem=send_sems.at[k],
-            recv_sem=recv_sems.at[k],
-            device_id=device,
-            device_id_type=MESH,
-        )
-
-    to_pair = copy(
-        h_ref.at[:, :, pl.ds(pl.multiple_of(HALF * (1 - col), HALF), HALF)],
-        o_ref.at[:, pl.ds(pad, tile_rows), pl.ds(spot, HALF)],
-        0,
-        pair,
-    )
-    up = copy(h_ref.at[:, pl.ds(0, reach)], o_ref.at[:, lower, own], 1, above)
-    down = copy(h_ref.at[:, pl.ds(tile_rows - reach, reach)], o_ref.at[:, upper, own], 2, below)
-    from_below = copy(o_ref.at[:, lower, mid], o_ref.at[:, lower, pl.ds(spot, HALF)], 3, pair)
-    from_above = copy(o_ref.at[:, upper, mid], o_ref.at[:, upper, pl.ds(spot, HALF)], 4, pair)
-
-    @pl.when(row > 0)
-    def _():
-        up.start()
-
-    @pl.when(row < rows - 1)
-    def _():
-        down.start()
-
-    to_pair.start()
-    for n in range(h_ref.shape[0]):
-        o_ref[n, pl.ds(pad, tile_rows), own, :] = h_ref[n]
-
-    @pl.when(row < rows - 1)
-    def _():
-        up.wait_recv()
-        from_below.start()
-
-    @pl.when(row > 0)
-    def _():
-        down.wait_recv()
-        from_above.start()
-
-    to_pair.wait()
-
-    @pl.when(row < rows - 1)
-    def _():
-        down.wait_send()
-        from_below.wait()
-
-    @pl.when(row > 0)
-    def _():
-        up.wait_send()
-        from_above.wait()
-
-
-def with_halo(tile, pad, reach):
-    images, rows, cols, width = tile.shape
-    return pl.pallas_call(
-        functools.partial(halo_kernel, pad, reach),
-        out_shape=jax.ShapeDtypeStruct((images, rows + 2 * pad, cols + HALF, width), tile.dtype),
-        in_specs=[VMEM],
-        out_specs=VMEM,
-        scratch_shapes=[pltpu.SemaphoreType.DMA((5,)), pltpu.SemaphoreType.DMA((5,))],
-        compiler_params=pltpu.CompilerParams(
-            collective_id=HALO_CID, has_side_effects=True, vmem_limit_bytes=VMEM_LIMIT
-        ),
-    )(tile)
 
 
 BLOCK_ROWS = 8
@@ -297,51 +115,6 @@
         table[r * cols : (r + 1) * cols, lane : lane + pixels] = (
             row_w[r : r + 1, :] * col_w
         ).astype(BF16)
-
-
-def sample_kernel(rim_ref, w_ref, up_ref, left_ref, fr_ref, fc_ref, s_ref, d_ref, table):
-    block = pl.program_id(1)
-    width = rim_ref.shape[1]
-    cols = table.shape[0] // WINDOW
-    base = block * (BLOCK_ROWS * cols)
-    for tap in range(9):
-        row_w, _, col_w, _ = tap_weights(tap, block, cols, up_ref, left_ref, fr_ref, fc_ref)
-        write_table(table, 0, row_w, col_w, tap // 3, cols)
-        _, start, stop = tap_span(tap // 3, cols)
-        cells = pl.ds(pl.multiple_of(base + start, 128), stop - start)
-        value = jnp.dot(rim_ref[0, :, cells], table[start:stop, :], preferred_element_type=F32)
-        s_ref[tap * width : (tap + 1) * width, :] = value.astype(BF16)
-    d_ref[...] = jnp.dot(w_ref[...], s_ref[...], preferred_element_type=F32)
-
-
-def sample_forward(rim_t, w_t, up, left, fr, fc, cols):
-    images, width, cells = rim_t.shape
-    pixels = up.shape[-1]
-    blocks = 2
-    step = pixels // blocks
-    tap_spec = pl.BlockSpec((1, 16, step), lambda i, b: (i, 0, b))
-    return pl.pallas_call(
-        sample_kernel,
-        grid=(images, blocks),
-        out_shape=(
-            jax.ShapeDtypeStruct((9 * width, images * pixels), BF16),
-            jax.ShapeDtypeStruct((width, images * pixels), F32),
-        ),
-        in_specs=[
-            pl.BlockSpec((1, width, cells), lambda i, b: (i, 0, 0)),
-            pl.BlockSpec((width, 9 * width), lambda i, b: (0, 0)),
-            tap_spec,
-            tap_spec,
-            tap_spec,
-            tap_spec,
-        ],
-        out_specs=(
-            pl.BlockSpec((9 * width, step), lambda i, b: (0, i * blocks + b)),
-            pl.BlockSpec((width, step), lambda i, b: (0, i * blocks + b)),
-        ),
-        scratch_shapes=[pltpu.VMEM((WINDOW * cols, step), BF16)],
-        compiler_params=pltpu.CompilerParams(vmem_limit_bytes=VMEM_LIMIT),
-    )(rim_t, w_t, up, left, fr, fc)
 
 
 def build_shifted(rim_ref, shifted):
@@ -657,8 +430,9 @@
             copy.wait()
 
 
-def fused(work, cid, ins, staged, outs, pushed, scratch):
+def fused(work, cid, ins, staged, outs, pushed, scratch, smem={}):
     sizes = (len(ins), len(staged), len(outs), len(pushed))
+    scalars = pl.BlockSpec(memory_space=pltpu.SMEM)
 
     def kernel(*refs):
         r = Refs()
@@ -669,6 +443,8 @@
             del refs[:count]
             return taken
 
+        for key, ref in zip(smem, take(len(smem))):
+            setattr(r, key, ref)
         in_refs, in_raw, out_refs, out_raw = (take(count) for count in sizes)
         for key, shape in scratch.items():
             setattr(r, key, take(len(shape)) if isinstance(shape, list) else take(1)[0])
@@ -694,13 +470,13 @@
     result = pl.pallas_call(
         kernel,
         out_shape=[*outs.values(), *pushed.values()],
-        in_specs=[VMEM] * sizes[0] + [anywhere] * sizes[1],
+        in_specs=[scalars] * len(smem) + [VMEM] * sizes[0] + [anywhere] * sizes[1],
         out_specs=[VMEM] * sizes[2] + [anywhere] * sizes[3],
         scratch_shapes=flat,
         compiler_params=pltpu.CompilerParams(
             collective_id=cid, has_side_effects=True, vmem_limit_bytes=VMEM_LIMIT
         ),
-    )(*ins.values(), *staged.values())
+    )(*smem.values(), *ins.values(), *staged.values())
     return types.SimpleNamespace(**dict(zip((*outs, *pushed), result)))
 
 
@@ -935,14 +711,15 @@
 NORM_ROWS = 8
 
 
-def norm_table(exchange, gain_ref, shift_ref, out_ref):
+def norm_table(exchange, gain_ref, shift_ref, out_ref, first):
     mean, var = exchange.rows()
+    lanes = slice(first, first + mean.shape[1])
     inv = lax.rsqrt(var + EPSILON)
     out_ref[...] = jnp.zeros_like(out_ref)
     out_ref[0:1, :] = mean
     out_ref[1:2, :] = inv
-    out_ref[2:3, :] = inv * gain_ref[...]
-    out_ref[3:4, :] = shift_ref[...]
+    out_ref[2:3, :] = inv * gain_ref[:, lanes]
+    out_ref[3:4, :] = shift_ref[:, lanes]
     out_ref[4:5, :] = var
 
 
@@ -1062,6 +839,212 @@
     out_ref[0:1, :] = first
     out_ref[1:2, :] = second
     return first, second
+
+
+def order_taps(rows, width):
+    to = lax.broadcasted_iota(jnp.int32, (rows, width), 0)
+    at = lax.broadcasted_iota(jnp.int32, (rows, width), 1)
+    picked = jnp.where(to < 16, 2 * to, 2 * (to - 16) + 1)
+    real = lax.rem(to, 16) < 9
+    return jnp.where(jnp.logical_and(at == picked, real), 1.0, 0.0)
+
+
+def make_mask(r, tile_cols):
+    row, col = lax.axis_index(ROW), lax.axis_index(COL)
+    rows, cols = lax.axis_size(ROW), lax.axis_size(COL)
+    images = r.orientation.shape[0]
+    tile_rows = r.mask.shape[0] // images // tile_cols
+    tall = [r.orientation[n].astype(F32) for n in range(images)]
+    for n in range(images):
+
+        def fill(i, carry, n=n):
+            column = lax.broadcasted_iota(jnp.int32, (tile_cols, 128), 0) + col * tile_cols
+            portrait = jnp.where(column < SHORT, 1.0, 0.0)
+            line = jnp.zeros((tile_cols, 128), jnp.int32) + (row * tile_rows + i)
+            landscape = jnp.where(line < SHORT, 1.0, 0.0)
+            at = (n * tile_rows + i) * tile_cols
+            r.mask[pl.ds(pl.multiple_of(at, tile_cols), tile_cols), :] = (
+                landscape * (1.0 - tall[n]) + portrait * tall[n]
+            )
+            return carry
+
+        lax.fori_loop(0, tile_rows, fill, 0)
+
+    def count(row, col):
+        return (
+            jnp.clip(SHORT - row * tile_rows, 0, tile_rows) * tile_cols,
+            jnp.clip(SHORT - col * tile_cols, 0, tile_cols) * tile_rows,
+        )
+
+    def fill_count(at, row, col):
+        flat, upright = (c.astype(F32) for c in count(row, col))
+        total = added([flat * (1.0 - t) + upright * t for t in tall])
+        r.counts[at : at + 1, :] = jnp.zeros((1, 128), F32) + total
+
+    r.counts[...] = jnp.zeros_like(r.counts)
+    for k in range(rows * cols):
+        fill_count(k, jnp.int32(k // cols), jnp.int32(k % cols))
+    fill_count(8, row, col)
+
+
+def make_corners(r, cols):
+    images, _, pixels = r.up.shape
+    tile_cols = cols - HALF
+    order = order_taps(32, r.base.shape[1]).astype(BF16)
+    tap = lax.broadcasted_iota(jnp.int32, (16, pixels), 0)
+    pixel = lax.broadcasted_iota(jnp.int32, (16, pixels), 1)
+    up0 = pixel // tile_cols + PAD + 2 * (tap // 3 - 1)
+    left0 = lax.rem(pixel, tile_cols) + HALF * lax.axis_index(COL) + 2 * (lax.rem(tap, 3) - 1)
+    for n in range(images):
+        base = r.base[n * pixels : (n + 1) * pixels, :].astype(F32).astype(BF16)
+        moved = lax.dot_general(
+            order, base, (((1,), (1,)), ((), ())), preferred_element_type=F32
+        ).astype(jnp.int32)
+        r.up[n] = moved[:16] + up0
+        r.left[n] = moved[16:] + left0
+
+
+def first(plane_count, r):
+    signal_all()
+    ex = Exchange(r.ex1)
+    images, _, cols, width = r.rim.shape
+    halo = Halo(PAD, REACH, r.tile, r.rim, r.halo)
+    make_mask(r, cols - HALF)
+    halo.blank()
+    r.ready(r.feature, r.w_reduce)
+    product(r.feature, r.w_reduce, r.u_a1)
+    r.push(r.u_a1)
+    total, spread = device_stats(r.u_a1, r.mask, r.counts[8:9, :])
+    wait_all()
+    ex.put(total, spread)
+    make_corners(r, cols)
+    ex.middle_stats(r.counts, plane_count)
+    order = order_taps(32, r.w_offset.shape[1]).astype(BF16)
+    for tap in range(9):
+        rows = r.w_offset[tap * width : (tap + 1) * width, :]
+        r.w_off[32 * tap : 32 * tap + 32, :] = lax.dot_general(
+            order, rows, (((1,), (1,)), ((), ())), preferred_element_type=F32
+        ).astype(BF16)
+    ex.finish_stats(plane_count)
+    norm_table(ex, r.scale, r.shift, r.norm_a1, 0)
+    activate(r.u_a1, r.norm_a1, r.mask, r.tile)
+    halo.start()
+    select_cells(r, cols)
+    r.push(r.select)
+    halo.middle()
+    r.ready(r.w_deform)
+    turn(r.w_deform, r.w_turned)
+    r.push(r.w_turned)
+    halo.finish()
+    r.push(r.rim)
+
+
+def offset_fractions(r, cols):
+    images, width, cells = r.rim_t.shape
+    column = lax.rem(lax.broadcasted_iota(jnp.int32, (32, cells), 1), cols)
+    for n in range(images):
+        r.spread[...] = jnp.dot(r.w_off[...], r.rim_t[n], preferred_element_type=F32)
+        total = None
+        for tap in range(9):
+            i, j = 2 * (tap // 3 - 1), 2 * (tap % 3 - 1)
+            term = r.spread[32 * tap : 32 * tap + 32, :]
+            shift = -(i * cols + j) % cells
+            if shift:
+                term = pltpu.roll(term, shift, axis=1)
+            if j < 0:
+                term = jnp.where(column >= -j, term, 0.0)
+            if j > 0:
+                term = jnp.where(column < cols - j, term, 0.0)
+            total = term if total is None else total + term
+        parts = []
+        for _ in range(3):
+            parts.append(total.astype(BF16))
+            total = total - parts[-1].astype(F32)
+        on_tile = lax.dot_general(
+            jnp.concatenate(parts, axis=0),
+            r.select[...],
+            (((1,), (1,)), ((), ())),
+            preferred_element_type=F32,
+        )
+        offsets = on_tile[:32] + on_tile[32:64] + on_tile[64:]
+        fraction = 1.0 / (1.0 + jnp.exp(-offsets))
+        r.fr[n] = fraction[:16]
+        r.fc[n] = fraction[16:]
+
+
+def sample(plane_count, r):
+    signal_all()
+    ex = Exchange(r.ex2)
+    images, cells, width = r.rim.shape
+    cols = r.table.shape[0] // WINDOW
+    block = r.table.shape[1]
+    r.ready(r.rim)
+    for n in range(images):
+        for at in range(0, cells, 512):
+            r.rim_t[n, :, at : at + 512] = r.rim[n, at : at + 512, :].T
+    r.ready(r.select, r.w_off)
+    offset_fractions(r, cols)
+    r.push(r.fr, r.fc)
+
+    def unit(step, carry):
+        n, b = step // 2, lax.rem(step, 2)
+        lanes = pl.ds(pl.multiple_of(b * block, block), block)
+        mine = pl.ds(pl.multiple_of(step * block, block), block)
+        base = b * (BLOCK_ROWS * cols)
+        for tap in range(9):
+            row_w, _, col_w, _ = tap_weights(
+                tap, b, cols, r.up, r.left, r.fr, r.fc, n, lanes
+            )
+            write_table(r.table, 0, row_w, col_w, tap // 3, cols)
+            _, start, stop = tap_span(tap // 3, cols)
+            at = pl.ds(pl.multiple_of(base + start, 128), stop - start)
+            value = jnp.dot(r.rim_t[n, :, at], r.table[start:stop, :], preferred_element_type=F32)
+            r.samples[tap * width : (tap + 1) * width, mine] = value.astype(BF16)
+        deformed = jnp.dot(r.w_turned[...], r.samples[:, mine], preferred_element_type=F32)
+        r.u_a2[mine, :] = deformed.T
+        return carry
+
+    r.ready(r.w_turned)
+    lax.fori_loop(0, 2 * images, unit, 0)
+    r.push(r.samples, r.u_a2)
+    total, spread = device_stats(r.u_a2, r.mask, r.counts[8:9, :])
+    wait_all()
+    ex.put(total, spread)
+    ex.middle_stats(r.counts, plane_count)
+    ex.finish_stats(plane_count)
+    norm_table(ex, r.scale, r.shift, r.norm_a2, width)
+
+
+def finish_kernel(unbias, *refs):
+    conv_b, reduce_b, reduce_a, expand_b, expand_a, deform, off = refs[:7]
+    tables, outs = refs[7:19], refs[19:]
+    for src, out in zip((conv_b, reduce_b, reduce_a), outs[:3]):
+        eighth = src.shape[1]
+        for s in range(0, 8, 2):
+            rows = jnp.concatenate([src[s], src[s + 1]], axis=0).astype(F32)
+            out[:, s * eighth : (s + 2) * eighth] = rows.T
+    for src, out in zip((expand_b, expand_a, deform), outs[3:6]):
+        rows = src.shape[1]
+        for s in range(8):
+            out[s * rows : (s + 1) * rows, :] = src[s].astype(F32)
+    rest, total = off[...], None
+    order = order_taps(32, 18).astype(BF16)
+    for _ in range(3):
+        part = rest.astype(BF16)
+        rest = rest - part.astype(F32)
+        term = lax.dot_general(part, order, (((0,), (0,)), ((), ())), preferred_element_type=F32)
+        total = term if total is None else total + term
+    outs[6][...] = total
+    for k in range(4):
+        group, which = tables[3 * k : 3 * k + 3], outs[7 + 2 * k : 9 + 2 * k]
+        norms = k >= 2
+        for out, row in zip(which, (0, 4) if norms else (1, 0)):
+            at = 0
+            for table in group:
+                for first_lane in range(0, table.shape[1], 128):
+                    value = table[row : row + 1, first_lane : first_lane + 128]
+                    out[at : at + 1, :] = value * unbias if norms and row == 4 else value
+                    at += 1
 
 
 def forward_a(plane_count, r):
@@ -1081,7 +1064,7 @@
     r.ready(r.feature, r.w_reduce)
     ex3.middle_stats(r.counts, plane_count)
     ex3.finish_stats(plane_count)
-    norm_table(ex3, r.gain_a3, r.shift_a3, r.norm_a3)
+    norm_table(ex3, r.scale_a, r.shift_a, r.norm_a3, 2 * r.h2_a.shape[1])
     activate(r.wide, r.norm_a3, r.mask, r.middle, r.feature, r.slope_a, r.u_a3)
     r.push(r.middle, r.slope_a, r.u_a3)
     product(r.middle, r.w_reduce, r.u_b1)
@@ -1090,7 +1073,7 @@
     ex1.put(total, spread)
     ex1.middle_stats(r.counts, plane_count)
     ex1.finish_stats(plane_count)
-    norm_table(ex1, r.gain_b1, r.shift_b1, r.norm_b1)
+    norm_table(ex1, r.scale_b, r.shift_b, r.norm_b1, 0)
     activate(r.u_b1, r.norm_b1, r.mask, r.tile)
     halo.start()
     halo.middle()
@@ -1112,7 +1095,7 @@
     ex2.put(total, spread)
     ex2.middle_stats(r.counts, plane_count)
     ex2.finish_stats(plane_count)
-    norm_table(ex2, r.gain_b2, r.shift_b2, r.norm_b2)
+    norm_table(ex2, r.scale, r.shift, r.norm_b2, r.h2_b.shape[1])
     activate(r.u_b2, r.norm_b2, r.mask, r.h2_b)
     r.push(r.h2_b)
     r.ready(r.w_expand)
@@ -1123,7 +1106,7 @@
     ex3.middle_stats(r.counts, plane_count)
     ex3.finish_stats(plane_count)
     norm = r.norm_b3
-    norm_table(ex3, r.gain_b3, r.shift_b3, norm)
+    norm_table(ex3, r.scale, r.shift, norm, 2 * r.h2_b.shape[1])
 
     def work(i, lanes):
         x, away = normed(r.wide, norm, i, lanes)
@@ -1329,7 +1312,6 @@
 def unoffset(r):
     images, cells, width = r.rim.shape
     cols = r.table.shape[0] // WINDOW
-    select_cells(r, cols)
     column = lax.rem(lax.broadcasted_iota(jnp.int32, (32, cells), 1), cols)
     for n in range(images):
         parts = []
@@ -1520,7 +1502,7 @@
     r.ready(r.gd, r.rim, r.w_deform)
     turn(r.gd, r.turned)
     unsample(r, plan)
-    r.ready(r.w_off)
+    r.ready(r.w_off, r.select)
     unoffset(r)
     spill.start()
     r.push(r.gw_off)
@@ -1590,34 +1572,6 @@
         r.push(r.sum_deform, r.sum_reduce_a)
 
 
-def local_stats(values, weight_col, count):
-    total = jnp.sum(values * weight_col, axis=0)
-    away = values - total / jnp.maximum(count, 1.0)
-    return total, jnp.sum(away * away * weight_col, axis=0)
-
-
-def norm_forward(pre_norm, weight_col, norm_gain, norm_shift, counts):
-    own_count, all_counts, plane_count = counts
-    total, spread = local_stats(pre_norm, weight_col, own_count)
-    batch_mean, spread = stats_over_devices(total, spread, all_counts, plane_count)
-    inv_std = lax.rsqrt(spread + EPSILON)
-    unit_value = (pre_norm - batch_mean) * inv_std
-    return (unit_value * norm_gain + norm_shift, unit_value, inv_std, batch_mean, spread)
-
-
-def inside_counts(orientation, tile_rows, tile_cols):
-    rows, cols = lax.axis_size(ROW), lax.axis_size(COL)
-    tall = np.clip(SHORT - np.arange(rows) * tile_rows, 0, tile_rows)[:, None] * tile_cols
-    wide = np.clip(SHORT - np.arange(cols) * tile_cols, 0, tile_cols)[None, :] * tile_rows
-    tall = jnp.asarray(np.broadcast_to(tall, (rows, cols)).reshape(-1), F32)
-    wide = jnp.asarray(np.broadcast_to(wide, (rows, cols)).reshape(-1), F32)
-    flat = (orientation == 0).astype(F32)[:, None]
-    each = jnp.sum(flat * tall + (1.0 - flat) * wide, axis=0)
-    place = lax.axis_index(ROW) * cols + lax.axis_index(COL)
-    own = lax.dynamic_index_in_dim(each, place, keepdims=False)
-    return own, jnp.broadcast_to(each[:, None], (rows * cols, 128))
-
-
 def body(
     feature_in,
     orientation,
@@ -1637,76 +1591,14 @@
 ):
     images, tile_rows, tile_cols, channels = feature_in.shape
     inner_width = w_reduce_a.shape[1]
-    second_cut = 2 * inner_width
     tile_pixels = tile_rows * tile_cols
+    pixels = images * tile_pixels
     win_cols = tile_cols + HALF
     win_rows = tile_rows + 2 * PAD
+    cells = win_rows * win_cols
     plane_count = 1.0 * images * LONG * SHORT
     pixel_count = plane_count * lax.axis_size(IMG)
     unbias = pixel_count / (pixel_count - 1.0)
-    col_at = lax.axis_index(COL)
-    row_ids = lax.axis_index(ROW) * tile_rows + jnp.arange(tile_rows, dtype=jnp.int32)
-    col_ids = col_at * tile_cols + jnp.arange(tile_cols, dtype=jnp.int32)
-    landscape = jnp.broadcast_to((row_ids < SHORT)[:, None], (tile_rows, tile_cols))
-    portrait = jnp.broadcast_to((col_ids < SHORT)[None, :], (tile_rows, tile_cols))
-    inside = jnp.where(orientation[:, None, None] == 0, landscape[None], portrait[None]).astype(F32)
-    weight_col = inside.reshape(-1, 1)
-    pixels = weight_col.shape[0]
-    own_count, all_counts = inside_counts(orientation, tile_rows, tile_cols)
-    counts = (own_count, all_counts, plane_count)
-    block_in = (
-        (feature_in.astype(F32) * inside[..., None]).astype(BF16).reshape(pixels, channels)
-    )
-    reduced_a = jnp.dot(block_in, w_reduce_a, preferred_element_type=F32)
-    normed_a1, unit_a1, inv_a1, mean_a1, spread_a1 = norm_forward(
-        reduced_a, weight_col, scale_a[:inner_width], shift_a[:inner_width], counts
-    )
-    hidden_a = (gelu_exact(normed_a1) * weight_col).astype(BF16)
-    rim_a = with_halo(
-        hidden_a.reshape(images, tile_rows, tile_cols, inner_width), PAD, REACH
-    )
-    rim_flat = rim_a.reshape(images, -1, inner_width)
-    own_at = HALF * col_at
-    w_off = w_offset_a.reshape(9, inner_width, 18).transpose(1, 0, 2).reshape(inner_width, 162)
-    spread_taps = jnp.dot(
-        rim_flat.reshape(-1, inner_width), w_off, preferred_element_type=F32
-    ).reshape(images, win_rows, win_cols, 162)
-    spread_taps = jnp.pad(spread_taps, ((0, 0), (0, 0), (2, 2), (0, 0)))
-    spread_taps = lax.dynamic_slice_in_dim(spread_taps, own_at, tile_cols + 4, axis=2)
-    offsets = 0.0
-    for tap in range(9):
-        i, j = 2 * (tap // 3), 2 * (tap % 3)
-        offsets = offsets + spread_taps[
-            :, PAD - 2 + i : PAD - 2 + i + tile_rows, j : j + tile_cols, 18 * tap : 18 * tap + 18
-        ]
-    pad_taps = ((0, 0), (0, 16 - 9), (0, 0))
-    fraction = jax.nn.sigmoid(offsets).reshape(images, tile_pixels, 18).transpose(0, 2, 1)
-    frac_row, frac_col = (jnp.pad(fraction[:, k::2], pad_taps) for k in range(2))
-    base = offset_base.reshape(images, tile_pixels, 18).transpose(0, 2, 1)
-    cell = np.arange(tile_pixels)
-    tap_row = np.array([2 * (tap // 3 - 1) for tap in range(9)])[:, None]
-    tap_col = np.array([2 * (tap % 3 - 1) for tap in range(9)])[:, None]
-    upper = base[:, 0::2] + jnp.asarray(cell // tile_cols + PAD + tap_row, jnp.int32)
-    left = base[:, 1::2] + jnp.asarray(cell % tile_cols + tap_col, jnp.int32) + own_at
-    upper, left = jnp.pad(upper, pad_taps), jnp.pad(left, pad_taps)
-    samples, deformed = sample_forward(
-        rim_flat.transpose(0, 2, 1), w_deform_a.T, upper, left, frac_row, frac_col, win_cols
-    )
-    deformed = deformed.T
-    total, spread = local_stats(deformed, weight_col, own_count)
-    mean_a2, spread_a2 = stats_over_devices(total, spread, all_counts, plane_count)
-    one, two, three = slice(0, inner_width), slice(inner_width, second_cut), slice(second_cut, None)
-
-    def norm_rows(mean, var, part):
-        inv = lax.rsqrt(var + EPSILON)
-        rows = jnp.stack([mean, inv, inv * scale_a[part], shift_a[part], var])
-        return jnp.pad(rows, ((0, NORM_ROWS - 5), (0, 0)))
-
-    norm_a1 = norm_rows(mean_a1, spread_a1, one)
-    norm_a2 = norm_rows(mean_a2, spread_a2, two)
-    mask = jnp.broadcast_to(weight_col, (pixels, 128))
-    own_counts = jnp.broadcast_to(own_count, (8, 128))
-    count_rows = jnp.concatenate([all_counts, own_counts], axis=0)
 
     def array(*shape, dtype=BF16):
         return jax.ShapeDtypeStruct(shape, dtype)
@@ -1724,6 +1616,59 @@
     direct = inner_width % (images_axis * 8 * 16) == 0
     cuts = images_axis if direct else 1
     feature = feature_in.reshape(big)
+    scale_a, shift_a, scale_b, shift_b = (v[None] for v in (scale_a, shift_a, scale_b, shift_b))
+    taps_shape = (images, 16, tile_pixels)
+    start = fused(
+        functools.partial(first, plane_count),
+        FIRST_CID,
+        ins=dict(
+            base=offset_base.reshape(pixels, 18),
+            w_offset=w_offset_a,
+            scale=scale_a,
+            shift=shift_a,
+        ),
+        smem=dict(orientation=orientation),
+        staged=dict(feature=feature, w_reduce=w_reduce_a, w_deform=w_deform_a),
+        outs=dict(
+            mask=array(pixels, 128, dtype=F32),
+            counts=array(16, 128, dtype=F32),
+            up=array(*taps_shape, dtype=jnp.int32),
+            left=array(*taps_shape, dtype=jnp.int32),
+            w_off=array(288, inner_width),
+            norm_a1=table(inner_width),
+        ),
+        pushed=dict(
+            u_a1=array(*small, dtype=F32),
+            rim=array(images, win_rows, win_cols, inner_width),
+            select=array(tile_pixels, cells),
+            w_turned=array(inner_width, 9 * inner_width),
+        ),
+        scratch=dict(ex1=Exchange.scratch(inner_width), halo=Halo.scratch, tile=tile),
+    )
+    mask, count_rows, norm_a1 = start.mask, start.counts, start.norm_a1
+    rim_flat = start.rim.reshape(images, cells, inner_width)
+    sampled = fused(
+        functools.partial(sample, plane_count),
+        SAMPLE_CID,
+        ins=dict(
+            mask=mask, counts=count_rows, up=start.up, left=start.left, scale=scale_a, shift=shift_a
+        ),
+        staged=dict(rim=rim_flat, select=start.select, w_off=start.w_off, w_turned=start.w_turned),
+        outs=dict(norm_a2=table(inner_width)),
+        pushed=dict(
+            fr=array(*taps_shape, dtype=F32),
+            fc=array(*taps_shape, dtype=F32),
+            samples=array(9 * inner_width, pixels),
+            u_a2=array(*small, dtype=F32),
+        ),
+        scratch=dict(
+            ex2=Exchange.scratch(inner_width),
+            rim_t=pltpu.VMEM((images, inner_width, cells), BF16),
+            spread=pltpu.VMEM((288, cells), F32),
+            table=pltpu.VMEM((WINDOW * win_cols, tile_pixels // 2), BF16),
+        ),
+    )
+    norm_a2, deformed = sampled.norm_a2, sampled.u_a2
     fwd_a = fused(
         functools.partial(forward_a, plane_count),
         FORWARD_A_CID,
@@ -1731,10 +1676,10 @@
             norm_a2=norm_a2,
             mask=mask,
             counts=count_rows,
-            gain_a3=scale_a[None, three],
-            shift_a3=shift_a[None, three],
-            gain_b1=scale_b[None, one],
-            shift_b1=shift_b[None, one],
+            scale_a=scale_a,
+            shift_a=shift_a,
+            scale_b=scale_b,
+            shift_b=shift_b,
         ),
         staged=dict(u_a2=deformed, w_expand=w_expand_a, feature=feature, w_reduce=w_reduce_b),
         outs=dict(norm_a3=table(channels), norm_b1=table(inner_width)),
@@ -1760,10 +1705,8 @@
         ins=dict(
             mask=mask,
             counts=count_rows,
-            gain_b2=scale_b[None, two],
-            shift_b2=shift_b[None, two],
-            gain_b3=scale_b[None, three],
-            shift_b3=shift_b[None, three],
+            scale=scale_b,
+            shift=shift_b,
         ),
         staged=dict(
             rim_b=fwd_a.rim_b,
@@ -1879,10 +1822,7 @@
             turned=turned,
         ),
     )
-    feature_out = fwd_b.feature_out.reshape(feature_in.shape)
-    gw_deform = jnp.dot(samples, bwd_a.gd, preferred_element_type=F32).astype(BF16)
-    w_off_rows = w_offset_a.reshape(9, inner_width, 9, 2).transpose(0, 3, 2, 1)
-    w_off_rows = jnp.pad(w_off_rows, ((0, 0), (0, 0), (0, 7), (0, 0))).reshape(288, inner_width)
+    gw_deform = jnp.dot(sampled.samples, bwd_a.gd, preferred_element_type=F32).astype(BF16)
     staged_s, pushed_s, scratch_s = {}, {}, {}
     if direct:
         reduce_b, expand_a = eighths(bwd_a.gw_reduce), eighths(bwd_a.gw_expand)
@@ -1912,20 +1852,26 @@
             line_reduce_b=Line.scratch(eighth_of(reduce_b).shape),
             line_expand_a=Line.scratch(eighth_of(expand_a).shape),
         )
-    cells = win_rows * win_cols
-    taps_shape = (images, 16, tile_pixels)
     block = tile_pixels // 2
     bwd_s = fused(
         functools.partial(backward_s, pixel_count, direct),
         BACKWARD_S_CID,
-        ins=dict(mask=mask, norm_a1=norm_a1, up=upper, left=left, fr=frac_row, fc=frac_col),
+        ins=dict(
+            mask=mask,
+            norm_a1=norm_a1,
+            up=start.up,
+            left=start.left,
+            fr=sampled.fr,
+            fc=sampled.fc,
+        ),
         staged=dict(
             **staged_s,
             gd=bwd_a.gd,
             rim=rim_flat,
             w_deform=w_deform_a,
-            w_off=w_off_rows,
-            u_a1=reduced_a,
+            w_off=start.w_off,
+            select=start.select,
+            u_a1=start.u_a1,
         ),
         outs=dict(gr_a=array(*small), sums_a1=table(inner_width)),
         pushed=dict(**pushed_s, gw_off=array(cuts, 32, 9 * inner_width // cuts)),
@@ -1939,7 +1885,6 @@
             turned=turned,
             grad_row=pltpu.VMEM(taps_shape, F32),
             grad_col=pltpu.VMEM(taps_shape, F32),
-            select=pltpu.VMEM((tile_pixels, cells), BF16),
             on_cells=pltpu.VMEM((288, cells), BF16),
             gw_off_sum=pltpu.VMEM((288, inner_width), F32),
             grad=pltpu.VMEM(small, F32),
@@ -1973,57 +1918,75 @@
         pushed=dict(**pushed_l, grad_in=array(*big)),
         scratch=dict(**scratch_l, turned=turned),
     )
-    if direct:
-
-        def rows_of(grad):
-            return grad.reshape(-1, grad.shape[-1]).astype(F32)
-
-        gw_expand_b, gw_expand_a = rows_of(bwd_s.sum_expand_b), rows_of(bwd_s.sum_expand_a)
-        gw_conv_b, gw_reduce_b = rows_of(bwd_s.sum_conv_b).T, rows_of(bwd_s.sum_reduce_b).T
-        gw_deform_a, gw_reduce_a = rows_of(end.sum_deform), rows_of(end.sum_reduce_a).T
-        gw_off = end.sum_off
-    else:
-
-        def over_devices(grad, dim):
-            part = lax.psum_scatter(grad, IMG, scatter_dimension=dim, tiled=True)
-            return lax.psum(part, (ROW, COL)).astype(F32)
-
-        gw_expand_b, gw_expand_a = (
-            over_devices(g[0], 0) for g in (bwd_b.gw_expand, bwd_a.gw_expand)
-        )
-        gw_conv_b, gw_reduce_b, gw_reduce_a, gw_off_t = (
-            over_devices(g[0], 1).T
-            for g in (bwd_b.gw_conv, bwd_a.gw_reduce, end.gw_reduce, bwd_s.gw_off)
-        )
-        gw_deform_a = over_devices(gw_deform, 0)
-        gw_off = gw_off_t.T
-    gw_offset_a = gw_off.reshape(2, 16, -1)[:, :9].transpose(2, 1, 0).reshape(-1, 18)
     sums_a = [bwd_s.sums_a1, bwd_a.sums_a2, bwd_a.sums_a3]
     sums_b = [bwd_b.sums_b1, bwd_b.sums_b2, fwd_b.sums_b3]
     norms_a = [norm_a1, norm_a2, fwd_a.norm_a3]
     norms_b = [fwd_a.norm_b1, fwd_b.norm_b2, fwd_b.norm_b3]
-
-    def join(tables, row):
-        return jnp.concatenate([t[row] for t in tables])
-
+    if direct:
+        sums = [
+            bwd_s.sum_conv_b,
+            bwd_s.sum_reduce_b,
+            end.sum_reduce_a,
+            bwd_s.sum_expand_b,
+            bwd_s.sum_expand_a,
+            end.sum_deform,
+            end.sum_off,
+        ]
+    else:
+
+        def over_devices(grad, dim):
+            part = lax.psum_scatter(grad, IMG, scatter_dimension=dim, tiled=True)
+            return lax.psum(part, (ROW, COL))
+
+        turned_grads = (bwd_b.gw_conv, bwd_a.gw_reduce, end.gw_reduce)
+        sums = [over_devices(g[0], 1) for g in turned_grads]
+        sums += [over_devices(g[0], 0) for g in (bwd_b.gw_expand, bwd_a.gw_expand)]
+        sums.append(over_devices(gw_deform, 0))
+        sums = [g.reshape(8, -1, g.shape[1]) for g in sums]
+        sums.append(over_devices(bwd_s.gw_off[0], 1).astype(F32))
+    share = inner_width // images_axis
+    long_share, wide_share = 9 * share, channels // images_axis
+    shapes = [
+        (long_share, inner_width),
+        (wide_share, inner_width),
+        (wide_share, inner_width),
+        (share, channels),
+        (share, channels),
+        (long_share, inner_width),
+        (long_share, 18),
+    ]
+    vectors = ((2 * inner_width + channels) // 128, 128)
+    shapes += [vectors] * 8
+    operands = sums + sums_a + sums_b + norms_a + norms_b
+    results = pl.pallas_call(
+        functools.partial(finish_kernel, unbias),
+        out_shape=[array(*shape, dtype=F32) for shape in shapes],
+        in_specs=[VMEM] * len(operands),
+        out_specs=[VMEM] * len(shapes),
+        compiler_params=pltpu.CompilerParams(vmem_limit_bytes=VMEM_LIMIT),
+    )(*operands)
+    conv_b, reduce_b, reduce_a, expand_b, expand_a, deform_a, offset_a = results[:7]
+    scale_sums_a, shift_sums_a, scale_sums_b, shift_sums_b, mean_a, var_a, mean_b, var_b = (
+        v.reshape(-1) for v in results[7:]
+    )
     return (
-        feature_out,
+        fwd_b.feature_out.reshape(feature_in.shape),
         end.grad_in.reshape(feature_in.shape),
-        gw_reduce_a,
-        gw_offset_a,
-        gw_deform_a,
-        gw_expand_a,
-        join(sums_a, 1),
-        join(sums_a, 0),
-        join(norms_a, 0),
-        join(norms_a, 4) * unbias,
-        gw_reduce_b,
-        gw_conv_b,
-        gw_expand_b,
-        join(sums_b, 1),
-        join(sums_b, 0),
-        join(norms_b, 0),
-        join(norms_b, 4) * unbias,
+        reduce_a,
+        offset_a,
+        deform_a,
+        expand_a,
+        scale_sums_a,
+        shift_sums_a,
+        mean_a,
+        var_a,
+        reduce_b,
+        conv_b,
+        expand_b,
+        scale_sums_b,
+        shift_sums_b,
+        mean_b,
+        var_b,
     )
 
 

time: 524 us -> 463 us (0.88)
  local copies, waits for them, and re-layouts: 54.4 us -> 13.3 us
  other arithmetic: 31.1 us -> 0 us
  Pallas kernels: 417 us -> 432 us
    pallas_call x6 -> x8, Pallas kernels: 346 us -> 425 us  [fused(): pl.pallas_call(kernel, out_shape=[*outs.values(), *pushed.values()], in_s...]
    pallas_call x4 -> x1, Pallas kernels: 70.5 us -> 6.49 us  [body(): pl.pallas_call(functools.partial(finish_kernel, unbias), out_shape=[array...]
    slice x19 -> x0, local copies, waits for them, and re-layouts: 14.8 us -> none  [the longest x8 6.86 us: join(): return jnp.concatenate([t[row] for t in tables])]
    convert_element_type x6 -> x0, other arithmetic: 13.5 us -> none  [the longest x1 6.29 us: body(): hidden_a = (gelu_exact(normed_a1) * weight_col).astype(BF16)]
    transpose x7 -> x0, local copies, waits for them, and re-layouts: 10.1 us -> none  [the longest x1 4.64 us: body(): rim_flat.transpose(0, 2, 1)]
    dot_general x3 -> x1, matrix products: 14.4 us -> 9.37 us  [body(): jnp.dot(sampled.samples, bwd_a.gd, preferred_element_type=F32).astype(BF16)]
    unnamed x44 -> x7, local copies, waits for them, and re-layouts: 14.7 us -> 13.3 us
where the time goes in v4:
time: 463 us; the launch traced here: 456 us
  Pallas kernels  432 us (93%)
  local copies, waits for them, and re-layouts  13.3 us (3%)
  matrix products  9.37 us (2%)
    pallas_call x8, Pallas kernels, fused(): pl.pallas_call(kernel, out_shape=[*outs.values(), *pushed.values()], in_s...  425 us
    unnamed x7, local copies, waits for them, and re-layouts  13.3 us
    dot_general x1, matrix products, body(): jnp.dot(sampled.samples, bwd_a.gd, preferred_element_type=F32).astype(BF16)  9.37 us

profile of v4, /device:TPU:0, one launch (start us, length us, event | category | flops | bytes accessed | tf_op | source)
XLA Modules:
  0.0 455.6 jit_solution(17982189658549030237)
XLA Ops:
  0.7 2.0 copy.32
  2.7 2.4 copy.33.refs_2_
  5.1 39.7 %shard_map.278 = (f32[1024,128]{1,0:T(8,128)}, f32[16,128]{1,0:T(8,128)}, s32[2,16,512]{2,1,0:T(8,128)}, s32[2,16,512]{2,1,0:T(8,128)}, bf16[288,512]{1,0:T(8,12...) custom-call(s32[2]{0:T(128)} %refs_0_.1, ...), custom_call_target="tpu_custom_call" | custom-call | tf_op jit(solution)/shard_map/pallas_call | solution.py:470
  44.8 38.7 %shard_map.279 = (f32[8,512]{1,0:T(8,128)}, f32[2,16,512]{2,1,0:T(8,128)}, f32[2,16,512]{2,1,0:T(8,128)}, bf16[4608,1024]{1,0:T(8,128)(2,1)}, f32[1024,512]{1,0:T(8,128)}) custom-call(f32[1024,128]{1,0:T(8,128)} %get-tuple-element.88.refs_0_.refs_1_, f32[16,128]{1,0:T(8,128)} %get-tuple-element.89.refs_1_.refs_2_, s32[2,16,512]{2,1,0:T(8,128)} %get-tuple-element.90.refs_2_, ...), custom_call_target="tpu_custom_call" | custom-call | tf_op jit(solution)/shard_map/pallas_call | solution.py:470
  83.6 48.5 %shard_map.280 = (f32[8,2048]{1,0:T(8,128)}, f32[8,512]{1,0:T(8,128)}, bf16[1024,512]{1,0:T(8,128)(2,1)}, bf16[1024,2048]{1,0:T(8,128)(2,1)}, bf16[1024,2048]{1,...) custom-call(f32[8,512]{1,0:T(8,128)} %get-tuple-element.96.refs_0_.refs_2_.refs_1, ...), custom_call_target="tpu_custom_call" | custom-call | tf_op jit(solution)/shard_map/pallas_call | solution.py:470
  132.1 53.0 %shard_map.281 = (f32[8,512]{1,0:T(8,128)}, f32[8,2048]{1,0:T(8,128)}, f32[8,2048]{1,0:T(8,128)}, f32[1024,512]{1,0:T(8,128)}, bf16[1024,512]{1,0:T(8,128)(2,1)}...) custom-call(f32[1024,128]{1,0:T(8,128)} %get-tuple-element.88.refs_0_.refs_1_, ...), custom_call_target="tpu_custom_call" | custom-call | tf_op jit(solution)/shard_map/pallas_call | solution.py:470
  185.1 47.0 %shard_map.282 = (bf16[1024,512]{1,0:T(8,128)(2,1)}, f32[8,512]{1,0:T(8,128)}, f32[8,512]{1,0:T(8,128)}, bf16[1,512,2048]{2,1,0:T(8,128)(2,1)}, bf16[4,512,1152]{2,1,0:T(8,128)(2,1)}) custom-call(f32[1024,128]{1,0:T(8,128)} %get-tuple-element.88.refs_0_.refs_1_, f32[8,2048]{1,0:T(8,128)} %get-tuple-element.105.refs_1_.refs_18_, ...), custom_call_target="tpu_custom_call" | custom-call | tf_op jit(solution)/shard_map/pallas_call | solution.py:470
  232.2 51.8 %shard_map.283 = (bf16[1024,512]{1,0:T(8,128)(2,1)}, f32[8,2048]{1,0:T(8,128)}, f32[8,512]{1,0:T(8,128)}, bf16[4,64,1152]{2,1,0:T(8,128)(2,1)}, bf16[4,16,2048]{...) custom-call(f32[1024,128]{1,0:T(8,128)} %get-tuple-element.88.refs_0_.r, ...), custom_call_target="tpu_custom_call" | custom-call | tf_op jit(solution)/shard_map/pallas_call | solution.py:470
  284.0 9.4 %convolution_convert_fusion = bf16[4608,512]{1,0:T(8,128)(2,1)} fusion(bf16[4608,1024]{1,0:T(8,128)(2,1)} %get-tuple-element.124, bf16[1024,512]{1,0:T(8,128)(2,1)} %get-tuple-element.125.refs_11_), kind=kOutput, calls=%fused_computation | convolution fusion | flops 4834197504 | bytes 15204352 | tf_op jit(solution)/shard_map/dot_general | solution.py:1825
  293.4 99.4 %shard_map.284 = (bf16[1024,512]{1,0:T(8,128)(2,1)}, f32[8,512]{1,0:T(8,128)}, bf16[8,64,1152]{2,1,0:T(8,128)(2,1)}, bf16[8,16,2048]{2,1,0:T(8,128)(2,1)}, bf16[...) custom-call(f32[1024,128]{1,0:T(8,128)} %get-tuple-element.88.refs_0, ...), custom_call_target="tpu_custom_call" | custom-call | tf_op jit(solution)/shard_map/pallas_call | solution.py:470
  392.8 47.0 %shard_map.285 = (f32[32,1152]{1,0:T(8,128)}, bf16[8,144,512]{2,1,0:T(8,128)(2,1)}, bf16[8,64,512]{2,1,0:T(8,128)(2,1)}, bf16[1024,2048]{1,0:T(8,128)(2,1)}) custom-call(bf16[4,144,512]{2,1,0:T(8,128)(2,1)} %get-tuple-element.127.refs_0_, bf16[4,32,1152]{2,1,0:T(8,128)(2,1)} %get-tuple-element.128.refs_1_, bf16[1024,512]{1,0:T(8,128)(2,1)} %get-tuple-element.129.refs_2_, ...), custom_call_target="tpu_custom_call" | custom-call | tf_op jit(solution)/shard_map/pallas_call | solution.py:470
  439.8 6.5 %shard_map.286 = (f32[1152,512]{1,0:T(8,128)}, f32[512,512]{1,0:T(8,128)}, f32[512,512]{1,0:T(8,128)}, f32[128,2048]{1,0:T(8,128)}, f32[128,2048]{1,0:T(8,128)},...) custom-call(bf16[8,64,1152]{2,1,0:T(8,128)(2,1)} %get-tuple-element., ...), custom_call_target="tpu_custom_call" | custom-call | tf_op jit(solution)/shard_map/pallas_call | solution.py:1961
  446.3 1.9 copy.34
  448.2 0.0 copy-start
  448.2 4.9 %copy.37 = bf16[2,16,32,2048]{3,2,1,0:T(8,128)(2,1)} copy(bf16[2,16,32,2048]{3,2,1,0:T(8,128)(2,1)} %bitcast.32) | data formatting | bytes 8388608
  453.2 0.0 copy-done
  453.2 2.0 copy.38
Async XLA Ops:
  448.2 4.9 %copy-start = (bf16[1024,2048]{1,0:T(8,128)(2,1)S(1)}, bf16[1024,2048]{1,0:T(8,128)(2,1)}, u32[]{:S(2)}) copy-start(bf16[1024,2048]{1,0:T(8,128)(2,1)} %get-tuple-element.131) | copy-start | bytes 12582916
